TPU v7x, 1024 devices: a whole 4x8x16 slice. The times are simulated.
1024 devices in a mesh: tm: 32 (over z, core), expert: 16 (over x_lo, y), dp: 2 (over x_hi).
Axes of the slice: x: 4 (x_hi: 2, x_lo: 2; x = x_hi * 2 + x_lo), y: 8, z: 16, core: 2. Of those that a mesh axis runs over, the one named last changes fastest.
Arguments:
- resid: bfloat16 [2, 4096, 1024], P('dp', 'tm'), may hold values from -6 to 6
- glu_input: bfloat16 [2, 4096, 2048], P('dp', 'tm'), may hold values from -8 to 8
- dw_kernel: float32 [31, 1024], replicated, may hold values from -2 to 2
- w_in: bfloat16 [32, 1024, 4096], P('tm', None, 'expert'), may hold values from -0.1875 to 0.1875
- w_out: bfloat16 [32, 4096, 1024], P('tm', 'expert'), may hold values from -0.1875 to 0.1875
- expert_ids: int32 [2, 4096, 2], P('dp', 'tm'), may hold values from 0 to 31, all different within a row; in each aligned block of 128 rows (0 to 127, 128 to 255, ..., all dimensions but the last counted through in order) at most 16 rows name the same one
- mix_weights: float32 [2, 4096, 2], P('dp', 'tm'), may hold values from 0.2 to 1
- frame_kept: int32 [2, 4096], P('dp', 'tm'), may hold values 0 or 1
- out_grad: bfloat16 [2, 4096, 1024], P('dp', 'tm'), may hold values from -6 to 6
Outputs:
- block_out: bfloat16 [2, 4096, 1024], P('dp', 'tm')
- resid_grad: bfloat16 [2, 4096, 1024], P('dp', 'tm')
- glu_grad: bfloat16 [2, 4096, 2048], P('dp', 'tm')
- w_in_grad: float32 [32, 1024, 4096], P('tm', 'dp', 'expert')
- w_out_grad: float32 [32, 4096, 1024], P('tm', 'expert', 'dp')
Inputs may be any that keep to these rules, and one draw needn't show every extreme that they name: `expert_ids`: the two ids of a frame differ. Among the rows of one device (aligned blocks of 128 frames) no expert is named more than 16 times, a bound that some block reaches.
All inputs are finite; a program needn't handle non-finite values. No bound on the sum of `frame_kept` on one device may be relied on, other than what follows from the above.
Results may differ from a plain program's by a relative error of at most 0.023.
Values may be sent and summed in bfloat16 or wider, within the bound.
No kernel may reach another device: no remote copies, remote signals or barrier semaphores. Data moves between devices by JAX's collectives and lax.ppermute only.
A program may use at most 128 MiB of HBM per device.

v0:
```python
import jax
import jax.numpy as jnp
from jax import lax
from jax.sharding import PartitionSpec as P

KERNEL = 31


def extended(shard, sides, width):
    for axis, dim in sides:
        size, length = (lax.axis_size(axis), shard.shape[dim])
        up = [(i, (i + 1) % size) for i in range(size - 1)]
        down = [(j, i) for i, j in up]
        last = lax.slice_in_dim(shard, length - width, length, axis=dim)
        initial = lax.slice_in_dim(shard, 0, width, axis=dim)
        before = lax.ppermute(last, axis, up)
        after = lax.ppermute(initial, axis, down)
        shard = jnp.concatenate([before, shard, after], axis=dim)
    return shard


def swish_slope(value):
    sig = jax.nn.sigmoid(value)
    return sig * (1.0 + value * (1.0 - sig))


def with_rims(field):
    return extended(field.astype(jnp.bfloat16), (("tm", 0),), KERNEL // 2).astype(field.dtype)


def bucket_swap(rows):
    return lax.all_to_all(rows, "tm", split_axis=0, concat_axis=0, tiled=True)


def send_rows(rows):
    return bucket_swap(rows)


def combine_rows(part_rows, dest, weighting, experts, capacity, frames):
    width = part_rows.shape[1]
    total_rows = experts * capacity
    returned = bucket_swap(part_rows.reshape(experts, capacity, width)).reshape(total_rows, width)
    picked = returned[dest].astype(jnp.float32) * weighting[:, None]
    return lax.psum(
        jnp.sum(picked.reshape(frames, 2, width), axis=1).astype(jnp.bfloat16), "expert"
    ).astype(jnp.float32)


def shards(resid, glu_input, dw_kernel, w_in, w_out, expert_ids, mix_weights, frame_kept, out_grad):
    frames = resid.shape[1]
    width = resid.shape[2]
    experts = lax.axis_size("tm")
    capacity = 4 * frames // experts
    half = KERNEL // 2
    glu_in = glu_input[0]
    value = glu_in[:, :width].astype(jnp.float32)
    gate = glu_in[:, width:].astype(jnp.float32)
    sig_gate = jax.nn.sigmoid(gate)
    glu = value * sig_gate
    padded = with_rims(glu)
    conv = jnp.zeros_like(glu)
    for tap in range(KERNEL):
        conv = conv + dw_kernel[tap][None, :] * padded[tap : tap + frames]
    hidden_in = (resid[0].astype(jnp.float32) + conv * jax.nn.sigmoid(conv)).astype(jnp.bfloat16)
    ids = expert_ids[0].reshape(-1)
    onehot = (ids[:, None] == jnp.arange(experts, dtype=jnp.int32)[None, :]).astype(jnp.int32)
    slot = jnp.sum((jnp.cumsum(onehot, axis=0) - onehot) * onehot, axis=1)
    dest = ids * capacity + slot
    total_rows = experts * capacity
    rows = (
        jnp.zeros((total_rows, width), jnp.bfloat16).at[dest].set(jnp.repeat(hidden_in, 2, axis=0))
    )
    arrived = send_rows(rows.reshape(experts, capacity, width)).reshape(total_rows, width)
    weight_in = w_in[0]
    weight_out = w_out[0]
    pre = jnp.dot(arrived, weight_in, preferred_element_type=jnp.float32)
    act = (pre * jax.nn.sigmoid(pre)).astype(jnp.bfloat16)
    result = jnp.dot(act, weight_out, preferred_element_type=jnp.float32).astype(jnp.bfloat16)
    scale = (mix_weights[0] * frame_kept[0][:, None].astype(jnp.float32)).reshape(-1)
    moe = combine_rows(result, dest, scale, experts, capacity, frames)
    block_out = (hidden_in.astype(jnp.float32) + moe).astype(jnp.bfloat16)
    upstream = out_grad[0].astype(jnp.float32)
    scaled = (jnp.repeat(upstream, 2, axis=0) * scale[:, None]).astype(jnp.bfloat16)
    grad_rows = jnp.zeros((total_rows, width), jnp.bfloat16).at[dest].set(scaled)
    grad_arrived = send_rows(grad_rows.reshape(experts, capacity, width)).reshape(total_rows, width)
    back = lax.dot_general(
        grad_arrived, weight_out, (((1,), (1,)), ((), ())), preferred_element_type=jnp.float32
    )
    act_grad = (back * swish_slope(pre)).astype(jnp.bfloat16)
    input_part = lax.dot_general(
        act_grad, weight_in, (((1,), (1,)), ((), ())), preferred_element_type=jnp.float32
    ).astype(jnp.bfloat16)
    grad_out = lax.dot_general(
        act, grad_arrived, (((0,), (0,)), ((), ())), preferred_element_type=jnp.float32
    )
    grad_in = lax.dot_general(
        arrived, act_grad, (((0,), (0,)), ((), ())), preferred_element_type=jnp.float32
    )
    unit_weights = jnp.ones((2 * frames,), jnp.float32)
    hid_grad = upstream + combine_rows(input_part, dest, unit_weights, experts, capacity, frames)
    conv_grad = hid_grad * swish_slope(conv)
    padded_grad = with_rims(conv_grad)
    glu_back = jnp.zeros_like(conv_grad)
    for tap in range(KERNEL):
        start = 2 * half - tap
        glu_back = glu_back + dw_kernel[tap][None, :] * padded_grad[start : start + frames]
    glu_grad = jnp.concatenate(
        [glu_back * sig_gate, glu_back * value * sig_gate * (1.0 - sig_gate)], axis=1
    ).astype(jnp.bfloat16)
    w_in_grad, w_out_grad = (
        lax.psum_scatter(
            grad_in[None].astype(jnp.bfloat16), "dp", scatter_dimension=1, tiled=True
        ).astype(jnp.float32),
        lax.psum_scatter(
            grad_out[None].astype(jnp.bfloat16), "dp", scatter_dimension=2, tiled=True
        ).astype(jnp.float32),
    )
    return (
        block_out[None],
        hid_grad.astype(jnp.bfloat16)[None],
        glu_grad[None],
        w_in_grad,
        w_out_grad,
    )


def solution(mesh):
    return jax.shard_map(
        shards,
        mesh=mesh,
        in_specs=(
            P("dp", "tm", None),
            P("dp", "tm", None),
            P(),
            P("tm", None, "expert"),
            P("tm", "expert", None),
            P("dp", "tm", None),
            P("dp", "tm", None),
            P("dp", "tm"),
            P("dp", "tm", None),
        ),
        out_specs=(
            P("dp", "tm", None),
            P("dp", "tm", None),
            P("dp", "tm", None),
            P("tm", "dp", "expert"),
            P("tm", "expert", "dp"),
        ),
        check_vma=False,
    )
```

profile of v0, /device:TPU:1, one launch (start us, length us, event | category | flops | bytes accessed | tf_op | source)
XLA Modules:
  0.0 454.4 jit_solution(9607862654199151858)
XLA Ops:
  9.3 5.5 %collective-permute-start = (bf16[15,1024]{1,0:T(8,128)(2,1)S(1)}, bf16[15,1024]{1,0:T(8,128)(2,1)S(1)}, u32[]{:S(2)}, u32[]{:S(2)}) collective-permute-start(bf16[15,1024]{1,0:T(8,128)(2,1)S(1)} %get-tuple-element.15), channel_id=1, source_target_pairs={{0,32},{32,64},{64,96},{96,128},{128,160},{160,192},{192,224},{224... | collective-permute-start | bytes 92168 | tf_op jit(solution)/shard_map/ppermute | solution.py:16
  14.8 12.0 %collective-permute-start.1 = (bf16[15,1024]{1,0:T(8,128)(2,1)S(1)}, bf16[15,1024]{1,0:T(8,128)(2,1)S(1)}, u32[]{:S(2)}, u32[]{:S(2)}) collective-permute-start(bf16[15,1024]{1,0:T(8,128)(2,1)S(1)} %get-tuple-element.16), channel_id=1, source_target_pairs={{32,0},{64,32},{96,64},{128,96},{160,128},{192,160},{224,192},{256... | collective-permute-start | bytes 92168 | tf_op jit(solution)/shard_map/ppermute | solution.py:17
  30.1 2.9 fusion.68
  33.6 2.7 scatter_custom_fusion
  36.3 9.9 %all-to-all-start = ((bf16[32,16,1024]{2,1,0:T(8,128)(2,1)}), bf16[32,16,1024]{2,1,0:T(8,128)(2,1)S(1)}, u32[]{:S(2)}, u32[]{:S(2)}) async-start(bf16[32,16,1024]{2,1,0:T(8,128)(2,1)} %bitcast.36), calls=%async_computation | async-start | bytes 2097152 | tf_op jit(solution)/shard_map/all_to_all | solution.py:32
  46.8 1.3 broadcast_in_dim.10
  48.1 1.9 reshape.159
  50.1 2.7 scatter_custom_fusion.1
  52.8 49.2 %all-to-all-done = bf16[32,16,1024]{2,1,0:T(8,128)(2,1)S(1)} async-done(((bf16[32,16,1024]{2,1,0:T(8,128)(2,1)}), bf16[32,16,1024]{2,1,0:T(8,128)(2,1)S(1)}, u32[]{:S(2)}, u32[]{:S(2)}) %all-to-all-start) | async-done | bytes 1048608 | tf_op jit(solution)/shard_map/all_to_all | solution.py:32
  102.0 4.9 %all-to-all-start.2 = ((bf16[32,16,1024]{2,1,0:T(8,128)(2,1)}), bf16[32,16,1024]{2,1,0:T(8,128)(2,1)}, u32[]{:S(2)}, u32[]{:S(2)}) async-start(bf16[32,16,1024]{2,1,0:T(8,128)(2,1)} %bitcast.47), calls=%async_computation.2 | async-start | bytes 2097152 | tf_op jit(solution)/shard_map/all_to_all | solution.py:32
  107.3 1.4 convolution_convert_fusion.1
  108.8 53.9 %all-to-all-done.2 = bf16[32,16,1024]{2,1,0:T(8,128)(2,1)} async-done(((bf16[32,16,1024]{2,1,0:T(8,128)(2,1)}), bf16[32,16,1024]{2,1,0:T(8,128)(2,1)}, u32[]{:S(2)}, u32[]{:S(2)}) %all-to-all-start.2) | async-done | bytes 1048608 | tf_op jit(solution)/shard_map/all_to_all | solution.py:32
  162.7 4.6 %all-to-all-start.1 = ((bf16[32,16,1024]{2,1,0:T(8,128)(2,1)}), bf16[32,16,1024]{2,1,0:T(8,128)(2,1)S(1)}, u32[]{:S(2)}, u32[]{:S(2)}) async-start(bf16[32,16,1024]{2,1,0:T(8,128)(2,1)} %bitcast.40), calls=%async_computation.1 | async-start | bytes 2097152 | tf_op jit(solution)/shard_map/all_to_all | solution.py:32
  167.4 1.7 fusion.2
  169.1 1.4 convolution_convert_fusion
  170.5 52.7 %all-to-all-done.1 = bf16[32,16,1024]{2,1,0:T(8,128)(2,1)S(1)} async-done(((bf16[32,16,1024]{2,1,0:T(8,128)(2,1)}), bf16[32,16,1024]{2,1,0:T(8,128)(2,1)S(1)}, u32[]{:S(2)}, u32[]{:S(2)}) %all-to-all-start.1) | async-done | bytes 1048608 | tf_op jit(solution)/shard_map/all_to_all | solution.py:32
  223.2 4.6 %all-to-all-start.3 = ((bf16[32,16,1024]{2,1,0:T(8,128)(2,1)}), bf16[32,16,1024]{2,1,0:T(8,128)(2,1)S(1)}, u32[]{:S(2)}, u32[]{:S(2)}) async-start(bf16[32,16,1024]{2,1,0:T(8,128)(2,1)} %bitcast.105), calls=%async_computation.3 | async-start | bytes 2097152 | tf_op jit(solution)/shard_map/all_to_all | solution.py:32
  227.9 2.5 fusion.1
  230.6 2.5 fusion
  236.0 47.7 %all-to-all-done.3 = bf16[32,16,1024]{2,1,0:T(8,128)(2,1)S(1)} async-done(((bf16[32,16,1024]{2,1,0:T(8,128)(2,1)}), bf16[32,16,1024]{2,1,0:T(8,128)(2,1)S(1)}, u32[]{:S(2)}, u32[]{:S(2)}) %all-to-all-start.3) | async-done | bytes 1048608 | tf_op jit(solution)/shard_map/all_to_all | solution.py:32
  283.6 1.3 gather_fusion.1
  285.1 2.1 reduce_sum.35
  287.2 2.1 multiply_reduce_fusion
  289.4 1.9 convert_element_type.153
  291.2 4.4 reduce-scatter.3.cloned.1.call-done
  295.6 1.8 convert_element_type.150
  297.4 123.9 %all-reduce.3.cloned.1.call-done = (bf16[128,1024]{1,0:T(8,128)(2,1)}, bf16[128,1024]{1,0:T(8,128)(2,1)}) async-done(((bf16[128,1024]{1,0:T(8,128)(2,1)}, bf16[128,1024]{1,0:T(8,128)(2,1)}), (bf16[128,1024]{1,0:T(8,128)(2,1)}, bf16[128,1024]{1,0:T(8,128)(2,1)})) %all-reduce.3.cloned.1.call-update) | async-done | bytes 524304 | tf_op jit(solution)/shard_map/psum | solution.py:44
  421.3 1.9 multiply_convert_fusion.3
  423.3 14.9 %collective-permute-start.2 = (bf16[15,1024]{1,0:T(8,128)(2,1)S(1)}, bf16[15,1024]{1,0:T(8,128)(2,1)S(1)}, u32[]{:S(2)}, u32[]{:S(2)}) collective-permute-start(bf16[15,1024]{1,0:T(8,128)(2,1)S(1)} %get-tuple-element.13), channel_id=1, source_target_pairs={{0,32},{32,64},{64,96},{96,128},{128,160},{160,192},{192,224},{224... | collective-permute-start | bytes 92168 | tf_op jit(solution)/shard_map/ppermute | solution.py:16
  438.3 1.9 collective-permute-start.3
  441.0 2.5 collective-permute-done.3
  443.7 2.2 fusion.81
  (123 shorter events, 11.1 us)
Async XLA Ops:
  8.0 99.3 %copy-start = (bf16[1,256,1024]{2,1,0:T(8,128)(2,1)S(1)}, bf16[1,256,1024]{2,1,0:T(8,128)(2,1)}, u32[]{:S(2)}) copy-start(bf16[1,256,1024]{2,1,0:T(8,128)(2,1)} %param.13) | copy-start | bytes 1572868
  8.0 20.6 %copy-start.10 = (f32[31,1024]{1,0:T(8,128)S(1)}, f32[31,1024]{1,0:T(8,128)}, u32[]{:S(2)}) copy-start(f32[31,1024]{1,0:T(8,128)} %param.11) | copy-start | bytes 380932
  9.3 20.8 %copy-start.9 = (bf16[1,128,1024]{2,1,0:T(8,128)(2,1)S(1)}, bf16[1,128,1024]{2,1,0:T(8,128)(2,1)}, u32[]{:S(2)}) copy-start(bf16[1,128,1024]{2,1,0:T(8,128)(2,1)} %param.9) | copy-start | bytes 786436
  9.3 20.7 %collective-permute-start = (bf16[15,1024]{1,0:T(8,128)(2,1)S(1)}, bf16[15,1024]{1,0:T(8,128)(2,1)S(1)}, u32[]{:S(2)}, u32[]{:S(2)}) collective-permute-start(bf16[15,1024]{1,0:T(8,128)(2,1)S(1)} %get-tuple-element.15), channel_id=1, source_target_pairs={{0,32},{32,64},{64,96},{96,128},{128,160},{160,192},{192,224},{224... | collective-permute-start | bytes 92168 | tf_op jit(solution)/shard_map/ppermute | solution.py:16
  14.8 15.2 %collective-permute-start.1 = (bf16[15,1024]{1,0:T(8,128)(2,1)S(1)}, bf16[15,1024]{1,0:T(8,128)(2,1)S(1)}, u32[]{:S(2)}, u32[]{:S(2)}) collective-permute-start(bf16[15,1024]{1,0:T(8,128)(2,1)S(1)} %get-tuple-element.16), channel_id=1, source_target_pairs={{32,0},{64,32},{96,64},{128,96},{160,128},{192,160},{224,192},{256... | collective-permute-start | bytes 92168 | tf_op jit(solution)/shard_map/ppermute | solution.py:17
  30.0 20.1 %copy-start.34 = (s32[256,1]{0,1:T(1,128)}, s32[256,1]{0,1:T(1,128)S(1)}, u32[]{:S(2)}) copy-start(s32[256,1]{0,1:T(1,128)S(1)} %compare_select_fusion) | copy-start | bytes 3076
  36.3 10.5 %copy-start.5 = (bf16[1,128,1024]{2,1,0:T(8,128)(2,1)S(1)}, bf16[1,128,1024]{2,1,0:T(8,128)(2,1)}, u32[]{:S(2)}) copy-start(bf16[1,128,1024]{2,1,0:T(8,128)(2,1)} %param.17) | copy-start | bytes 786436
  36.3 65.7 %all-to-all-start = ((bf16[32,16,1024]{2,1,0:T(8,128)(2,1)}), bf16[32,16,1024]{2,1,0:T(8,128)(2,1)S(1)}, u32[]{:S(2)}, u32[]{:S(2)}) async-start(bf16[32,16,1024]{2,1,0:T(8,128)(2,1)} %bitcast.36), calls=%async_computation | async-start | bytes 2097152 | tf_op jit(solution)/shard_map/all_to_all | solution.py:32
  102.0 60.8 %all-to-all-start.2 = ((bf16[32,16,1024]{2,1,0:T(8,128)(2,1)}), bf16[32,16,1024]{2,1,0:T(8,128)(2,1)}, u32[]{:S(2)}, u32[]{:S(2)}) async-start(bf16[32,16,1024]{2,1,0:T(8,128)(2,1)} %bitcast.47), calls=%async_computation.2 | async-start | bytes 2097152 | tf_op jit(solution)/shard_map/all_to_all | solution.py:32
  162.7 60.4 %all-to-all-start.1 = ((bf16[32,16,1024]{2,1,0:T(8,128)(2,1)}), bf16[32,16,1024]{2,1,0:T(8,128)(2,1)S(1)}, u32[]{:S(2)}, u32[]{:S(2)}) async-start(bf16[32,16,1024]{2,1,0:T(8,128)(2,1)} %bitcast.40), calls=%async_computation.1 | async-start | bytes 2097152 | tf_op jit(solution)/shard_map/all_to_all | solution.py:32
  169.1 54.1 %copy-start.8 = (bf16[512,256]{1,0:T(8,128)(2,1)}, bf16[512,256]{1,0:T(8,128)(2,1)S(1)}, u32[]{:S(2)}) copy-start(bf16[512,256]{1,0:T(8,128)(2,1)S(1)} %fusion.2) | copy-start | bytes 786436
  223.2 60.4 %all-to-all-start.3 = ((bf16[32,16,1024]{2,1,0:T(8,128)(2,1)}), bf16[32,16,1024]{2,1,0:T(8,128)(2,1)S(1)}, u32[]{:S(2)}, u32[]{:S(2)}) async-start(bf16[32,16,1024]{2,1,0:T(8,128)(2,1)} %bitcast.105), calls=%async_computation.3 | async-start | bytes 2097152 | tf_op jit(solution)/shard_map/all_to_all | solution.py:32
  227.8 61.5 %reduce-scatter.5.cloned.1.call-start = ((), (), s32[]{:S(2)}) async-start(), calls=%async_computation.7 | async-start | bytes 786432 | tf_op jit(solution)/shard_map/reduce_scatter | solution.py:114
  230.4 65.2 %reduce-scatter.3.cloned.1.call-start = ((), (), s32[]{:S(2)}) async-start(), calls=%async_computation.6 | async-start | bytes 786432 | tf_op jit(solution)/shard_map/reduce_scatter | solution.py:111
  233.2 188.1 %all-reduce.3.cloned.1.call-start = ((), (), s32[]{:S(2)}) async-start(), calls=%async_computation.8 | async-start | bytes 1048576 | tf_op jit(solution)/shard_map/psum | solution.py:44
  289.3 132.0 %copy-start.4 = (f32[128,1024]{1,0:T(8,128)S(1)}, f32[128,1024]{1,0:T(8,128)}, u32[]{:S(2)}) copy-start(f32[128,1024]{1,0:T(8,128)} %get-tuple-element.10) | copy-start | bytes 1572868
  289.3 132.0 %copy-start.6 = (bf16[1,128,1024]{2,1,0:T(8,128)(2,1)S(1)}, bf16[1,128,1024]{2,1,0:T(8,128)(2,1)}, u32[]{:S(2)}) copy-start(bf16[1,128,1024]{2,1,0:T(8,128)(2,1)} %param.17) | copy-start | bytes 786436
  421.3 18.9 %copy-start.7 = (bf16[128,1024]{1,0:T(8,128)(2,1)S(1)}, bf16[128,1024]{1,0:T(8,128)(2,1)}, u32[]{:S(2)}) copy-start(bf16[128,1024]{1,0:T(8,128)(2,1)} %get-tuple-element.5) | copy-start | bytes 786436
  423.2 20.4 %copy-start.2 = (bf16[1,128,2048]{2,1,0:T(8,128)(2,1)S(1)}, bf16[1,128,2048]{2,1,0:T(8,128)(2,1)}, u32[]{:S(2)}) copy-start(bf16[1,128,2048]{2,1,0:T(8,128)(2,1)} %param.10) | copy-start | bytes 1572868
  423.2 20.4 %copy-start.12 = (f32[1,1024]{1,0:T(1,128)S(1)}, f32[1,1024]{1,0:T(1,128)}, u32[]{:S(2)}) copy-start(f32[1,1024]{1,0:T(1,128)} %copy-done.11) | copy-start | bytes 12292
  423.2 20.4 %copy-start.14 = (f32[1,1024]{1,0:T(1,128)S(1)}, f32[1,1024]{1,0:T(1,128)}, u32[]{:S(2)}) copy-start(f32[1,1024]{1,0:T(1,128)} %copy-done.13) | copy-start | bytes 12292
  423.2 20.4 %copy-start.16 = (f32[1,1024]{1,0:T(1,128)S(1)}, f32[1,1024]{1,0:T(1,128)}, u32[]{:S(2)}) copy-start(f32[1,1024]{1,0:T(1,128)} %copy-done.15) | copy-start | bytes 12292
  423.2 20.4 %copy-start.18 = (f32[1,1024]{1,0:T(1,128)S(1)}, f32[1,1024]{1,0:T(1,128)}, u32[]{:S(2)}) copy-start(f32[1,1024]{1,0:T(1,128)} %copy-done.17) | copy-start | bytes 12292
  423.2 20.4 %copy-start.20 = (f32[1,1024]{1,0:T(1,128)S(1)}, f32[1,1024]{1,0:T(1,128)}, u32[]{:S(2)}) copy-start(f32[1,1024]{1,0:T(1,128)} %copy-done.19) | copy-start | bytes 12292
  423.3 20.4 %copy-start.22 = (f32[1,1024]{1,0:T(1,128)S(1)}, f32[1,1024]{1,0:T(1,128)}, u32[]{:S(2)}) copy-start(f32[1,1024]{1,0:T(1,128)} %copy-done.21) | copy-start | bytes 12292
  423.3 20.4 %copy-start.24 = (f32[1,1024]{1,0:T(1,128)S(1)}, f32[1,1024]{1,0:T(1,128)}, u32[]{:S(2)}) copy-start(f32[1,1024]{1,0:T(1,128)} %copy-done.23) | copy-start | bytes 12292
  423.3 20.4 %copy-start.26 = (f32[1,1024]{1,0:T(1,128)S(1)}, f32[1,1024]{1,0:T(1,128)}, u32[]{:S(2)}) copy-start(f32[1,1024]{1,0:T(1,128)} %copy-done.25) | copy-start | bytes 12292
  423.3 20.4 %copy-start.28 = (f32[1,1024]{1,0:T(1,128)S(1)}, f32[1,1024]{1,0:T(1,128)}, u32[]{:S(2)}) copy-start(f32[1,1024]{1,0:T(1,128)} %copy-done.27) | copy-start | bytes 12292
  423.3 20.4 %copy-start.30 = (f32[1,1024]{1,0:T(1,128)S(1)}, f32[1,1024]{1,0:T(1,128)}, u32[]{:S(2)}) copy-start(f32[1,1024]{1,0:T(1,128)} %copy-done.29) | copy-start | bytes 12292
  423.3 20.4 %copy-start.32 = (f32[1,1024]{1,0:T(1,128)S(1)}, f32[1,1024]{1,0:T(1,128)}, u32[]{:S(2)}) copy-start(f32[1,1024]{1,0:T(1,128)} %copy-done.31) | copy-start | bytes 12292
  423.3 17.7 %collective-permute-start.2 = (bf16[15,1024]{1,0:T(8,128)(2,1)S(1)}, bf16[15,1024]{1,0:T(8,128)(2,1)S(1)}, u32[]{:S(2)}, u32[]{:S(2)}) collective-permute-start(bf16[15,1024]{1,0:T(8,128)(2,1)S(1)} %get-tuple-element.13), channel_id=1, source_target_pairs={{0,32},{32,64},{64,96},{96,128},{128,160},{160,192},{192,224},{224... | collective-permute-start | bytes 92168 | tf_op jit(solution)/shard_map/ppermute | solution.py:16
  438.3 5.2 %collective-permute-start.3 = (bf16[15,1024]{1,0:T(8,128)(2,1)S(1)}, bf16[15,1024]{1,0:T(8,128)(2,1)S(1)}, u32[]{:S(2)}, u32[]{:S(2)}) collective-permute-start(bf16[15,1024]{1,0:T(8,128)(2,1)S(1)} %get-tuple-element.14), channel_id=1, source_target_pairs={{32,0},{64,32},{96,64},{128,96},{160,128},{192,160},{224,192},{256... | collective-permute-start | bytes 92168 | tf_op jit(solution)/shard_map/ppermute | solution.py:17
  (16 other events, 80.9 us)
Sparse Core Ops, SparseCore 0:
  233.0 29.7 reduce-scatter.4
  266.7 28.9 reduce-scatter.2
Sparse Core Ops, SparseCore 1:
  289.4 131.8 all-reduce.2
where the time goes:
time: 455 us; the launch traced here: 454 us
  waiting for transfers between devices  334 us (73%)
  starting transfers between devices  58.7 us (13%)
  other arithmetic  22.8 us (5%)
  between operations  16.2 us (4%)
  local copies, waits for them, and re-layouts  12.2 us (3%)
  matrix products  10.1 us (2%)
    all_to_all x4, waiting for transfers between devices, bucket_swap(): return lax.all_to_all(rows, 'tm', split_axis=0, concat_axis=0, tiled=True)  203 us
    psum x1, waiting for transfers between devices, combine_rows(): lax.psum(jnp.sum(picked.reshape(frames, 2, width), axis=1).astype(jnp.bfl...  124 us
    all_to_all x4, starting transfers between devices, bucket_swap(): return lax.all_to_all(rows, 'tm', split_axis=0, concat_axis=0, tiled=True)  24.1 us
    ppermute x2, starting transfers between devices, extended(): before = lax.ppermute(last, axis, up)  20.5 us
    ppermute x2, starting transfers between devices, extended(): after = lax.ppermute(initial, axis, down)  13.9 us
  transfers between devices with their start and end apart: 11, of which 7 were waited for; matrix products, arithmetic and copies ran while one was open for 7% of the time, Pallas kernels for 0%

commit v1 on v0

v1 whole, which is shorter than its diff:
```python
import jax
import jax.numpy as jnp
from jax import lax
from jax.experimental import pallas as pl
from jax.experimental.pallas import tpu as pltpu
from jax.sharding import Mesh, PartitionSpec as P

KERNEL = 31
HALF = KERNEL // 2
F32 = jnp.float32
BF16 = jnp.bfloat16
NT = (((1,), (1,)), ((), ()))
TN = (((0,), (0,)), ((), ()))


def swish_slope(value):
    sig = jax.nn.sigmoid(value)
    return sig * (1.0 + value * (1.0 - sig))


def rims(shard):
    size, length = lax.axis_size("tm"), shard.shape[0]
    up = [(i, i + 1) for i in range(size - 1)]
    down = [(j, i) for i, j in up]
    before = lax.ppermute(shard[length - HALF :], "tm", up)
    after = lax.ppermute(shard[:HALF], "tm", down)
    return before, after


def gather_columns(rows_ref, hid, grad):
    parts = rows_ref.shape[0]
    cols = rows_ref.shape[2] // 2
    for part in range(parts):
        side, at = divmod(part, parts // 2)
        block = rows_ref[part]
        hid[side, :, at * cols : (at + 1) * cols] = block[:, :cols]
        grad[side, :, at * cols : (at + 1) * cols] = block[:, cols:]


def expert_kernel(rows_ref, win_a, win_b, wout_a, wout_b, act_ref, act_grad_ref, out_ref, hid, grad):
    gather_columns(rows_ref, hid, grad)
    width = hid.shape[2]
    result = [0.0, 0.0]
    part = [0.0, 0.0]
    for which, (w_in, w_out) in enumerate(((win_a, wout_a), (win_b, wout_b))):
        pre = sum(
            jnp.dot(hid[s], w_in[s * width : (s + 1) * width, :], preferred_element_type=F32)
            for s in range(2)
        )
        back = sum(
            lax.dot_general(
                grad[s], w_out[:, s * width : (s + 1) * width], NT, preferred_element_type=F32
            )
            for s in range(2)
        )
        sig = jax.nn.sigmoid(pre)
        act = (pre * sig).astype(BF16)
        act_grad = (back * (sig * (1.0 + pre * (1.0 - sig)))).astype(BF16)
        act_ref[which] = act
        act_grad_ref[which] = act_grad
        for s in range(2):
            result[s] += jnp.dot(
                act, w_out[:, s * width : (s + 1) * width], preferred_element_type=F32
            )
            part[s] += lax.dot_general(
                act_grad, w_in[s * width : (s + 1) * width, :], NT, preferred_element_type=F32
            )
    blocks = out_ref.shape[0] // 2
    cols = out_ref.shape[2]
    for index in range(blocks):
        side, at = divmod(index, blocks // 2)
        out_ref[index] = result[side][:, at * cols : (at + 1) * cols].astype(BF16)
        out_ref[blocks + index] = part[side][:, at * cols : (at + 1) * cols].astype(BF16)


def grads_kernel(dp_ref, rows_ref, act_ref, act_grad_ref, own_in, own_out, send, hid, grad):
    gather_columns(rows_ref, hid, grad)
    mine = dp_ref[0]
    hidden = act_ref.shape[2]
    slot = 0
    for which in range(2):
        for other in range(2):
            side = mine if other == 0 else 1 - mine
            g_in = lax.dot_general(hid[side], act_grad_ref[which], TN, preferred_element_type=F32)
            g_out = lax.dot_general(act_ref[which], grad[side], TN, preferred_element_type=F32)
            if which == 0 and other == 0:
                own_in[...] = g_in
                own_out[...] = g_out
            else:
                width = g_in.shape[0]
                send[slot, :width] = g_in.astype(BF16)
                for piece in range(g_out.shape[1] // hidden):
                    send[slot, width + piece * hidden : width + (piece + 1) * hidden] = g_out[
                        :, piece * hidden : (piece + 1) * hidden
                    ].astype(BF16)
                slot += 1


def vmem(count):
    return [pl.BlockSpec(memory_space=pltpu.VMEM)] * count


def expert_rows(rows, win, win_other, wout, wout_other):
    parts, count, pair = rows.shape
    width = parts * pair // 2
    hidden = win.shape[1]
    flops = 16 * count * width * hidden
    return pl.pallas_call(
        expert_kernel,
        out_shape=(
            jax.ShapeDtypeStruct((2, count, hidden), BF16),
            jax.ShapeDtypeStruct((2, count, hidden), BF16),
            jax.ShapeDtypeStruct((2 * parts, count, pair // 2), BF16),
        ),
        in_specs=vmem(5),
        out_specs=tuple(vmem(3)),
        scratch_shapes=[pltpu.VMEM((2, count, width // 2), BF16)] * 2,
        compiler_params=pltpu.CompilerParams(vmem_limit_bytes=40 * 2**20),
        cost_estimate=pl.CostEstimate(flops=flops, bytes_accessed=5 * 2**20, transcendentals=0),
    )(rows, win, win_other, wout, wout_other)


def weight_grads(dp, rows, act, act_grad):
    parts, count, pair = rows.shape
    width = parts * pair // 2
    hidden = act.shape[2]
    return pl.pallas_call(
        grads_kernel,
        out_shape=(
            jax.ShapeDtypeStruct((width // 2, hidden), F32),
            jax.ShapeDtypeStruct((hidden, width // 2), F32),
            jax.ShapeDtypeStruct((3, width, hidden), BF16),
        ),
        in_specs=[pl.BlockSpec(memory_space=pltpu.SMEM)] + vmem(3),
        out_specs=tuple(vmem(3)),
        scratch_shapes=[pltpu.VMEM((2, count, width // 2), BF16)] * 2,
        compiler_params=pltpu.CompilerParams(vmem_limit_bytes=40 * 2**20),
        cost_estimate=pl.CostEstimate(
            flops=8 * count * width * hidden, bytes_accessed=5 * 2**20, transcendentals=0
        ),
    )(dp, rows, act, act_grad)


def shards(resid, glu_input, dw_kernel, w_in, w_out, expert_ids, mix_weights, frame_kept, out_grad):
    frames = resid.shape[1]
    width = resid.shape[2]
    experts = lax.axis_size("tm")
    ranks = lax.axis_size("y")
    capacity = 4 * frames // experts
    half_cap = capacity // 2
    cols = width // ranks
    xl = lax.axis_index("xl")
    y = lax.axis_index("y")
    dp = lax.axis_index("dp")
    weight_in = w_in[0]
    weight_out = w_out[0]
    swap_xl = [(0, 1), (1, 0)]

    glu_in = glu_input[0]
    before, after = rims(glu_in)
    win_other = lax.ppermute(weight_in, "xl", swap_xl)
    wout_other = lax.ppermute(weight_out, "xl", swap_xl)

    ids = expert_ids[0].T.reshape(-1)
    order = 2 * (jnp.arange(2 * frames) % frames) + jnp.arange(2 * frames) // frames
    earlier = (ids[:, None] == ids[None, :]) & (order[None, :] < order[:, None])
    slot = jnp.sum(earlier.astype(jnp.int32), axis=1)
    dest = ids * capacity + slot
    scale = (mix_weights[0] * frame_kept[0][:, None].astype(F32)).T.reshape(-1)
    near = jnp.where(slot // half_cap == xl, ids * half_cap + slot % half_cap, -1)
    near_hot = near[None, :] == jnp.arange(experts * half_cap)[:, None]
    near_frames = (near_hot[:, :frames] | near_hot[:, frames:]).astype(BF16)
    near_scale = jnp.sum(jnp.where(near_hot, scale[None, :], 0.0), axis=1)
    pick = (dest[:, None] == jnp.arange(experts * capacity)[None, :]).astype(BF16)
    pick_scale = jnp.where(xl == 0, scale, 1.0)

    value = glu_in[:, :width].astype(F32)
    gate = glu_in[:, width:].astype(F32)
    sig_gate = jax.nn.sigmoid(gate)
    wide = jnp.concatenate([before, glu_in, after], axis=0).astype(F32)
    padded = wide[:, :width] * jax.nn.sigmoid(wide[:, width:])
    conv = jnp.zeros((frames, width), F32)
    for tap in range(KERNEL):
        conv = conv + dw_kernel[tap][None, :] * padded[tap : tap + frames]
    hidden_in = (resid[0].astype(F32) + conv * jax.nn.sigmoid(conv)).astype(BF16)

    hid_cols = lax.dynamic_slice_in_dim(hidden_in, y * cols, cols, axis=1)
    grad_cols = lax.dynamic_slice_in_dim(out_grad[0], y * cols, cols, axis=1)
    both = jnp.concatenate([hid_cols, grad_cols], axis=1)
    rows = jnp.dot(near_frames, both, preferred_element_type=F32)
    factor = jnp.where(jnp.arange(2 * cols)[None, :] < cols, 1.0, near_scale[:, None])
    rows = (rows * factor).astype(BF16).reshape(experts, half_cap, 2 * cols)
    rows = lax.all_to_all(rows, "tm", 0, 0, tiled=True)
    rows = rows.reshape(1, experts * half_cap, 2 * cols)
    rows = lax.all_to_all(
        jnp.broadcast_to(rows, (ranks,) + rows.shape[1:]), "y", 0, 0, tiled=True
    )

    act, act_grad, parts = expert_rows(rows, weight_in, win_other, weight_out, wout_other)
    parts = lax.all_to_all(parts, ("xl", "y"), 0, 0, tiled=True)
    own_in, own_out, send = weight_grads(dp.reshape(1), rows, act, act_grad)
    got = (
        lax.ppermute(send[0], "dp", swap_xl),
        lax.ppermute(send[1], "xl", swap_xl),
        lax.ppermute(send[2], ("xl", "dp"), [(0, 3), (3, 0), (1, 2), (2, 1)]),
    )

    parts = parts.reshape(2, ranks, experts, half_cap, cols).astype(F32).sum(axis=1)
    parts = parts.astype(BF16).transpose(1, 0, 2, 3).reshape(experts, capacity, cols)
    parts = lax.all_to_all(parts, "tm", 0, 0, tiled=True).reshape(experts * capacity, cols)
    picked = jnp.dot(pick, parts, preferred_element_type=F32) * pick_scale[:, None]
    summed = (picked[:frames] + picked[frames:]).astype(BF16)
    summed = lax.all_to_all(
        jnp.broadcast_to(summed[None], (2 * ranks,) + summed.shape), ("xl", "y"), 0, 0, tiled=True
    )
    moe = summed[:ranks].transpose(1, 0, 2).reshape(frames, width).astype(F32)
    moe_grad = summed[ranks:].transpose(1, 0, 2).reshape(frames, width).astype(F32)
    block_out = (hidden_in.astype(F32) + moe).astype(BF16)
    hid_grad = out_grad[0].astype(F32) + moe_grad

    conv_grad = hid_grad * swish_slope(conv)
    before, after = rims(conv_grad.astype(BF16))
    padded_grad = jnp.concatenate([before.astype(F32), conv_grad, after.astype(F32)], axis=0)
    glu_back = jnp.zeros_like(conv_grad)
    for tap in range(KERNEL):
        start = 2 * HALF - tap
        glu_back = glu_back + dw_kernel[tap][None, :] * padded_grad[start : start + frames]
    glu_grad = jnp.concatenate(
        [glu_back * sig_gate, glu_back * value * sig_gate * (1.0 - sig_gate)], axis=1
    ).astype(BF16)

    hidden = weight_in.shape[1]
    w_in_grad = own_in + sum(piece[: width // 2].astype(F32) for piece in got)
    rest = [
        piece[width // 2 :].reshape(-1, hidden, hidden).transpose(1, 0, 2).reshape(hidden, -1)
        for piece in got
    ]
    w_out_grad = own_out + sum(piece.astype(F32) for piece in rest)
    return (
        block_out[None],
        hid_grad.astype(BF16)[None],
        glu_grad[None],
        w_in_grad[None],
        w_out_grad[None],
    )


def solution(mesh):
    size = mesh.shape["expert"]
    axes = {"tm": mesh.shape["tm"], "xl": 2, "y": size // 2, "dp": mesh.shape["dp"]}
    split = Mesh(mesh.devices.reshape(tuple(axes.values())), tuple(axes))
    expert = ("xl", "y")
    return jax.shard_map(
        shards,
        mesh=split,
        in_specs=(
            P("dp", "tm", None),
            P("dp", "tm", None),
            P(),
            P("tm", None, expert),
            P("tm", expert, None),
            P("dp", "tm", None),
            P("dp", "tm", None),
            P("dp", "tm"),
            P("dp", "tm", None),
        ),
        out_specs=(
            P("dp", "tm", None),
            P("dp", "tm", None),
            P("dp", "tm", None),
            P("tm", "dp", expert),
            P("tm", expert, "dp"),
        ),
        check_vma=False,
    )
```

time: 455 us -> 210 us (0.46)
  waiting for transfers between devices: 334 us -> 51.1 us
  blocking collectives: 0 us -> 51.5 us
  between operations: 16.2 us -> 2.02 us
  matrix products: 10.1 us -> 0.47 us
  other arithmetic: 22.8 us -> 29.8 us
    all_to_all x4 -> x3, waiting for transfers between devices: 203 us -> 7.84 us  [the longest x1 4.53 us: shards(): lax.all_to_all(jnp.broadcast_to(rows, (ranks,) + rows.shape[1:]), 'y', 0,...]
    psum x1 -> x0, waiting for transfers between devices: 124 us -> none  [combine_rows(): lax.psum(jnp.sum(picked.reshape(frames, 2, width), axis=1).astype(jnp.bfl...]
    all_to_all x0 -> x2, blocking collectives: none -> 51.5 us  [the longest x1 25.9 us: shards(): parts = lax.all_to_all(parts, ('xl', 'y'), 0, 0, tiled=True)]
    ppermute x4 -> x9, waiting for transfers between devices: 2.53 us -> 43.2 us  [the longest x1 16.7 us: shards(): lax.ppermute(send[0], 'dp', swap_xl)]
    concatenate x3, other arithmetic: 3.23 us -> 13.9 us  [shards(): jnp.concatenate([glu_back * sig_gate, glu_back * value * sig_gate * (1.0...]
    dot_general x6 -> x2, matrix products: 10.1 us -> 0.47 us  [the longest x1 0.28 us: shards(): jnp.dot(pick, parts, preferred_element_type=F32) * pick_scale[:, None]]
    unnamed x76 -> x150, local copies, waits for them, and re-layouts: 1.06 us -> 6.7 us
    ppermute x4 -> x9, starting transfers between devices: 34.3 us -> 39.7 us  [the longest x2 18 us: rims(): after = lax.ppermute(shard[:HALF], 'tm', down)]
  transfers between devices with their start and end apart: 11 -> 12, of which waited for: 7 -> 8; matrix products, arithmetic and copies ran while one was open for 7% -> 5% of each run, Pallas kernels for 0% -> 0%
where the time goes in v1:
time: 210 us
  starting transfers between devices  60.8 us (29%)
  blocking collectives  51.5 us (25%)
  waiting for transfers between devices  51.1 us (24%)
  other arithmetic  29.8 us (14%)
  local copies, waits for them, and re-layouts  11.8 us (6%)
  Pallas kernels  2.26 us (1%)
    all_to_all x1, blocking collectives, shards(): parts = lax.all_to_all(parts, ('xl', 'y'), 0, 0, tiled=True)  25.9 us
    all_to_all x1, blocking collectives, shards(): rows = lax.all_to_all(rows, 'tm', 0, 0, tiled=True)  25.6 us
    ppermute x2, starting transfers between devices, rims(): after = lax.ppermute(shard[:HALF], 'tm', down)  18 us
    ppermute x1, waiting for transfers between devices, shards(): lax.ppermute(send[0], 'dp', swap_xl)  16.7 us
    concatenate x3, other arithmetic, shards(): jnp.concatenate([glu_back * sig_gate, glu_back * value * sig_gate * (1.0...  13.9 us
    ppermute x1, waiting for transfers between devices, shards(): wout_other = lax.ppermute(weight_out, 'xl', swap_xl)  11.2 us
    all_to_all x1, starting transfers between devices, shards(): lax.all_to_all(parts, 'tm', 0, 0, tiled=True)  9.96 us
    convert_element_type x1, other arithmetic, shards(): (resid[0].astype(F32) + conv * jax.nn.sigmoid(conv)).astype(BF16)  9.76 us
  transfers between devices with their start and end apart: 12, of which 8 were waited for; matrix products, arithmetic and copies ran while one was open for 5% of the time, Pallas kernels for 0%

profile of v1, /device:TPU:1, one launch (start us, length us, event | category | flops | bytes accessed | tf_op | source)
XLA Modules:
  0.0 209.6 jit_solution(13655536808869885283)
XLA Ops:
  0.7 1.4 copy.32
  2.3 16.1 %collective-permute-start.1 = (bf16[15,2048]{0,1:T(8,128)(2,1)S(1)}, bf16[15,2048]{0,1:T(8,128)(2,1)S(1)}, u32[]{:S(2)}, u32[]{:S(2)}) collective-permute-start(bf16[15,2048]{0,1:T(8,128)(2,1)S(1)} %get-tuple-element.43), channel_id=1, source_target_pairs={{32,0},{64,32},{96,64},{128,96},{160,128},{192,160},{224,192},{256... | collective-permute-start | bytes 184328 | tf_op jit(solution)/shard_map/ppermute | solution.py:26
  18.3 1.9 collective-permute-start
  23.4 3.0 %collective-permute-done = bf16[15,2048]{0,1:T(8,128)(2,1)S(1)} collective-permute-done((bf16[15,2048]{0,1:T(8,128)(2,1)S(1)}, bf16[15,2048]{0,1:T(8,128)(2,1)S(1)}, u32[]{:S(2)}, u32[]{:S(2)}) %collective-permute-start) | collective-permute-done | bytes 61472 | tf_op jit(solution)/shard_map/ppermute | solution.py:25
  27.5 9.8 %fusion.128 = (bf16[128,1024]{0,1:T(8,128)(2,1)S(1)}, f32[128,1024]{0,1:T(8,128)}) fusion(bf16[1,128,1024]{1,2,0:T(8,128)(2,1)S(1)} %copy.31, f32[158,1024]{0,1:T(8,128)S(1)} %fusion.5, f32[1024]{0:T(1024)S(1)} %bitcast.149, f32[1024]{0:T(1024)S(1)} %bitcast.151, f32[1024]{0:T(1024)S(1)} %bitcast.155, f32[1024]{0:T(1024)S(1)} %bitcast.157, ...), kind=kLoop, calls=%fused_computation.228 | loop fusion | flops 8912896 | bytes 17428480 | tf_op jit(solution)/shard_map/convert_element_type | solution.py:185
  38.2 25.6 %all_to_all.25 = bf16[32,8,256]{2,1,0:T(8,128)(2,1)S(1)} all-to-all(bf16[32,8,256]{2,1,0:T(8,128)(2,1)S(1)} %fusion.1), channel_id=1, replica_groups=mesh['tm'=32,'xl'=2,'y'=8,'dp'=2] {'tm'}, dimensions={0} | all-to-all | bytes 262144 | tf_op jit(solution)/shard_map/all_to_all | solution.py:193
  63.8 1.0 broadcast_in_dim.80
  64.8 6.8 %all-to-all-start.1 = ((bf16[8,256,256]{2,1,0:T(8,128)(2,1)}), bf16[8,256,256]{2,1,0:T(8,128)(2,1)S(1)}, u32[]{:S(2)}, u32[]{:S(2)}) async-start(bf16[8,256,256]{2,1,0:T(8,128)(2,1)} %broadcast_in_dim.80), calls=%async_computation.1 | async-start | bytes 2097152 | tf_op jit(solution)/shard_map/all_to_all | solution.py:195
  71.6 3.1 %collective-permute-start.2 = (bf16[1024,256]{1,0:T(8,128)(2,1)S(1)}, bf16[1024,256]{1,0:T(8,128)(2,1)S(1)}, u32[]{:S(2)}, u32[]{:S(2)}) collective-permute-start(bf16[1024,256]{1,0:T(8,128)(2,1)S(1)} %bitcast.115), channel_id=1, source_target_pairs={{0,16},{16,0},{1,17},{17,1},{2,18},{18,2},{3,19},{19,3},{4,20},{20... | collective-permute-start | bytes 1572872 | tf_op jit(solution)/shard_map/ppermute | solution.py:161
  74.8 2.2 %collective-permute-start.3 = (bf16[256,1024]{1,0:T(8,128)(2,1)S(1)}, bf16[256,1024]{1,0:T(8,128)(2,1)S(1)}, u32[]{:S(2)}, u32[]{:S(2)}) collective-permute-start(bf16[256,1024]{1,0:T(8,128)(2,1)S(1)} %bitcast.117), channel_id=1, source_target_pairs={{0,16},{16,0},{1,17},{17,1},{2,18},{18,2},{3,19},{19,3},{4,20},{20... | collective-permute-start | bytes 1572872 | tf_op jit(solution)/shard_map/ppermute | solution.py:162
  76.9 8.1 %collective-permute-done.2.win_b = bf16[1024,256]{1,0:T(8,128)(2,1)S(1)} collective-permute-done((bf16[1024,256]{1,0:T(8,128)(2,1)S(1)}, bf16[1024,256]{1,0:T(8,128)(2,1)S(1)}, u32[]{:S(2)}, u32[]{:S(2)}) %collective-permute-start.2) | collective-permute-done | bytes 524320 | tf_op jit(solution)/shard_map/ppermute | solution.py:161
  85.0 11.2 %collective-permute-done.3.wout_b = bf16[256,1024]{1,0:T(8,128)(2,1)S(1)} collective-permute-done((bf16[256,1024]{1,0:T(8,128)(2,1)S(1)}, bf16[256,1024]{1,0:T(8,128)(2,1)S(1)}, u32[]{:S(2)}, u32[]{:S(2)}) %collective-permute-start.3) | collective-permute-done | bytes 524320 | tf_op jit(solution)/shard_map/ppermute | solution.py:162
  96.3 4.5 %all-to-all-done.1.rows_ref = bf16[8,256,256]{2,1,0:T(8,128)(2,1)S(1)} async-done(((bf16[8,256,256]{2,1,0:T(8,128)(2,1)}), bf16[8,256,256]{2,1,0:T(8,128)(2,1)S(1)}, u32[]{:S(2)}, u32[]{:S(2)}) %all-to-all-start.1) | async-done | bytes 1048608 | tf_op jit(solution)/shard_map/all_to_all | solution.py:195
  100.8 1.4 shard_map.128
  102.2 25.9 %all_to_all.26 = bf16[16,256,128]{2,1,0:T(8,128)(2,1)S(1)} all-to-all(bf16[16,256,128]{2,1,0:T(8,128)(2,1)S(1)} %get-tuple-element.11), channel_id=1, replica_groups=mesh['tm'=32,'xl'=2,'y'=8,'dp'=2] {'xl','y'}, dimensions={0} | all-to-all | bytes 2097152 | tf_op jit(solution)/shard_map/all_to_all | solution.py:200
  128.9 10.0 %all-to-all-start.3 = ((bf16[32,16,128]{2,1,0:T(8,128)(2,1)}), bf16[32,16,128]{2,1,0:T(8,128)(2,1)S(1)}, u32[]{:S(2)}, u32[]{:S(2)}) async-start(bf16[32,16,128]{2,1,0:T(8,128)(2,1)} %copy_bitcast_fusion), calls=%async_computation.3 | async-start | bytes 262144 | tf_op jit(solution)/shard_map/all_to_all | solution.py:210
  138.9 0.9 copy-done.3
  140.8 1.1 slice_bitcast_fusion.4
  141.8 3.8 %collective-permute-start.8 = (bf16[1024,256]{1,0:T(8,128)(2,1)}, bf16[1024,256]{1,0:T(8,128)(2,1)S(1)}, u32[]{:S(2)}, u32[]{:S(2)}) collective-permute-start(bf16[1024,256]{1,0:T(8,128)(2,1)} %get-tuple-element.38), channel_id=1, source_target_pairs={{0,17},{17,0},{1,16},{16,1},{2,19},{19,2},{3,18},{18,3},{4,21},{21... | collective-permute-start | bytes 1572872 | tf_op jit(solution)/shard_map/ppermute | solution.py:205
  145.6 2.2 %collective-permute-start.7 = (bf16[1024,256]{1,0:T(8,128)(2,1)}, bf16[1024,256]{1,0:T(8,128)(2,1)}, u32[]{:S(2)}, u32[]{:S(2)}) collective-permute-start(bf16[1024,256]{1,0:T(8,128)(2,1)} %get-tuple-element.39), channel_id=1, source_target_pairs={{0,16},{16,0},{1,17},{17,1},{2,18},{18,2},{3,19},{19,3},{4,20},{20... | collective-permute-start | bytes 1572872 | tf_op jit(solution)/shard_map/ppermute | solution.py:204
  147.8 3.7 %collective-permute-start.6 = (bf16[1024,256]{1,0:T(8,128)(2,1)S(1)}, bf16[1024,256]{1,0:T(8,128)(2,1)}, u32[]{:S(2)}, u32[]{:S(2)}) collective-permute-start(bf16[1024,256]{1,0:T(8,128)(2,1)S(1)} %get-tuple-element.37), channel_id=1, source_target_pairs={{0,1},{1,0},{2,3},{3,2},{4,5},{5,4},{6,7},{7,6},{8,9},{9,8},{10,11... | collective-permute-start | bytes 1572872 | tf_op jit(solution)/shard_map/ppermute | solution.py:203
  151.4 3.3 %all-to-all-done.3 = bf16[32,16,128]{2,1,0:T(8,128)(2,1)S(1)} async-done(((bf16[32,16,128]{2,1,0:T(8,128)(2,1)}), bf16[32,16,128]{2,1,0:T(8,128)(2,1)S(1)}, u32[]{:S(2)}, u32[]{:S(2)}) %all-to-all-start.3) | async-done | bytes 131104 | tf_op jit(solution)/shard_map/all_to_all | solution.py:210
  155.0 0.9 broadcast_in_dim.82
  155.9 4.4 %all-to-all-start.4 = ((bf16[16,128,128]{2,1,0:T(8,128)(2,1)}), bf16[16,128,128]{2,1,0:T(8,128)(2,1)S(1)}, u32[]{:S(2)}, u32[]{:S(2)}) async-start(bf16[16,128,128]{2,1,0:T(8,128)(2,1)} %broadcast_in_dim.82), calls=%async_computation.4 | async-start | bytes 1048576 | tf_op jit(solution)/shard_map/all_to_all | solution.py:213
  160.8 16.7 %collective-permute-done.6 = bf16[1024,256]{1,0:T(8,128)(2,1)} collective-permute-done((bf16[1024,256]{1,0:T(8,128)(2,1)S(1)}, bf16[1024,256]{1,0:T(8,128)(2,1)}, u32[]{:S(2)}, u32[]{:S(2)}) %collective-permute-start.6) | collective-permute-done | bytes 524320 | tf_op jit(solution)/shard_map/ppermute | solution.py:203
  177.5 2.2 %convert_add_fusion.2 = (f32[512,256]{1,0:T(8,128)S(1)}, f32[1,512,256]{2,1,0:T(8,128)}) fusion(bf16[1024,256]{1,0:T(8,128)(2,1)S(1)} %collective-permute-done.8, bf16[1024,256]{1,0:T(8,128)(2,1)} %collective-permute-done.7, bf16[1024,256]{1,0:T(8,128)(2,1)} %collective-permute-done.6, f32[512,256]{1,0:T(8,128)S(1)} %get-tuple-element.14), kind=kLoop, calls=%fused_computation.229 | loop fusion | flops 1441792 | bytes 3145728 | tf_op jit(solution)/shard_map/add | solution.py:238
  179.7 0.9 add_bitcast_fusion
  181.8 4.9 %collective-permute-start.5 = (bf16[15,1024]{0,1:T(8,128)(2,1)S(1)}, bf16[15,1024]{0,1:T(8,128)(2,1)S(1)}, u32[]{:S(2)}, u32[]{:S(2)}) collective-permute-start(bf16[15,1024]{0,1:T(8,128)(2,1)S(1)} %get-tuple-element.45), channel_id=1, source_target_pairs={{0,32},{32,64},{64,96},{96,128},{128,160},{160,192},{192,224},{224... | collective-permute-start | bytes 92168 | tf_op jit(solution)/shard_map/ppermute | solution.py:25
  186.7 1.9 collective-permute-start.4
  190.4 4.0 %collective-permute-done.4 = bf16[15,1024]{0,1:T(8,128)(2,1)S(1)} collective-permute-done((bf16[15,1024]{0,1:T(8,128)(2,1)S(1)}, bf16[15,1024]{0,1:T(8,128)(2,1)S(1)}, u32[]{:S(2)}, u32[]{:S(2)}) %collective-permute-start.4) | collective-permute-done | bytes 30752 | tf_op jit(solution)/shard_map/ppermute | solution.py:26
  194.7 13.6 %fusion.129 = (bf16[1,128,1024]{1,2,0:T(8,128)(2,1)S(1)}, f32[128,1024]{0,1:T(8,128)S(1)}) fusion(bf16[128,2048]{0,1:T(8,128)(2,1)S(1)} %bitcast.120, f32[128,1024]{0,1:T(8,128)S(1)} %get-tuple-element.30, f32[15,1024]{0,1:T(8,128)S(1)} %convert_element_type.163, f32[1024]{0:T(1024)S(1)} %bitcast.150, f32[1024]{0:T(1024)S(1)} %bitcast.152, ...), kind=kLoop, calls=%fused_computation.240 | loop fusion | flops 12713984 | bytes 1822720 | tf_op jit(solution)/shard_map/concatenate | solution.py:228
  208.6 1.0 copy.43
  (184 shorter events, 10.4 us)
Async XLA Ops:
  0.6 19.6 %copy-start.11 = (f32[31,1024]{1,0:T(8,128)S(1)}, f32[31,1024]{1,0:T(8,128)}, u32[]{:S(2)}) copy-start(f32[31,1024]{1,0:T(8,128)} %param.11) | copy-start | bytes 380932
  0.6 20.0 %copy-start.10 = (bf16[1,128,1024]{2,1,0:T(8,128)(2,1)S(1)}, bf16[1,128,1024]{2,1,0:T(8,128)(2,1)}, u32[]{:S(2)}) copy-start(bf16[1,128,1024]{2,1,0:T(8,128)(2,1)} %param.9) | copy-start | bytes 786436
  0.7 20.2 %copy-start.70 = (s32[1,128]{1,0:T(1,128)S(1)}, s32[1,128]{1,0:T(1,128)}, u32[]{:S(2)}) copy-start(s32[1,128]{1,0:T(1,128)} %param.16) | copy-start | bytes 1540
  0.7 20.2 %copy-start.66 = (s32[1,128,2]{1,2,0:T(2,128)S(1)}, s32[1,128,2]{1,2,0:T(2,128)}, u32[]{:S(2)}) copy-start(s32[1,128,2]{1,2,0:T(2,128)} %param.14) | copy-start | bytes 3076
  0.7 21.1 %copy-start.67 = (f32[1,128,2]{1,2,0:T(2,128)S(1)}, f32[1,128,2]{1,2,0:T(2,128)}, u32[]{:S(2)}) copy-start(f32[1,128,2]{1,2,0:T(2,128)} %param.15) | copy-start | bytes 3076
  2.0 24.9 %copy-start.4 = (bf16[1,128,2048]{1,2,0:T(8,128)(2,1)}, bf16[1,128,2048]{1,2,0:T(8,128)(2,1)S(1)}, u32[]{:S(2)}) copy-start(bf16[1,128,2048]{1,2,0:T(8,128)(2,1)S(1)} %copy.32) | copy-start | bytes 1572868
  2.3 21.1 %collective-permute-start.1 = (bf16[15,2048]{0,1:T(8,128)(2,1)S(1)}, bf16[15,2048]{0,1:T(8,128)(2,1)S(1)}, u32[]{:S(2)}, u32[]{:S(2)}) collective-permute-start(bf16[15,2048]{0,1:T(8,128)(2,1)S(1)} %get-tuple-element.43), channel_id=1, source_target_pairs={{32,0},{64,32},{96,64},{128,96},{160,128},{192,160},{224,192},{256... | collective-permute-start | bytes 184328 | tf_op jit(solution)/shard_map/ppermute | solution.py:26
  18.3 8.0 %collective-permute-start = (bf16[15,2048]{0,1:T(8,128)(2,1)S(1)}, bf16[15,2048]{0,1:T(8,128)(2,1)S(1)}, u32[]{:S(2)}, u32[]{:S(2)}) collective-permute-start(bf16[15,2048]{0,1:T(8,128)(2,1)S(1)} %get-tuple-element.42), channel_id=1, source_target_pairs={{0,32},{32,64},{64,96},{96,128},{128,160},{160,192},{192,224},{224... | collective-permute-start | bytes 184328 | tf_op jit(solution)/shard_map/ppermute | solution.py:25
  37.3 34.3 %copy-start = (bf16[1,1024,256]{2,1,0:T(8,128)(2,1)S(1)}, bf16[1,1024,256]{2,1,0:T(8,128)(2,1)}, u32[]{:S(2)}) copy-start(bf16[1,1024,256]{2,1,0:T(8,128)(2,1)} %param.12) | copy-start | bytes 1572868
  37.3 37.5 %copy-start.1 = (bf16[1,256,1024]{2,1,0:T(8,128)(2,1)S(1)}, bf16[1,256,1024]{2,1,0:T(8,128)(2,1)}, u32[]{:S(2)}) copy-start(bf16[1,256,1024]{2,1,0:T(8,128)(2,1)} %param.13) | copy-start | bytes 1572868
  64.8 36.0 %all-to-all-start.1 = ((bf16[8,256,256]{2,1,0:T(8,128)(2,1)}), bf16[8,256,256]{2,1,0:T(8,128)(2,1)S(1)}, u32[]{:S(2)}, u32[]{:S(2)}) async-start(bf16[8,256,256]{2,1,0:T(8,128)(2,1)} %broadcast_in_dim.80), calls=%async_computation.1 | async-start | bytes 2097152 | tf_op jit(solution)/shard_map/all_to_all | solution.py:195
  71.6 13.4 %collective-permute-start.2 = (bf16[1024,256]{1,0:T(8,128)(2,1)S(1)}, bf16[1024,256]{1,0:T(8,128)(2,1)S(1)}, u32[]{:S(2)}, u32[]{:S(2)}) collective-permute-start(bf16[1024,256]{1,0:T(8,128)(2,1)S(1)} %bitcast.115), channel_id=1, source_target_pairs={{0,16},{16,0},{1,17},{17,1},{2,18},{18,2},{3,19},{19,3},{4,20},{20... | collective-permute-start | bytes 1572872 | tf_op jit(solution)/shard_map/ppermute | solution.py:161
  74.8 21.5 %collective-permute-start.3 = (bf16[256,1024]{1,0:T(8,128)(2,1)S(1)}, bf16[256,1024]{1,0:T(8,128)(2,1)S(1)}, u32[]{:S(2)}, u32[]{:S(2)}) collective-permute-start(bf16[256,1024]{1,0:T(8,128)(2,1)S(1)} %bitcast.117), channel_id=1, source_target_pairs={{0,16},{16,0},{1,17},{17,1},{2,18},{18,2},{3,19},{19,3},{4,20},{20... | collective-permute-start | bytes 1572872 | tf_op jit(solution)/shard_map/ppermute | solution.py:162
  102.2 25.9 %copy-start.2 = (bf16[2,256,256]{2,1,0:T(8,128)(2,1)}, bf16[2,256,256]{2,1,0:T(8,128)(2,1)S(1)}, u32[]{:S(2)}) copy-start(bf16[2,256,256]{2,1,0:T(8,128)(2,1)S(1)} %get-tuple-element.13.act_grad_ref) | copy-start | bytes 786436
  128.9 25.8 %all-to-all-start.3 = ((bf16[32,16,128]{2,1,0:T(8,128)(2,1)}), bf16[32,16,128]{2,1,0:T(8,128)(2,1)S(1)}, u32[]{:S(2)}, u32[]{:S(2)}) async-start(bf16[32,16,128]{2,1,0:T(8,128)(2,1)} %copy_bitcast_fusion), calls=%async_computation.3 | async-start | bytes 262144 | tf_op jit(solution)/shard_map/all_to_all | solution.py:210
  140.7 14.0 %copy-start.68 = (s32[256]{0:T(256)S(1)}, s32[256]{0:T(256)}, u32[]{:S(2)}) copy-start(s32[256]{0:T(256)} %get-tuple-element.77) | copy-start | bytes 3076
  140.7 14.0 %copy-start.69 = (f32[256]{0:T(256)S(1)}, f32[256]{0:T(256)}, u32[]{:S(2)}) copy-start(f32[256]{0:T(256)} %get-tuple-element.31) | copy-start | bytes 3076
  140.7 19.6 %copy-start.9 = (bf16[1,128,1024]{2,1,0:T(8,128)(2,1)S(1)}, bf16[1,128,1024]{2,1,0:T(8,128)(2,1)}, u32[]{:S(2)}) copy-start(bf16[1,128,1024]{2,1,0:T(8,128)(2,1)} %param.17) | copy-start | bytes 786436
  141.8 18.7 %collective-permute-start.8 = (bf16[1024,256]{1,0:T(8,128)(2,1)}, bf16[1024,256]{1,0:T(8,128)(2,1)S(1)}, u32[]{:S(2)}, u32[]{:S(2)}) collective-permute-start(bf16[1024,256]{1,0:T(8,128)(2,1)} %get-tuple-element.38), channel_id=1, source_target_pairs={{0,17},{17,0},{1,16},{16,1},{2,19},{19,2},{3,18},{18,3},{4,21},{21... | collective-permute-start | bytes 1572872 | tf_op jit(solution)/shard_map/ppermute | solution.py:205
  145.6 15.2 %collective-permute-start.7 = (bf16[1024,256]{1,0:T(8,128)(2,1)}, bf16[1024,256]{1,0:T(8,128)(2,1)}, u32[]{:S(2)}, u32[]{:S(2)}) collective-permute-start(bf16[1024,256]{1,0:T(8,128)(2,1)} %get-tuple-element.39), channel_id=1, source_target_pairs={{0,16},{16,0},{1,17},{17,1},{2,18},{18,2},{3,19},{19,3},{4,20},{20... | collective-permute-start | bytes 1572872 | tf_op jit(solution)/shard_map/ppermute | solution.py:204
  147.8 29.7 %collective-permute-start.6 = (bf16[1024,256]{1,0:T(8,128)(2,1)S(1)}, bf16[1024,256]{1,0:T(8,128)(2,1)}, u32[]{:S(2)}, u32[]{:S(2)}) collective-permute-start(bf16[1024,256]{1,0:T(8,128)(2,1)S(1)} %get-tuple-element.37), channel_id=1, source_target_pairs={{0,1},{1,0},{2,3},{3,2},{4,5},{5,4},{6,7},{7,6},{8,9},{9,8},{10,11... | collective-permute-start | bytes 1572872 | tf_op jit(solution)/shard_map/ppermute | solution.py:203
  155.9 24.7 %all-to-all-start.4 = ((bf16[16,128,128]{2,1,0:T(8,128)(2,1)}), bf16[16,128,128]{2,1,0:T(8,128)(2,1)S(1)}, u32[]{:S(2)}, u32[]{:S(2)}) async-start(bf16[16,128,128]{2,1,0:T(8,128)(2,1)} %broadcast_in_dim.82), calls=%async_computation.4 | async-start | bytes 1048576 | tf_op jit(solution)/shard_map/all_to_all | solution.py:213
  181.5 12.9 %copy-start.5 = (bf16[1,128,2048]{1,2,0:T(8,128)(2,1)S(1)}, bf16[1,128,2048]{1,2,0:T(8,128)(2,1)}, u32[]{:S(2)}) copy-start(bf16[1,128,2048]{1,2,0:T(8,128)(2,1)} %copy-done.4) | copy-start | bytes 1572868
  181.5 12.9 %copy-start.13 = (f32[1,1024]{1,0:T(1,128)S(1)}, f32[1,1024]{1,0:T(1,128)}, u32[]{:S(2)}) copy-start(f32[1,1024]{1,0:T(1,128)} %copy-done.12) | copy-start | bytes 12292
  181.5 12.9 %copy-start.15 = (f32[1,1024]{1,0:T(1,128)S(1)}, f32[1,1024]{1,0:T(1,128)}, u32[]{:S(2)}) copy-start(f32[1,1024]{1,0:T(1,128)} %copy-done.14) | copy-start | bytes 12292
  181.6 12.9 %copy-start.17 = (f32[1,1024]{1,0:T(1,128)S(1)}, f32[1,1024]{1,0:T(1,128)}, u32[]{:S(2)}) copy-start(f32[1,1024]{1,0:T(1,128)} %copy-done.16) | copy-start | bytes 12292
  181.6 12.9 %copy-start.19 = (f32[1,1024]{1,0:T(1,128)S(1)}, f32[1,1024]{1,0:T(1,128)}, u32[]{:S(2)}) copy-start(f32[1,1024]{1,0:T(1,128)} %copy-done.18) | copy-start | bytes 12292
  181.6 12.9 %copy-start.21 = (f32[1,1024]{1,0:T(1,128)S(1)}, f32[1,1024]{1,0:T(1,128)}, u32[]{:S(2)}) copy-start(f32[1,1024]{1,0:T(1,128)} %copy-done.20) | copy-start | bytes 12292
  181.6 12.9 %copy-start.23 = (f32[1,1024]{1,0:T(1,128)S(1)}, f32[1,1024]{1,0:T(1,128)}, u32[]{:S(2)}) copy-start(f32[1,1024]{1,0:T(1,128)} %copy-done.22) | copy-start | bytes 12292
  181.6 12.9 %copy-start.25 = (f32[1,1024]{1,0:T(1,128)S(1)}, f32[1,1024]{1,0:T(1,128)}, u32[]{:S(2)}) copy-start(f32[1,1024]{1,0:T(1,128)} %copy-done.24) | copy-start | bytes 12292
  181.8 8.6 %collective-permute-start.5 = (bf16[15,1024]{0,1:T(8,128)(2,1)S(1)}, bf16[15,1024]{0,1:T(8,128)(2,1)S(1)}, u32[]{:S(2)}, u32[]{:S(2)}) collective-permute-start(bf16[15,1024]{0,1:T(8,128)(2,1)S(1)} %get-tuple-element.45), channel_id=1, source_target_pairs={{0,32},{32,64},{64,96},{96,128},{128,160},{160,192},{192,224},{224... | collective-permute-start | bytes 92168 | tf_op jit(solution)/shard_map/ppermute | solution.py:25
  186.7 7.7 %collective-permute-start.4 = (bf16[15,1024]{0,1:T(8,128)(2,1)S(1)}, bf16[15,1024]{0,1:T(8,128)(2,1)S(1)}, u32[]{:S(2)}, u32[]{:S(2)}) collective-permute-start(bf16[15,1024]{0,1:T(8,128)(2,1)S(1)} %get-tuple-element.44), channel_id=1, source_target_pairs={{32,0},{64,32},{96,64},{128,96},{160,128},{192,160},{224,192},{256... | collective-permute-start | bytes 92168 | tf_op jit(solution)/shard_map/ppermute | solution.py:26
  (51 other events, 448.5 us)

commit v2 on v1

v2 whole, which is shorter than its diff:
```python
import jax
import jax.numpy as jnp
from jax import lax
from jax.experimental import pallas as pl
from jax.experimental.pallas import tpu as pltpu
from jax.sharding import Mesh, PartitionSpec as P

KERNEL = 31
HALF = KERNEL // 2
F32 = jnp.float32
BF16 = jnp.bfloat16
NT = (((1,), (1,)), ((), ()))
TN = (((0,), (0,)), ((), ()))


RIM = 16


def swish_slope(value):
    sig = jax.nn.sigmoid(value)
    return sig * (1.0 + value * (1.0 - sig))


def rims(top, bottom):
    size = lax.axis_size("tm")
    up = [(i, i + 1) for i in range(size - 1)]
    down = [(j, i) for i, j in up]
    return lax.ppermute(bottom, "tm", up), lax.ppermute(top, "tm", down)


def taps_sum(padded, taps, frames, start, step):
    total = None
    for residue in range(8):
        offsets = [(start + step * j, j) for j in range(KERNEL) if (start + step * j) % 8 == residue]
        reach = max(offset for offset, _ in offsets) - residue
        shifted = padded[residue : residue + reach + frames, :]
        for offset, j in offsets:
            base = offset - residue
            term = taps[j : j + 1, :] * shifted[base : base + frames]
            total = term if total is None else total + term
    return total


def glu(value, gate):
    return value.astype(F32) * jax.nn.sigmoid(gate.astype(F32))


def glu_conv(value, gate, before_value, before_gate, after_value, after_gate, taps, padded):
    frames = value.shape[0]
    padded[:RIM] = glu(before_value[...], before_gate[...])
    padded[RIM : RIM + frames] = glu(value[...], gate[...])
    padded[RIM + frames :] = glu(after_value[...], after_gate[...])
    return taps_sum(padded, taps, frames, RIM - HALF, 1)


def dispatch_kernel(
    where_ref,
    value,
    gate,
    before_value,
    before_gate,
    after_value,
    after_gate,
    taps,
    resid,
    out_grad,
    dest,
    scale,
    rows_ref,
    padded,
):
    frames = value.shape[0]
    conv = glu_conv(value, gate, before_value, before_gate, after_value, after_gate, taps, padded)
    hidden_in = (resid[...].astype(F32) + conv * jax.nn.sigmoid(conv)).astype(BF16)
    first = where_ref[0] == 0
    chosen = jnp.where(first, hidden_in.astype(F32), out_grad[...].astype(F32)).astype(BF16)
    total = rows_ref.shape[0]
    hot = dest[...] == lax.broadcasted_iota(jnp.int32, (total, 2 * frames), 0)
    factor = jnp.sum(jnp.where(hot, scale[...], 0.0), axis=1, keepdims=True)
    ones = jnp.where(hot, 1.0, 0.0)
    ones = (ones[:, :frames] + ones[:, frames:]).astype(BF16)
    rows = jnp.dot(ones, chosen, preferred_element_type=F32)
    rows_ref[...] = jnp.where(first, rows, rows * factor).astype(BF16)


def forward_kernel(
    value,
    gate,
    before_value,
    before_gate,
    after_value,
    after_gate,
    taps,
    resid,
    hidden_ref,
    slope_ref,
    padded,
):
    conv = glu_conv(value, gate, before_value, before_gate, after_value, after_gate, taps, padded)
    sig = jax.nn.sigmoid(conv)
    hidden_ref[...] = (resid[...].astype(F32) + conv * sig).astype(BF16)
    slope_ref[...] = sig * (1.0 + conv * (1.0 - sig))


def edges_kernel(part_ref, out_grad, slope, edges_ref):
    for at in range(part_ref.shape[0]):
        cols = slice(at * part_ref.shape[2], (at + 1) * part_ref.shape[2])
        hid_grad = out_grad[:, cols].astype(F32) + part_ref[at].astype(F32)
        edges_ref[:, cols] = (hid_grad * slope[:, cols]).astype(BF16)


def outputs_kernel(moe_ref, part_ref, hidden, out_grad, slope, block_ref, resid_ref, conv_grad_ref):
    block_ref[...] = (hidden[...].astype(F32) + moe_ref[0].astype(F32)).astype(BF16)
    hid_grad = out_grad[...].astype(F32) + part_ref[0].astype(F32)
    resid_ref[...] = hid_grad.astype(BF16)
    conv_grad_ref[...] = hid_grad * slope[...]


def backward_kernel(conv_grad, before, after, taps, glu_in, out, padded):
    frames, width = conv_grad.shape
    cols = padded.shape[1]

    def step(index, carry):
        at = pl.ds(pl.multiple_of(index * cols, cols), cols)
        at_gate = pl.ds(pl.multiple_of(width + index * cols, cols), cols)
        padded[:RIM] = before[:, at].astype(F32)
        padded[RIM : RIM + frames] = conv_grad[:, at]
        padded[RIM + frames :] = after[:, at].astype(F32)
        back = taps_sum(padded, taps[:, at], frames, RIM + HALF, -1)
        sig = jax.nn.sigmoid(glu_in[:, at_gate].astype(F32))
        grad = back * sig
        out[:, at] = grad.astype(BF16)
        out[:, at_gate] = (grad * glu_in[:, at].astype(F32) * (1.0 - sig)).astype(BF16)
        return carry

    lax.fori_loop(0, width // cols, step, 0)


def gather_columns(rows_ref, hid, grad):
    parts = rows_ref.shape[0] // 2
    cols = rows_ref.shape[2]
    for part in range(parts):
        side, at = divmod(part, parts // 2)
        hid[side, :, at * cols : (at + 1) * cols] = rows_ref[part]
        grad[side, :, at * cols : (at + 1) * cols] = rows_ref[parts + part]


def expert_kernel(rows_ref, win_a, win_b, wout_a, wout_b, act_ref, act_grad_ref, out_ref, hid, grad):
    gather_columns(rows_ref, hid, grad)
    width = hid.shape[2]
    result = [0.0, 0.0]
    part = [0.0, 0.0]
    for which, (w_in, w_out) in enumerate(((win_a, wout_a), (win_b, wout_b))):
        pre = sum(
            jnp.dot(hid[s], w_in[s * width : (s + 1) * width, :], preferred_element_type=F32)
            for s in range(2)
        )
        back = sum(
            lax.dot_general(
                grad[s], w_out[:, s * width : (s + 1) * width], NT, preferred_element_type=F32
            )
            for s in range(2)
        )
        sig = jax.nn.sigmoid(pre)
        act = (pre * sig).astype(BF16)
        act_grad = (back * (sig * (1.0 + pre * (1.0 - sig)))).astype(BF16)
        act_ref[which] = act
        act_grad_ref[which] = act_grad
        for s in range(2):
            result[s] += jnp.dot(
                act, w_out[:, s * width : (s + 1) * width], preferred_element_type=F32
            )
            part[s] += lax.dot_general(
                act_grad, w_in[s * width : (s + 1) * width, :], NT, preferred_element_type=F32
            )
    blocks = out_ref.shape[0] // 2
    cols = out_ref.shape[2]
    for index in range(blocks):
        side, at = divmod(index, blocks // 2)
        out_ref[index] = result[side][:, at * cols : (at + 1) * cols].astype(BF16)
        out_ref[blocks + index] = part[side][:, at * cols : (at + 1) * cols].astype(BF16)


def grads_kernel(
    dp_ref, rows_ref, act_ref, act_grad_ref, own_in, own_out, send_a, send_b, send_c, hid, grad
):
    gather_columns(rows_ref, hid, grad)
    mine = dp_ref[0]
    hidden = act_ref.shape[2]
    sends = [send_a, send_b, send_c]
    for which in range(2):
        for other in range(2):
            side = mine if other == 0 else 1 - mine
            g_in = lax.dot_general(hid[side], act_grad_ref[which], TN, preferred_element_type=F32)
            g_out = lax.dot_general(act_ref[which], grad[side], TN, preferred_element_type=F32)
            if which == 0 and other == 0:
                own_in[...] = g_in
                own_out[...] = g_out
            else:
                width = g_in.shape[0]
                send = sends.pop(0)
                send[:width] = g_in.astype(BF16)
                for piece in range(g_out.shape[1] // hidden):
                    send[width + piece * hidden : width + (piece + 1) * hidden] = g_out[
                        :, piece * hidden : (piece + 1) * hidden
                    ].astype(BF16)


def vmem(count):
    return [pl.BlockSpec(memory_space=pltpu.VMEM)] * count


def expert_rows(rows, win, win_other, wout, wout_other):
    parts, count, cols = rows.shape
    width = parts * cols // 2
    hidden = win.shape[1]
    flops = 16 * count * width * hidden
    return pl.pallas_call(
        expert_kernel,
        out_shape=(
            jax.ShapeDtypeStruct((2, count, hidden), BF16),
            jax.ShapeDtypeStruct((2, count, hidden), BF16),
            jax.ShapeDtypeStruct((parts, count, cols), BF16),
        ),
        in_specs=vmem(5),
        out_specs=tuple(vmem(3)),
        scratch_shapes=[pltpu.VMEM((2, count, width // 2), BF16)] * 2,
        compiler_params=pltpu.CompilerParams(vmem_limit_bytes=40 * 2**20),
        cost_estimate=pl.CostEstimate(flops=flops, bytes_accessed=5 * 2**20, transcendentals=0),
    )(rows, win, win_other, wout, wout_other)


def weight_grads(dp, rows, act, act_grad):
    parts, count, cols = rows.shape
    width = parts * cols // 2
    hidden = act.shape[2]
    return pl.pallas_call(
        grads_kernel,
        out_shape=(
            jax.ShapeDtypeStruct((width // 2, hidden), F32),
            jax.ShapeDtypeStruct((hidden, width // 2), F32),
        )
        + (jax.ShapeDtypeStruct((width, hidden), BF16),) * 3,
        in_specs=[pl.BlockSpec(memory_space=pltpu.SMEM)] + vmem(3),
        out_specs=tuple(vmem(5)),
        scratch_shapes=[pltpu.VMEM((2, count, width // 2), BF16)] * 2,
        compiler_params=pltpu.CompilerParams(vmem_limit_bytes=40 * 2**20),
        cost_estimate=pl.CostEstimate(
            flops=8 * count * width * hidden, bytes_accessed=5 * 2**20, transcendentals=0
        ),
    )(dp, rows, act, act_grad)


def glu_specs(frames, cols, blocks, place):
    def spec(rows, shift):
        return pl.BlockSpec((rows, cols), lambda i, *ref: (0, shift + place(i, *ref)))

    return [spec(rows, shift) for rows in (frames, RIM, RIM) for shift in (0, blocks)]


def dispatch_rows(where, glu_in, before, after, taps, resid, out_grad, dest, scale, total, cols):
    frames, width = resid.shape
    blocks = width // cols

    def place(i, ref):
        return ref[1]

    def spec(rows):
        return pl.BlockSpec((rows, cols), lambda i, ref: (0, place(i, ref)))

    whole = pl.BlockSpec((1, 2 * frames), lambda i, ref: (0, 0))
    return pl.pallas_call(
        dispatch_kernel,
        out_shape=jax.ShapeDtypeStruct((total, cols), BF16),
        grid_spec=pltpu.PrefetchScalarGridSpec(
            num_scalar_prefetch=1,
            grid=(1,),
            in_specs=glu_specs(frames, cols, blocks, place)
            + [spec(KERNEL), spec(frames), spec(frames), whole, whole],
            out_specs=pl.BlockSpec((total, cols), lambda i, ref: (0, 0)),
            scratch_shapes=[pltpu.VMEM((frames + 2 * RIM, cols), F32)],
        ),
        compiler_params=pltpu.CompilerParams(vmem_limit_bytes=16 * 2**20),
        cost_estimate=pl.CostEstimate(flops=2 * 10**7, bytes_accessed=2**20, transcendentals=0),
    )(where, glu_in, glu_in, before, before, after, after, taps, resid, out_grad, dest, scale)


def column(rows, cols):
    return pl.BlockSpec((rows, cols), lambda i: (0, i))


def forward_full(glu_in, before, after, taps, resid, cols):
    frames, width = resid.shape
    blocks = width // cols
    return pl.pallas_call(
        forward_kernel,
        grid=(blocks,),
        out_shape=(
            jax.ShapeDtypeStruct((frames, width), BF16),
            jax.ShapeDtypeStruct((frames, width), F32),
        ),
        in_specs=glu_specs(frames, cols, blocks, lambda i: i)
        + [column(KERNEL, cols), column(frames, cols)],
        out_specs=(column(frames, cols), column(frames, cols)),
        scratch_shapes=[pltpu.VMEM((frames + 2 * RIM, cols), F32)],
        compiler_params=pltpu.CompilerParams(vmem_limit_bytes=16 * 2**20),
        cost_estimate=pl.CostEstimate(flops=2 * 10**7, bytes_accessed=2**21, transcendentals=0),
    )(glu_in, glu_in, before, before, after, after, taps, resid)


def edge_rows(summed, out_grad, slope):
    blocks, frames, cols = summed.shape
    blocks //= 2
    width = blocks * cols
    last = frames // RIM - 1
    row = pl.BlockSpec((RIM, width), lambda i: (i * last, 0))
    return pl.pallas_call(
        edges_kernel,
        grid=(2,),
        out_shape=jax.ShapeDtypeStruct((2 * RIM, width), BF16),
        in_specs=[pl.BlockSpec((blocks, RIM, cols), lambda i: (1, i * last, 0)), row, row],
        out_specs=pl.BlockSpec((RIM, width), lambda i: (i, 0)),
        compiler_params=pltpu.CompilerParams(vmem_limit_bytes=16 * 2**20),
        cost_estimate=pl.CostEstimate(flops=10**5, bytes_accessed=2**18, transcendentals=0),
    )(summed, out_grad, slope)


def finish(summed, hidden_in, out_grad, slope):
    blocks, frames, cols = summed.shape
    blocks //= 2
    width = blocks * cols
    return pl.pallas_call(
        outputs_kernel,
        grid=(blocks,),
        out_shape=(
            jax.ShapeDtypeStruct((frames, width), BF16),
            jax.ShapeDtypeStruct((frames, width), BF16),
            jax.ShapeDtypeStruct((frames, width), F32),
        ),
        in_specs=[
            pl.BlockSpec((1, frames, cols), lambda i: (i, 0, 0)),
            pl.BlockSpec((1, frames, cols), lambda i: (blocks + i, 0, 0)),
        ]
        + [column(frames, cols)] * 3,
        out_specs=(column(frames, cols),) * 3,
        compiler_params=pltpu.CompilerParams(vmem_limit_bytes=16 * 2**20),
        cost_estimate=pl.CostEstimate(flops=10**6, bytes_accessed=2**21, transcendentals=0),
    )(summed, summed, hidden_in, out_grad, slope)


def backward_full(conv_grad, before, after, taps, glu_in, cols):
    frames = conv_grad.shape[0]
    return pl.pallas_call(
        backward_kernel,
        out_shape=jax.ShapeDtypeStruct(glu_in.shape, BF16),
        in_specs=vmem(5),
        out_specs=pl.BlockSpec(memory_space=pltpu.VMEM),
        scratch_shapes=[pltpu.VMEM((frames + 2 * RIM, cols), F32)],
        compiler_params=pltpu.CompilerParams(vmem_limit_bytes=16 * 2**20),
        cost_estimate=pl.CostEstimate(flops=2 * 10**7, bytes_accessed=2**21, transcendentals=0),
    )(conv_grad, before, after, taps, glu_in)


def shards(resid, glu_input, dw_kernel, w_in, w_out, expert_ids, mix_weights, frame_kept, out_grad):
    frames = resid.shape[1]
    width = resid.shape[2]
    experts = lax.axis_size("tm")
    ranks = lax.axis_size("y")
    capacity = 4 * frames // experts
    half_cap = capacity // 2
    cols = width // ranks
    xl = lax.axis_index("xl")
    y = lax.axis_index("y")
    dp = lax.axis_index("dp")
    weight_in = w_in[0]
    weight_out = w_out[0]
    swap = [(0, 1), (1, 0)]

    glu_in = glu_input[0]
    before, after = rims(glu_in[:RIM], glu_in[frames - RIM :])

    ids = expert_ids[0].T.reshape(-1)
    order = 2 * (jnp.arange(2 * frames) % frames) + jnp.arange(2 * frames) // frames
    earlier = (ids[:, None] == ids[None, :]) & (order[None, :] < order[:, None])
    slot = jnp.sum(earlier.astype(jnp.int32), axis=1)
    dest = ids * capacity + slot
    scale = (mix_weights[0] * frame_kept[0][:, None].astype(F32)).T.reshape(-1)
    pick = (dest[:, None] == jnp.arange(experts * capacity)[None, :]).astype(BF16)
    pick_scale = jnp.where(xl == 0, scale, 1.0)

    rows = dispatch_rows(
        jnp.stack([xl, y]),
        glu_in,
        before,
        after,
        dw_kernel,
        resid[0],
        out_grad[0],
        dest[None],
        scale[None],
        experts * capacity,
        cols,
    )
    rows = lax.all_to_all(rows.reshape(experts, capacity, cols), "tm", 0, 0, tiled=True)
    hidden_in, slope = forward_full(glu_in, before, after, dw_kernel, resid[0], cols)
    win_other = lax.ppermute(weight_in, "xl", swap)
    wout_other = lax.ppermute(weight_out, "xl", swap)
    rows, win_other, wout_other = lax.optimization_barrier((rows, win_other, wout_other))
    rows = rows.reshape(experts, 2, half_cap, cols).transpose(1, 0, 2, 3)
    rows = rows.reshape(2, 1, experts * half_cap, cols)
    rows = jnp.broadcast_to(rows, (2, ranks) + rows.shape[2:]).reshape((-1,) + rows.shape[2:])
    rows = lax.all_to_all(rows, ("xl", "y"), 0, 0, tiled=True)

    act, act_grad, parts = expert_rows(rows, weight_in, win_other, weight_out, wout_other)
    parts = lax.all_to_all(parts, ("xl", "y"), 0, 0, tiled=True)
    own_in, own_out, *send = weight_grads(dp.reshape(1), rows, act, act_grad)
    got = (
        lax.ppermute(send[0], "dp", swap),
        lax.ppermute(send[1], "xl", swap),
        lax.ppermute(send[2], ("xl", "dp"), [(0, 3), (3, 0), (1, 2), (2, 1)]),
    )

    parts = parts.reshape(2, ranks, experts, half_cap, cols).astype(F32).sum(axis=1)
    parts = parts.astype(BF16).transpose(1, 0, 2, 3).reshape(experts, capacity, cols)
    parts = lax.all_to_all(parts, "tm", 0, 0, tiled=True).reshape(experts * capacity, cols)
    picked = jnp.dot(pick, parts, preferred_element_type=F32) * pick_scale[:, None]
    summed = (picked[:frames] + picked[frames:]).astype(BF16)
    summed = lax.all_to_all(
        jnp.broadcast_to(summed[None], (2 * ranks,) + summed.shape), ("xl", "y"), 0, 0, tiled=True
    )

    edges = edge_rows(summed, out_grad[0], slope)
    before, after = rims(edges[:RIM], edges[RIM:])
    block_out, resid_grad, conv_grad = finish(summed, hidden_in, out_grad[0], slope)
    glu_grad = backward_full(conv_grad, before, after, dw_kernel, glu_in, cols)

    hidden = weight_in.shape[1]
    w_in_grad = own_in + sum(piece[: width // 2].astype(F32) for piece in got)
    rest = [
        piece[width // 2 :].reshape(-1, hidden, hidden).transpose(1, 0, 2).reshape(hidden, -1)
        for piece in got
    ]
    w_out_grad = own_out + sum(piece.astype(F32) for piece in rest)
    return (
        block_out[None],
        resid_grad[None],
        glu_grad[None],
        w_in_grad[None],
        w_out_grad[None],
    )


def solution(mesh):
    size = mesh.shape["expert"]
    axes = {"tm": mesh.shape["tm"], "xl": 2, "y": size // 2, "dp": mesh.shape["dp"]}
    split = Mesh(mesh.devices.reshape(tuple(axes.values())), tuple(axes))
    expert = ("xl", "y")
    return jax.shard_map(
        shards,
        mesh=split,
        in_specs=(
            P("dp", "tm", None),
            P("dp", "tm", None),
            P(),
            P("tm", None, expert),
            P("tm", expert, None),
            P("dp", "tm", None),
            P("dp", "tm", None),
            P("dp", "tm"),
            P("dp", "tm", None),
        ),
        out_specs=(
            P("dp", "tm", None),
            P("dp", "tm", None),
            P("dp", "tm", None),
            P("tm", "dp", expert),
            P("tm", expert, "dp"),
        ),
        check_vma=False,
    )
```

time: 210 us -> 196 us (0.933)
  other arithmetic: 29.8 us -> 2.37 us
  blocking collectives: 51.5 us -> 62.1 us
  Pallas kernels: 2.26 us -> 11 us
  local copies, waits for them, and re-layouts: 11.8 us -> 7.5 us
    ppermute x8, waiting for transfers between devices: 43.2 us -> 25.5 us  [the longest x1 11.2 us: shards(): lax.ppermute(send[1], 'xl', swap)]
    concatenate x3 -> x0, other arithmetic: 13.9 us -> none  [shards(): jnp.concatenate([glu_back * sig_gate, glu_back * value * sig_gate * (1.0...]
    all_to_all x1, waiting for transfers between devices: 3.31 us -> 15.8 us  [shards(): lax.all_to_all(parts, 'tm', 0, 0, tiled=True)]
    convert_element_type x7 -> x0, other arithmetic: 10.8 us -> none  [the longest x1 9.76 us: shards(): (resid[0].astype(F32) + conv * jax.nn.sigmoid(conv)).astype(BF16)]
    pallas_call x0 -> x5, Pallas kernels: none -> 8.73 us  [the longest x1 2.77 us: finish(): pl.pallas_call(outputs_kernel, grid=(blocks,), out_shape=(jax.ShapeDtypeS...]
    all_to_all x1, blocking collectives: 25.6 us -> 32.2 us  [shards(): rows = lax.all_to_all(rows, ('xl', 'y'), 0, 0, tiled=True)]
    all_to_all x1, waiting for transfers between devices: 4.53 us -> 10.2 us  [shards(): lax.all_to_all(rows.reshape(experts, capacity, cols), 'tm', 0, 0, tiled=T...]
    all_to_all x1, blocking collectives: 25.9 us -> 29.8 us  [shards(): parts = lax.all_to_all(parts, ('xl', 'y'), 0, 0, tiled=True)]
  transfers between devices with their start and end apart: 12 -> 12, of which waited for: 8 -> 5; matrix products, arithmetic and copies ran while one was open for 5% -> 1% of each run, Pallas kernels for 0% -> 4%
where the time goes in v2:
time: 196 us; the launch traced here: 195 us
  blocking collectives  62.1 us (32%)
  starting transfers between devices  59.6 us (30%)
  waiting for transfers between devices  51.5 us (26%)
  Pallas kernels  11 us (6%)
  local copies, waits for them, and re-layouts  7.5 us (4%)
  other arithmetic  2.37 us (1%)
    all_to_all x1, blocking collectives, shards(): rows = lax.all_to_all(rows, ('xl', 'y'), 0, 0, tiled=True)  32.2 us
    all_to_all x1, blocking collectives, shards(): parts = lax.all_to_all(parts, ('xl', 'y'), 0, 0, tiled=True)  29.8 us
    ppermute x4, starting transfers between devices, rims(): return (lax.ppermute(bottom, 'tm', up), lax.ppermute(top, 'tm', down))  23.7 us
    all_to_all x1, waiting for transfers between devices, shards(): lax.all_to_all(parts, 'tm', 0, 0, tiled=True)  15.8 us
    ppermute x1, waiting for transfers between devices, shards(): lax.ppermute(send[1], 'xl', swap)  11.2 us
    all_to_all x1, waiting for transfers between devices, shards(): lax.all_to_all(rows.reshape(experts, capacity, cols), 'tm', 0, 0, tiled=T...  10.2 us
    all_to_all x1, starting transfers between devices, shards(): lax.all_to_all(rows.reshape(experts, capacity, cols), 'tm', 0, 0, tiled=T...  8.65 us
    ppermute x1, waiting for transfers between devices, shards(): lax.ppermute(send[0], 'dp', swap)  8.51 us
  transfers between devices with their start and end apart: 12, of which 5 were waited for; matrix products, arithmetic and copies ran while one was open for 1% of the time, Pallas kernels for 4%

profile of v2, /device:TPU:1, one launch (start us, length us, event | category | flops | bytes accessed | tf_op | source)
XLA Modules:
  0.0 195.3 jit_solution(6834961162918985774)
XLA Ops:
  0.6 0.9 slice_bitcast_fusion
  1.6 16.1 %collective-permute-start.1 = (bf16[16,2048]{1,0:T(8,128)(2,1)S(1)}, bf16[16,2048]{1,0:T(8,128)(2,1)S(1)}, u32[]{:S(2)}, u32[]{:S(2)}) collective-permute-start(bf16[16,2048]{1,0:T(8,128)(2,1)S(1)} %get-tuple-element.41), channel_id=1, source_target_pairs={{32,0},{64,32},{96,64},{128,96},{160,128},{192,160},{224,192},{256... | collective-permute-start | bytes 196616 | tf_op jit(solution)/shard_map/ppermute | solution.py:28
  17.6 1.9 collective-permute-start
  19.6 1.9 collective-permute-start.2
  21.5 3.4 %collective-permute-start.3 = (bf16[256,1024]{1,0:T(8,128)(2,1)}, bf16[256,1024]{1,0:T(8,128)(2,1)S(1)}, u32[]{:S(2)}, u32[]{:S(2)}) collective-permute-start(bf16[256,1024]{1,0:T(8,128)(2,1)} %bitcast.76), channel_id=1, source_target_pairs={{0,16},{16,0},{1,17},{17,1},{2,18},{18,2},{3,19},{19,3},{4,20},{20... | collective-permute-start | bytes 1572872 | tf_op jit(solution)/shard_map/ppermute | solution.py:407
  27.0 1.0 copy-done
  28.1 0.9 copy-done.3
  29.0 0.9 copy-done.5
  29.9 1.6 shard_map.128
  31.6 8.6 %all-to-all-start = ((bf16[32,16,128]{2,1,0:T(8,128)(2,1)}), bf16[32,16,128]{2,1,0:T(8,128)(2,1)S(1)}, u32[]{:S(2)}, u32[]{:S(2)}) async-start(bf16[32,16,128]{2,1,0:T(8,128)(2,1)} %bitcast.18), calls=%async_computation | async-start | bytes 262144 | tf_op jit(solution)/shard_map/all_to_all | solution.py:404
  40.2 5.7 %collective-permute-done.3.wout_b = bf16[256,1024]{1,0:T(8,128)(2,1)S(1)} collective-permute-done((bf16[256,1024]{1,0:T(8,128)(2,1)}, bf16[256,1024]{1,0:T(8,128)(2,1)S(1)}, u32[]{:S(2)}, u32[]{:S(2)}) %collective-permute-start.3) | collective-permute-done | bytes 524320 | tf_op jit(solution)/shard_map/ppermute | solution.py:407
  45.9 10.2 %all-to-all-done = bf16[32,16,128]{2,1,0:T(8,128)(2,1)S(1)} async-done(((bf16[32,16,128]{2,1,0:T(8,128)(2,1)}), bf16[32,16,128]{2,1,0:T(8,128)(2,1)S(1)}, u32[]{:S(2)}, u32[]{:S(2)}) %all-to-all-start) | async-done | bytes 131104 | tf_op jit(solution)/shard_map/all_to_all | solution.py:404
  56.3 32.2 %all_to_all.25.rows_ref = bf16[16,256,128]{2,1,0:T(8,128)(2,1)S(1)} all-to-all(bf16[16,256,128]{2,1,0:T(8,128)(2,1)S(1)} %bitcast.79), channel_id=1, replica_groups=mesh['tm'=32,'xl'=2,'y'=8,'dp'=2] {'xl','y'}, dimensions={0} | all-to-all | bytes 2097152 | tf_op jit(solution)/shard_map/all_to_all | solution.py:412
  88.6 1.4 shard_map.129
  90.0 29.8 %all_to_all.26 = bf16[16,256,128]{2,1,0:T(8,128)(2,1)S(1)} all-to-all(bf16[16,256,128]{2,1,0:T(8,128)(2,1)S(1)} %get-tuple-element.24), channel_id=1, replica_groups=mesh['tm'=32,'xl'=2,'y'=8,'dp'=2] {'xl','y'}, dimensions={0} | all-to-all | bytes 2097152 | tf_op jit(solution)/shard_map/all_to_all | solution.py:415
  120.6 7.8 %all-to-all-start.3 = ((bf16[32,16,128]{2,1,0:T(8,128)(2,1)}), bf16[32,16,128]{2,1,0:T(8,128)(2,1)S(1)}, u32[]{:S(2)}, u32[]{:S(2)}) async-start(bf16[32,16,128]{2,1,0:T(8,128)(2,1)} %copy_bitcast_fusion), calls=%async_computation.3 | async-start | bytes 262144 | tf_op jit(solution)/shard_map/all_to_all | solution.py:425
  128.4 15.8 %all-to-all-done.3 = bf16[32,16,128]{2,1,0:T(8,128)(2,1)S(1)} async-done(((bf16[32,16,128]{2,1,0:T(8,128)(2,1)}), bf16[32,16,128]{2,1,0:T(8,128)(2,1)S(1)}, u32[]{:S(2)}, u32[]{:S(2)}) %all-to-all-start.3) | async-done | bytes 131104 | tf_op jit(solution)/shard_map/all_to_all | solution.py:425
  144.5 0.9 broadcast_in_dim.41
  145.4 4.7 %all-to-all-start.4 = ((bf16[16,128,128]{2,1,0:T(8,128)(2,1)}), bf16[16,128,128]{2,1,0:T(8,128)(2,1)S(1)}, u32[]{:S(2)}, u32[]{:S(2)}) async-start(bf16[16,128,128]{2,1,0:T(8,128)(2,1)} %broadcast_in_dim.41), calls=%async_computation.4 | async-start | bytes 1048576 | tf_op jit(solution)/shard_map/all_to_all | solution.py:428
  150.1 0.9 shard_map.134
  151.1 4.4 %collective-permute-start.6 = (bf16[1024,256]{1,0:T(8,128)(2,1)S(1)}, bf16[1024,256]{1,0:T(8,128)(2,1)S(1)}, u32[]{:S(2)}, u32[]{:S(2)}) collective-permute-start(bf16[1024,256]{1,0:T(8,128)(2,1)S(1)} %get-tuple-element.33), channel_id=1, source_target_pairs={{0,1},{1,0},{2,3},{3,2},{4,5},{5,4},{6,7},{7,6},{8,9},{9,8},{10,11... | collective-permute-start | bytes 1572872 | tf_op jit(solution)/shard_map/ppermute | solution.py:418
  155.4 2.7 %collective-permute-start.7 = (bf16[1024,256]{1,0:T(8,128)(2,1)S(1)}, bf16[1024,256]{1,0:T(8,128)(2,1)S(1)}, u32[]{:S(2)}, u32[]{:S(2)}) collective-permute-start(bf16[1024,256]{1,0:T(8,128)(2,1)S(1)} %get-tuple-element.34), channel_id=1, source_target_pairs={{0,16},{16,0},{1,17},{17,1},{2,18},{18,2},{3,19},{19,3},{4,20},{20... | collective-permute-start | bytes 1572872 | tf_op jit(solution)/shard_map/ppermute | solution.py:419
  158.1 2.5 %collective-permute-start.8 = (bf16[1024,256]{1,0:T(8,128)(2,1)S(1)}, bf16[1024,256]{1,0:T(8,128)(2,1)S(1)}, u32[]{:S(2)}, u32[]{:S(2)}) collective-permute-start(bf16[1024,256]{1,0:T(8,128)(2,1)S(1)} %get-tuple-element.35), channel_id=1, source_target_pairs={{0,17},{17,0},{1,16},{16,1},{2,19},{19,2},{3,18},{18,3},{4,21},{21... | collective-permute-start | bytes 1572872 | tf_op jit(solution)/shard_map/ppermute | solution.py:420
  160.6 2.1 %shard_map.130 = (bf16[128,1024]{1,0:T(8,128)(2,1)S(1)}, f32[128,1024]{1,0:T(8,128)S(1)}) custom-call(bf16[128,2048]{1,0:T(8,128)(2,1)S(1)} %bitcast.65, bf16[128,2048]{1,0:T(8,128)(2,1)S(1)} %bitcast.66, bf16[16,2048]{1,0:T(8,128)(2,1)S(1)} %collective-permute-done.before_value.before_gate, ...), custom_call_target="tpu_custom_call" | custom-call | flops 20000000 | bytes 2097152 | tf_op jit(solution)/shard_map/pallas_call | solution.py:295
  162.7 8.5 %collective-permute-done.6 = bf16[1024,256]{1,0:T(8,128)(2,1)S(1)} collective-permute-done((bf16[1024,256]{1,0:T(8,128)(2,1)S(1)}, bf16[1024,256]{1,0:T(8,128)(2,1)S(1)}, u32[]{:S(2)}, u32[]{:S(2)}) %collective-permute-start.6) | collective-permute-done | bytes 524320 | tf_op jit(solution)/shard_map/ppermute | solution.py:418
  171.2 11.2 %collective-permute-done.7 = bf16[1024,256]{1,0:T(8,128)(2,1)S(1)} collective-permute-done((bf16[1024,256]{1,0:T(8,128)(2,1)S(1)}, bf16[1024,256]{1,0:T(8,128)(2,1)S(1)}, u32[]{:S(2)}, u32[]{:S(2)}) %collective-permute-start.7) | collective-permute-done | bytes 524320 | tf_op jit(solution)/shard_map/ppermute | solution.py:419
  182.4 1.0 convert_add_fusion
  183.7 3.8 %collective-permute-start.5 = (bf16[16,1024]{1,0:T(8,128)(2,1)S(1)}, bf16[16,1024]{1,0:T(8,128)(2,1)S(1)}, u32[]{:S(2)}, u32[]{:S(2)}) collective-permute-start(bf16[16,1024]{1,0:T(8,128)(2,1)S(1)} %get-tuple-element.43), channel_id=1, source_target_pairs={{32,0},{64,32},{96,64},{128,96},{160,128},{192,160},{224,192},{256... | collective-permute-start | bytes 98312 | tf_op jit(solution)/shard_map/ppermute | solution.py:28
  187.5 1.9 collective-permute-start.4
  189.5 0.9 add_bitcast_fusion
  190.3 2.8 %shard_map.131 = (bf16[128,1024]{1,0:T(8,128)(2,1)}, bf16[128,1024]{1,0:T(8,128)(2,1)}, f32[128,1024]{1,0:T(8,128)S(1)}) custom-call(bf16[16,128,128]{2,1,0:T(8,128)(2,1)S(1)} %all-to-all-done.4.moe_ref.part_ref, bf16[16,128,128]{2,1,0:T(8,128)(2,1)S(1)} %all-to-all-done.4.moe_ref.part_ref, bf16[128,1024]{1,0:T(8,128)(2,1)S(1)} %get-tuple-element.25.hidden, ...), custom_call_target="tpu_custom_call" | custom-call | flops 1000000 | bytes 2097152 | tf_op jit(solution)/shard_map/pallas_call | solution.py:332
  193.1 2.2 %shard_map.133 = bf16[128,2048]{1,0:T(8,128)(2,1)} custom-call(f32[128,1024]{1,0:T(8,128)S(1)} %get-tuple-element.29.conv_grad, bf16[16,1024]{1,0:T(8,128)(2,1)S(1)} %collective-permute-done.4.before, bf16[16,1024]{1,0:T(8,128)(2,1)S(1)} %collective-permute-done.5.after, f32[31,1024]{1,0:T(8,128)S(1)} %copy-done.4, bf16[128,2048]{1,0:T(8,128)(2,1)S(1)} %bitcast.67), custom_call_target="tpu_custom_call" | custom-call | flops 20000000 | bytes 2097152 | tf_op jit(solution)/shard_map/pallas_call | solution.py:353
  (53 shorter events, 3.7 us)
Async XLA Ops:
  0.6 26.4 %copy-start.2 = (bf16[1,128,1024]{2,1,0:T(8,128)(2,1)S(1)}, bf16[1,128,1024]{2,1,0:T(8,128)(2,1)}, u32[]{:S(2)}) copy-start(bf16[1,128,1024]{2,1,0:T(8,128)(2,1)} %param.17) | copy-start | bytes 786436
  1.6 25.4 %collective-permute-start.1 = (bf16[16,2048]{1,0:T(8,128)(2,1)S(1)}, bf16[16,2048]{1,0:T(8,128)(2,1)S(1)}, u32[]{:S(2)}, u32[]{:S(2)}) collective-permute-start(bf16[16,2048]{1,0:T(8,128)(2,1)S(1)} %get-tuple-element.41), channel_id=1, source_target_pairs={{32,0},{64,32},{96,64},{128,96},{160,128},{192,160},{224,192},{256... | collective-permute-start | bytes 196616 | tf_op jit(solution)/shard_map/ppermute | solution.py:28
  17.6 9.4 %collective-permute-start = (bf16[16,2048]{1,0:T(8,128)(2,1)S(1)}, bf16[16,2048]{1,0:T(8,128)(2,1)S(1)}, u32[]{:S(2)}, u32[]{:S(2)}) collective-permute-start(bf16[16,2048]{1,0:T(8,128)(2,1)S(1)} %get-tuple-element.42), channel_id=1, source_target_pairs={{0,32},{32,64},{64,96},{96,128},{128,160},{160,192},{192,224},{224... | collective-permute-start | bytes 196616 | tf_op jit(solution)/shard_map/ppermute | solution.py:28
  19.6 20.6 %collective-permute-start.2 = (bf16[1024,256]{1,0:T(8,128)(2,1)}, bf16[1024,256]{1,0:T(8,128)(2,1)S(1)}, u32[]{:S(2)}, u32[]{:S(2)}) collective-permute-start(bf16[1024,256]{1,0:T(8,128)(2,1)} %bitcast.74), channel_id=1, source_target_pairs={{0,16},{16,0},{1,17},{17,1},{2,18},{18,2},{3,19},{19,3},{4,20},{20... | collective-permute-start | bytes 1572872 | tf_op jit(solution)/shard_map/ppermute | solution.py:406
  21.5 24.4 %collective-permute-start.3 = (bf16[256,1024]{1,0:T(8,128)(2,1)}, bf16[256,1024]{1,0:T(8,128)(2,1)S(1)}, u32[]{:S(2)}, u32[]{:S(2)}) collective-permute-start(bf16[256,1024]{1,0:T(8,128)(2,1)} %bitcast.76), channel_id=1, source_target_pairs={{0,16},{16,0},{1,17},{17,1},{2,18},{18,2},{3,19},{19,3},{4,20},{20... | collective-permute-start | bytes 1572872 | tf_op jit(solution)/shard_map/ppermute | solution.py:407
  24.9 0.7 copy-start.15
  25.6 0.7 copy-start.13
  26.2 0.7 copy-start.14
  27.0 1.0 copy-start
  28.1 0.9 copy-start.3
  29.0 0.9 copy-start.5
  31.6 24.5 %all-to-all-start = ((bf16[32,16,128]{2,1,0:T(8,128)(2,1)}), bf16[32,16,128]{2,1,0:T(8,128)(2,1)S(1)}, u32[]{:S(2)}, u32[]{:S(2)}) async-start(bf16[32,16,128]{2,1,0:T(8,128)(2,1)} %bitcast.18), calls=%async_computation | async-start | bytes 262144 | tf_op jit(solution)/shard_map/all_to_all | solution.py:404
  56.3 32.3 %copy-start.9 = (bf16[1,1024,256]{2,1,0:T(8,128)(2,1)S(1)}, bf16[1,1024,256]{2,1,0:T(8,128)(2,1)}, u32[]{:S(2)}) copy-start(bf16[1,1024,256]{2,1,0:T(8,128)(2,1)} %param.12) | copy-start | bytes 1572868
  56.3 32.3 %copy-start.10 = (bf16[1,256,1024]{2,1,0:T(8,128)(2,1)S(1)}, bf16[1,256,1024]{2,1,0:T(8,128)(2,1)}, u32[]{:S(2)}) copy-start(bf16[1,256,1024]{2,1,0:T(8,128)(2,1)} %param.13) | copy-start | bytes 1572868
  89.9 29.8 %copy-start.11 = (bf16[2,256,256]{2,1,0:T(8,128)(2,1)}, bf16[2,256,256]{2,1,0:T(8,128)(2,1)S(1)}, u32[]{:S(2)}) copy-start(bf16[2,256,256]{2,1,0:T(8,128)(2,1)S(1)} %get-tuple-element.31.act_grad_ref) | copy-start | bytes 786436
  120.6 23.6 %all-to-all-start.3 = ((bf16[32,16,128]{2,1,0:T(8,128)(2,1)}), bf16[32,16,128]{2,1,0:T(8,128)(2,1)S(1)}, u32[]{:S(2)}, u32[]{:S(2)}) async-start(bf16[32,16,128]{2,1,0:T(8,128)(2,1)} %copy_bitcast_fusion), calls=%async_computation.3 | async-start | bytes 262144 | tf_op jit(solution)/shard_map/all_to_all | solution.py:425
  145.4 4.7 %copy-start.12 = (bf16[2,256,256]{2,1,0:T(8,128)(2,1)S(1)}, bf16[2,256,256]{2,1,0:T(8,128)(2,1)}, u32[]{:S(2)}) copy-start(bf16[2,256,256]{2,1,0:T(8,128)(2,1)} %copy-done.11) | copy-start | bytes 786436
  145.4 38.1 %all-to-all-start.4 = ((bf16[16,128,128]{2,1,0:T(8,128)(2,1)}), bf16[16,128,128]{2,1,0:T(8,128)(2,1)S(1)}, u32[]{:S(2)}, u32[]{:S(2)}) async-start(bf16[16,128,128]{2,1,0:T(8,128)(2,1)} %broadcast_in_dim.41), calls=%async_computation.4 | async-start | bytes 1048576 | tf_op jit(solution)/shard_map/all_to_all | solution.py:428
  150.1 10.5 %copy-start.1 = (bf16[1,128,2048]{2,1,0:T(8,128)(2,1)S(1)}, bf16[1,128,2048]{2,1,0:T(8,128)(2,1)}, u32[]{:S(2)}) copy-start(bf16[1,128,2048]{2,1,0:T(8,128)(2,1)} %param.10) | copy-start | bytes 1572868
  150.1 10.5 %copy-start.4 = (f32[31,1024]{1,0:T(8,128)S(1)}, f32[31,1024]{1,0:T(8,128)}, u32[]{:S(2)}) copy-start(f32[31,1024]{1,0:T(8,128)} %taps.5) | copy-start | bytes 380932
  150.1 10.5 %copy-start.6 = (bf16[1,128,1024]{2,1,0:T(8,128)(2,1)S(1)}, bf16[1,128,1024]{2,1,0:T(8,128)(2,1)}, u32[]{:S(2)}) copy-start(bf16[1,128,1024]{2,1,0:T(8,128)(2,1)} %param.9) | copy-start | bytes 786436
  151.0 11.6 %copy-start.7 = (f32[256,512]{1,0:T(8,128)}, f32[256,512]{1,0:T(8,128)S(1)}, u32[]{:S(2)}) copy-start(f32[256,512]{1,0:T(8,128)S(1)} %get-tuple-element.36) | copy-start | bytes 1572868
  151.1 20.1 %collective-permute-start.6 = (bf16[1024,256]{1,0:T(8,128)(2,1)S(1)}, bf16[1024,256]{1,0:T(8,128)(2,1)S(1)}, u32[]{:S(2)}, u32[]{:S(2)}) collective-permute-start(bf16[1024,256]{1,0:T(8,128)(2,1)S(1)} %get-tuple-element.33), channel_id=1, source_target_pairs={{0,1},{1,0},{2,3},{3,2},{4,5},{5,4},{6,7},{7,6},{8,9},{9,8},{10,11... | collective-permute-start | bytes 1572872 | tf_op jit(solution)/shard_map/ppermute | solution.py:418
  155.4 27.0 %collective-permute-start.7 = (bf16[1024,256]{1,0:T(8,128)(2,1)S(1)}, bf16[1024,256]{1,0:T(8,128)(2,1)S(1)}, u32[]{:S(2)}, u32[]{:S(2)}) collective-permute-start(bf16[1024,256]{1,0:T(8,128)(2,1)S(1)} %get-tuple-element.34), channel_id=1, source_target_pairs={{0,16},{16,0},{1,17},{17,1},{2,18},{18,2},{3,19},{19,3},{4,20},{20... | collective-permute-start | bytes 1572872 | tf_op jit(solution)/shard_map/ppermute | solution.py:419
  158.1 24.3 %collective-permute-start.8 = (bf16[1024,256]{1,0:T(8,128)(2,1)S(1)}, bf16[1024,256]{1,0:T(8,128)(2,1)S(1)}, u32[]{:S(2)}, u32[]{:S(2)}) collective-permute-start(bf16[1024,256]{1,0:T(8,128)(2,1)S(1)} %get-tuple-element.35), channel_id=1, source_target_pairs={{0,17},{17,0},{1,16},{16,1},{2,19},{19,2},{3,18},{18,3},{4,21},{21... | collective-permute-start | bytes 1572872 | tf_op jit(solution)/shard_map/ppermute | solution.py:420
  183.5 5.9 %copy-start.8 = (f32[256,512]{1,0:T(8,128)S(1)}, f32[256,512]{1,0:T(8,128)}, u32[]{:S(2)}) copy-start(f32[256,512]{1,0:T(8,128)} %copy-done.7) | copy-start | bytes 1572868
  183.7 9.4 %collective-permute-start.5 = (bf16[16,1024]{1,0:T(8,128)(2,1)S(1)}, bf16[16,1024]{1,0:T(8,128)(2,1)S(1)}, u32[]{:S(2)}, u32[]{:S(2)}) collective-permute-start(bf16[16,1024]{1,0:T(8,128)(2,1)S(1)} %get-tuple-element.43), channel_id=1, source_target_pairs={{32,0},{64,32},{96,64},{128,96},{160,128},{192,160},{224,192},{256... | collective-permute-start | bytes 98312 | tf_op jit(solution)/shard_map/ppermute | solution.py:28
  187.5 5.6 %collective-permute-start.4 = (bf16[16,1024]{1,0:T(8,128)(2,1)S(1)}, bf16[16,1024]{1,0:T(8,128)(2,1)S(1)}, u32[]{:S(2)}, u32[]{:S(2)}) collective-permute-start(bf16[16,1024]{1,0:T(8,128)(2,1)S(1)} %get-tuple-element.44), channel_id=1, source_target_pairs={{0,32},{32,64},{64,96},{96,128},{128,160},{160,192},{192,224},{224... | collective-permute-start | bytes 98312 | tf_op jit(solution)/shard_map/ppermute | solution.py:28

commit v3 on v2

--- a/solution.py
+++ b/solution.py
@@ -1,3 +1,5 @@
+import functools
+
 import jax
 import jax.numpy as jnp
 from jax import lax
@@ -54,6 +56,7 @@
 
 
 def dispatch_kernel(
+    experts,
     where_ref,
     value,
     gate,
@@ -64,21 +67,42 @@
     taps,
     resid,
     out_grad,
-    dest,
-    scale,
+    ids,
+    mix,
+    kept,
     rows_ref,
+    dest_ref,
     padded,
 ):
     frames = value.shape[0]
+    total = rows_ref.shape[0]
     conv = glu_conv(value, gate, before_value, before_gate, after_value, after_gate, taps, padded)
     hidden_in = (resid[...].astype(F32) + conv * jax.nn.sigmoid(conv)).astype(BF16)
     first = where_ref[0] == 0
     chosen = jnp.where(first, hidden_in.astype(F32), out_grad[...].astype(F32)).astype(BF16)
-    total = rows_ref.shape[0]
-    hot = dest[...] == lax.broadcasted_iota(jnp.int32, (total, 2 * frames), 0)
-    factor = jnp.sum(jnp.where(hot, scale[...], 0.0), axis=1, keepdims=True)
-    ones = jnp.where(hot, 1.0, 0.0)
-    ones = (ones[:, :frames] + ones[:, frames:]).astype(BF16)
+    expert = lax.broadcasted_iota(jnp.int32, (experts, frames), 0)
+    named = [jnp.where(ids[k : k + 1, :] == expert, 1.0, 0.0) for k in range(2)]
+    earlier = lax.broadcasted_iota(jnp.int32, (frames, frames), 0) < lax.broadcasted_iota(
+        jnp.int32, (frames, frames), 1
+    )
+    ahead = jnp.dot(
+        (named[0] + named[1]).astype(BF16),
+        jnp.where(earlier, 1.0, 0.0).astype(BF16),
+        preferred_element_type=F32,
+    )
+    row = lax.broadcasted_iota(jnp.int32, (total, frames), 0)
+    ones = jnp.zeros((total, frames), F32)
+    factor = jnp.zeros((total, frames), F32)
+    for k in range(2):
+        slot = jnp.sum(named[k] * ahead, axis=0, keepdims=True).astype(jnp.int32)
+        dest = ids[k : k + 1, :] * (total // experts) + slot
+        dest_ref[k : k + 1, :] = dest
+        hot = row == dest
+        scale = mix[k : k + 1, :] * kept[...].astype(F32)
+        ones = jnp.where(hot, 1.0, ones)
+        factor = jnp.where(hot, scale, factor)
+    ones = ones.astype(BF16)
+    factor = jnp.sum(factor, axis=1, keepdims=True)
     rows = jnp.dot(ones, chosen, preferred_element_type=F32)
     rows_ref[...] = jnp.where(first, rows, rows * factor).astype(BF16)
 
@@ -109,11 +133,15 @@
         edges_ref[:, cols] = (hid_grad * slope[:, cols]).astype(BF16)
 
 
-def outputs_kernel(moe_ref, part_ref, hidden, out_grad, slope, block_ref, resid_ref, conv_grad_ref):
-    block_ref[...] = (hidden[...].astype(F32) + moe_ref[0].astype(F32)).astype(BF16)
-    hid_grad = out_grad[...].astype(F32) + part_ref[0].astype(F32)
-    resid_ref[...] = hid_grad.astype(BF16)
-    conv_grad_ref[...] = hid_grad * slope[...]
+def outputs_kernel(summed, hidden, out_grad, slope, block_ref, resid_ref, conv_grad_ref):
+    blocks = summed.shape[0] // 2
+    for at in range(blocks):
+        cols = slice(at * summed.shape[2], (at + 1) * summed.shape[2])
+        moe = summed[at].astype(F32)
+        block_ref[:, cols] = (hidden[:, cols].astype(F32) + moe).astype(BF16)
+        hid_grad = out_grad[:, cols].astype(F32) + summed[blocks + at].astype(F32)
+        resid_ref[:, cols] = hid_grad.astype(BF16)
+        conv_grad_ref[:, cols] = hid_grad * slope[:, cols]
 
 
 def backward_kernel(conv_grad, before, after, taps, glu_in, out, padded):
@@ -181,29 +209,27 @@
         out_ref[blocks + index] = part[side][:, at * cols : (at + 1) * cols].astype(BF16)
 
 
-def grads_kernel(
-    dp_ref, rows_ref, act_ref, act_grad_ref, own_in, own_out, send_a, send_b, send_c, hid, grad
-):
+def grads_kernel(pieces, dp_ref, rows_ref, act_ref, act_grad_ref, *refs):
+    *outs, hid, grad = refs
     gather_columns(rows_ref, hid, grad)
     mine = dp_ref[0]
     hidden = act_ref.shape[2]
-    sends = [send_a, send_b, send_c]
-    for which in range(2):
-        for other in range(2):
-            side = mine if other == 0 else 1 - mine
-            g_in = lax.dot_general(hid[side], act_grad_ref[which], TN, preferred_element_type=F32)
-            g_out = lax.dot_general(act_ref[which], grad[side], TN, preferred_element_type=F32)
-            if which == 0 and other == 0:
-                own_in[...] = g_in
-                own_out[...] = g_out
-            else:
-                width = g_in.shape[0]
-                send = sends.pop(0)
-                send[:width] = g_in.astype(BF16)
-                for piece in range(g_out.shape[1] // hidden):
-                    send[width + piece * hidden : width + (piece + 1) * hidden] = g_out[
-                        :, piece * hidden : (piece + 1) * hidden
-                    ].astype(BF16)
+    for which, other in pieces:
+        side = mine if other == 0 else 1 - mine
+        g_in = lax.dot_general(hid[side], act_grad_ref[which], TN, preferred_element_type=F32)
+        g_out = lax.dot_general(act_ref[which], grad[side], TN, preferred_element_type=F32)
+        if which == 0 and other == 0:
+            own_in, own_out, *outs = outs
+            own_in[...] = g_in
+            own_out[...] = g_out
+        else:
+            width = g_in.shape[0]
+            send, *outs = outs
+            send[:width] = g_in.astype(BF16)
+            for piece in range(g_out.shape[1] // hidden):
+                send[width + piece * hidden : width + (piece + 1) * hidden] = g_out[
+                    :, piece * hidden : (piece + 1) * hidden
+                ].astype(BF16)
 
 
 def vmem(count):
@@ -230,23 +256,28 @@
     )(rows, win, win_other, wout, wout_other)
 
 
-def weight_grads(dp, rows, act, act_grad):
+def weight_grads(pieces, dp, rows, act, act_grad):
     parts, count, cols = rows.shape
     width = parts * cols // 2
     hidden = act.shape[2]
-    return pl.pallas_call(
-        grads_kernel,
-        out_shape=(
-            jax.ShapeDtypeStruct((width // 2, hidden), F32),
-            jax.ShapeDtypeStruct((hidden, width // 2), F32),
-        )
-        + (jax.ShapeDtypeStruct((width, hidden), BF16),) * 3,
+    shapes = []
+    for piece in pieces:
+        if piece == (0, 0):
+            shapes.append(jax.ShapeDtypeStruct((width // 2, hidden), F32))
+            shapes.append(jax.ShapeDtypeStruct((hidden, width // 2), F32))
+        else:
+            shapes.append(jax.ShapeDtypeStruct((width, hidden), BF16))
+    return pl.pallas_call(
+        functools.partial(grads_kernel, pieces),
+        out_shape=tuple(shapes),
         in_specs=[pl.BlockSpec(memory_space=pltpu.SMEM)] + vmem(3),
-        out_specs=tuple(vmem(5)),
+        out_specs=tuple(vmem(len(shapes))),
         scratch_shapes=[pltpu.VMEM((2, count, width // 2), BF16)] * 2,
         compiler_params=pltpu.CompilerParams(vmem_limit_bytes=40 * 2**20),
         cost_estimate=pl.CostEstimate(
-            flops=8 * count * width * hidden, bytes_accessed=5 * 2**20, transcendentals=0
+            flops=2 * len(pieces) * count * width * hidden,
+            bytes_accessed=4 * 2**20,
+            transcendentals=0,
         ),
     )(dp, rows, act, act_grad)
 
@@ -258,7 +289,9 @@
     return [spec(rows, shift) for rows in (frames, RIM, RIM) for shift in (0, blocks)]
 
 
-def dispatch_rows(where, glu_in, before, after, taps, resid, out_grad, dest, scale, total, cols):
+def dispatch_rows(
+    where, glu_in, before, after, taps, resid, out_grad, ids, mix, kept, experts, total, cols
+):
     frames, width = resid.shape
     blocks = width // cols
 
@@ -268,21 +301,27 @@
     def spec(rows):
         return pl.BlockSpec((rows, cols), lambda i, ref: (0, place(i, ref)))
 
-    whole = pl.BlockSpec((1, 2 * frames), lambda i, ref: (0, 0))
-    return pl.pallas_call(
-        dispatch_kernel,
-        out_shape=jax.ShapeDtypeStruct((total, cols), BF16),
+    def whole(rows, columns):
+        return pl.BlockSpec((rows, columns), lambda i, ref: (0, 0))
+
+    return pl.pallas_call(
+        functools.partial(dispatch_kernel, experts),
+        out_shape=(
+            jax.ShapeDtypeStruct((total, cols), BF16),
+            jax.ShapeDtypeStruct((2, frames), jnp.int32),
+        ),
         grid_spec=pltpu.PrefetchScalarGridSpec(
             num_scalar_prefetch=1,
             grid=(1,),
             in_specs=glu_specs(frames, cols, blocks, place)
-            + [spec(KERNEL), spec(frames), spec(frames), whole, whole],
-            out_specs=pl.BlockSpec((total, cols), lambda i, ref: (0, 0)),
+            + [spec(KERNEL), spec(frames), spec(frames)]
+            + [whole(2, frames), whole(2, frames), whole(1, frames)],
+            out_specs=(whole(total, cols), whole(2, frames)),
             scratch_shapes=[pltpu.VMEM((frames + 2 * RIM, cols), F32)],
         ),
-        compiler_params=pltpu.CompilerParams(vmem_limit_bytes=16 * 2**20),
+        compiler_params=pltpu.CompilerParams(vmem_limit_bytes=56 * 2**20),
         cost_estimate=pl.CostEstimate(flops=2 * 10**7, bytes_accessed=2**20, transcendentals=0),
-    )(where, glu_in, glu_in, before, before, after, after, taps, resid, out_grad, dest, scale)
+    )(where, glu_in, glu_in, before, before, after, after, taps, resid, out_grad, ids, mix, kept)
 
 
 def column(rows, cols):
@@ -326,26 +365,15 @@
 
 
 def finish(summed, hidden_in, out_grad, slope):
-    blocks, frames, cols = summed.shape
-    blocks //= 2
-    width = blocks * cols
+    half = jax.ShapeDtypeStruct(hidden_in.shape, BF16)
     return pl.pallas_call(
         outputs_kernel,
-        grid=(blocks,),
-        out_shape=(
-            jax.ShapeDtypeStruct((frames, width), BF16),
-            jax.ShapeDtypeStruct((frames, width), BF16),
-            jax.ShapeDtypeStruct((frames, width), F32),
-        ),
-        in_specs=[
-            pl.BlockSpec((1, frames, cols), lambda i: (i, 0, 0)),
-            pl.BlockSpec((1, frames, cols), lambda i: (blocks + i, 0, 0)),
-        ]
-        + [column(frames, cols)] * 3,
-        out_specs=(column(frames, cols),) * 3,
+        out_shape=(half, half, jax.ShapeDtypeStruct(hidden_in.shape, F32)),
+        in_specs=vmem(4),
+        out_specs=tuple(vmem(3)),
         compiler_params=pltpu.CompilerParams(vmem_limit_bytes=16 * 2**20),
         cost_estimate=pl.CostEstimate(flops=10**6, bytes_accessed=2**21, transcendentals=0),
-    )(summed, summed, hidden_in, out_grad, slope)
+    )(summed, hidden_in, out_grad, slope)
 
 
 def backward_full(conv_grad, before, after, taps, glu_in, cols):
@@ -375,20 +403,14 @@
     weight_in = w_in[0]
     weight_out = w_out[0]
     swap = [(0, 1), (1, 0)]
+    swap_both = [(0, 3), (3, 0), (1, 2), (2, 1)]
 
     glu_in = glu_input[0]
     before, after = rims(glu_in[:RIM], glu_in[frames - RIM :])
 
-    ids = expert_ids[0].T.reshape(-1)
-    order = 2 * (jnp.arange(2 * frames) % frames) + jnp.arange(2 * frames) // frames
-    earlier = (ids[:, None] == ids[None, :]) & (order[None, :] < order[:, None])
-    slot = jnp.sum(earlier.astype(jnp.int32), axis=1)
-    dest = ids * capacity + slot
-    scale = (mix_weights[0] * frame_kept[0][:, None].astype(F32)).T.reshape(-1)
-    pick = (dest[:, None] == jnp.arange(experts * capacity)[None, :]).astype(BF16)
-    pick_scale = jnp.where(xl == 0, scale, 1.0)
-
-    rows = dispatch_rows(
+    ids = expert_ids[0].T
+    mix = mix_weights[0].T
+    rows, dest = dispatch_rows(
         jnp.stack([xl, y]),
         glu_in,
         before,
@@ -396,16 +418,17 @@
         dw_kernel,
         resid[0],
         out_grad[0],
-        dest[None],
-        scale[None],
+        ids,
+        mix,
+        frame_kept,
+        experts,
         experts * capacity,
         cols,
     )
     rows = lax.all_to_all(rows.reshape(experts, capacity, cols), "tm", 0, 0, tiled=True)
     hidden_in, slope = forward_full(glu_in, before, after, dw_kernel, resid[0], cols)
     win_other = lax.ppermute(weight_in, "xl", swap)
-    wout_other = lax.ppermute(weight_out, "xl", swap)
-    rows, win_other, wout_other = lax.optimization_barrier((rows, win_other, wout_other))
+    wout_other = lax.ppermute(weight_out, ("xl", "dp"), swap_both)
     rows = rows.reshape(experts, 2, half_cap, cols).transpose(1, 0, 2, 3)
     rows = rows.reshape(2, 1, experts * half_cap, cols)
     rows = jnp.broadcast_to(rows, (2, ranks) + rows.shape[2:]).reshape((-1,) + rows.shape[2:])
@@ -413,16 +436,21 @@
 
     act, act_grad, parts = expert_rows(rows, weight_in, win_other, weight_out, wout_other)
     parts = lax.all_to_all(parts, ("xl", "y"), 0, 0, tiled=True)
-    own_in, own_out, *send = weight_grads(dp.reshape(1), rows, act, act_grad)
-    got = (
-        lax.ppermute(send[0], "dp", swap),
-        lax.ppermute(send[1], "xl", swap),
-        lax.ppermute(send[2], ("xl", "dp"), [(0, 3), (3, 0), (1, 2), (2, 1)]),
-    )
+    pieces = [(0, 0), (0, 1), (1, 0), (1, 1)]
+    own_in, own_out, *send = weight_grads(pieces, dp.reshape(1), rows, act, act_grad)
+    got_both = lax.ppermute(send[2], ("xl", "dp"), swap_both)
+    got_xl = lax.ppermute(send[1], "xl", swap)
+    got_dp = lax.ppermute(send[0], "dp", swap)
+    parts, got_both, got_xl = lax.optimization_barrier((parts, got_both, got_xl))
 
     parts = parts.reshape(2, ranks, experts, half_cap, cols).astype(F32).sum(axis=1)
     parts = parts.astype(BF16).transpose(1, 0, 2, 3).reshape(experts, capacity, cols)
     parts = lax.all_to_all(parts, "tm", 0, 0, tiled=True).reshape(experts * capacity, cols)
+    parts, got_dp = lax.optimization_barrier((parts, got_dp))
+    got = (got_dp, got_xl, got_both)
+    scale = (mix * frame_kept.astype(F32)).reshape(-1)
+    pick = (dest.reshape(-1)[:, None] == jnp.arange(experts * capacity)[None, :]).astype(BF16)
+    pick_scale = jnp.where(xl == 0, scale, 1.0)
     picked = jnp.dot(pick, parts, preferred_element_type=F32) * pick_scale[:, None]
     summed = (picked[:frames] + picked[frames:]).astype(BF16)
     summed = lax.all_to_all(

time: 196 us -> 182 us (0.929)
  blocking collectives: 62.1 us -> 27.9 us
  starting transfers between devices: 59.6 us -> 68.6 us
  waiting for transfers between devices: 51.5 us -> 58.9 us
  other arithmetic: 2.37 us -> 4.86 us
    all_to_all x2 -> x1, blocking collectives: 62.1 us -> 27.9 us  [shards(): lax.all_to_all(rows.reshape(experts, capacity, cols), 'tm', 0, 0, tiled=T...]
    ppermute x1, waiting for transfers between devices: 0.01 us -> 18.2 us  [shards(): win_other = lax.ppermute(weight_in, 'xl', swap)]
    all_to_all x1 -> x2, waiting for transfers between devices: 10.2 us -> 0.01 us  [the longest x1 0.01 us: shards(): rows = lax.all_to_all(rows, ('xl', 'y'), 0, 0, tiled=True)]
    all_to_all x1, waiting for transfers between devices: 0.01 us -> 8.88 us  [shards(): lax.all_to_all(jnp.broadcast_to(summed[None], (2 * ranks,) + summed.shape...]
    ppermute x4, waiting for transfers between devices: 25.4 us -> 16.7 us  [the longest x1 9.54 us: shards(): got_xl = lax.ppermute(send[1], 'xl', swap)]
    all_to_all x1 -> x2, starting transfers between devices: 8.65 us -> 14.9 us  [the longest x1 7.98 us: shards(): rows = lax.all_to_all(rows, ('xl', 'y'), 0, 0, tiled=True)]
    all_to_all x1, waiting for transfers between devices: 15.8 us -> 13.4 us  [shards(): lax.all_to_all(parts, 'tm', 0, 0, tiled=True)]
    unnamed x32 -> x38, local copies, waits for them, and re-layouts: 4.74 us -> 5.1 us
  transfers between devices with their start and end apart: 12 -> 13, of which waited for: 5 -> 8; matrix products, arithmetic and copies ran while one was open for 1% -> 3% of each run, Pallas kernels for 4% -> 2%
where the time goes in v3:
time: 182 us; the launch traced here: 181 us
  starting transfers between devices  68.6 us (38%)
  waiting for transfers between devices  58.9 us (32%)
  blocking collectives  27.9 us (15%)
  Pallas kernels  11.1 us (6%)
  local copies, waits for them, and re-layouts  8.82 us (5%)
  other arithmetic  4.86 us (3%)
    all_to_all x1, blocking collectives, shards(): lax.all_to_all(rows.reshape(experts, capacity, cols), 'tm', 0, 0, tiled=T...  27.9 us
    ppermute x4, starting transfers between devices, rims(): return (lax.ppermute(bottom, 'tm', up), lax.ppermute(top, 'tm', down))  24.1 us
    ppermute x1, waiting for transfers between devices, shards(): win_other = lax.ppermute(weight_in, 'xl', swap)  18.2 us
    all_to_all x1, waiting for transfers between devices, shards(): lax.all_to_all(parts, 'tm', 0, 0, tiled=True)  13.4 us
    ppermute x1, waiting for transfers between devices, shards(): got_xl = lax.ppermute(send[1], 'xl', swap)  9.54 us
    all_to_all x1, waiting for transfers between devices, shards(): lax.all_to_all(jnp.broadcast_to(summed[None], (2 * ranks,) + summed.shape...  8.88 us
    all_to_all x1, starting transfers between devices, shards(): rows = lax.all_to_all(rows, ('xl', 'y'), 0, 0, tiled=True)  7.98 us
    all_to_all x1, starting transfers between devices, shards(): parts = lax.all_to_all(parts, ('xl', 'y'), 0, 0, tiled=True)  6.96 us
  transfers between devices with their start and end apart: 13, of which 8 were waited for; matrix products, arithmetic and copies ran while one was open for 3% of the time, Pallas kernels for 2%

profile of v3, /device:TPU:1, one launch (start us, length us, event | category | flops | bytes accessed | tf_op | source)
XLA Modules:
  0.0 181.5 jit_solution(6021747700094713352)
XLA Ops:
  1.5 5.4 %collective-permute-start = (bf16[16,2048]{1,0:T(8,128)(2,1)S(1)}, bf16[16,2048]{1,0:T(8,128)(2,1)S(1)}, u32[]{:S(2)}, u32[]{:S(2)}) collective-permute-start(bf16[16,2048]{1,0:T(8,128)(2,1)S(1)} %get-tuple-element.48), channel_id=1, source_target_pairs={{0,32},{32,64},{64,96},{96,128},{128,160},{160,192},{192,224},{224... | collective-permute-start | bytes 196616 | tf_op jit(solution)/shard_map/ppermute | solution.py:30
  6.9 12.0 %collective-permute-start.1 = (bf16[16,2048]{1,0:T(8,128)(2,1)S(1)}, bf16[16,2048]{1,0:T(8,128)(2,1)S(1)}, u32[]{:S(2)}, u32[]{:S(2)}) collective-permute-start(bf16[16,2048]{1,0:T(8,128)(2,1)S(1)} %get-tuple-element.47), channel_id=1, source_target_pairs={{32,0},{64,32},{96,64},{128,96},{160,128},{192,160},{224,192},{256... | collective-permute-start | bytes 196616 | tf_op jit(solution)/shard_map/ppermute | solution.py:30
  20.4 2.6 %shard_map.128 = (bf16[512,128]{1,0:T(8,128)(2,1)}, s32[2,128]{1,0:T(2,128)}) custom-call(s32[2]{0:T(128)} %pad_add_fusion.where_ref, bf16[128,2048]{1,0:T(8,128)(2,1)} %bitcast.53, bf16[128,2048]{1,0:T(8,128)(2,1)} %bitcast.54, bf16[16,2048]{1,0:T(8,128)(2,1)} %copy-done.4, bf16[16,2048]{1,0:T(8,128)(2,1)} %copy-done.4, bf16[16,2048]{1,0:T(8,128)(2,1)} %copy-done.6, ...), custom_call_target="tpu_custom_call" | custom-call | flops 20000000 | bytes 1048576 | tf_op jit(solution)/shard_map/pallas_call | solution.py:307
  23.0 27.9 %all_to_all.25 = bf16[32,16,128]{2,1,0:T(8,128)(2,1)S(1)} all-to-all(bf16[32,16,128]{2,1,0:T(8,128)(2,1)} %bitcast.71), channel_id=1, replica_groups=mesh['tm'=32,'xl'=2,'y'=8,'dp'=2] {'tm'}, dimensions={0} | all-to-all | bytes 262144 | tf_op jit(solution)/shard_map/all_to_all | solution.py:428
  50.9 1.2 broadcast_in_dim.35
  52.1 8.0 %all-to-all-start.1 = ((bf16[16,256,128]{2,1,0:T(8,128)(2,1)}), bf16[16,256,128]{2,1,0:T(8,128)(2,1)S(1)}, u32[]{:S(2)}, u32[]{:S(2)}) async-start(bf16[16,256,128]{2,1,0:T(8,128)(2,1)} %bitcast.16), calls=%async_computation.1 | async-start | bytes 2097152 | tf_op jit(solution)/shard_map/all_to_all | solution.py:435
  60.1 3.3 %collective-permute-start.2 = (bf16[1024,256]{1,0:T(8,128)(2,1)S(1)}, bf16[1024,256]{1,0:T(8,128)(2,1)S(1)}, u32[]{:S(2)}, u32[]{:S(2)}) collective-permute-start(bf16[1024,256]{1,0:T(8,128)(2,1)S(1)} %bitcast.63), channel_id=1, source_target_pairs={{0,16},{16,0},{1,17},{17,1},{2,18},{18,2},{3,19},{19,3},{4,20},{20... | collective-permute-start | bytes 1572872 | tf_op jit(solution)/shard_map/ppermute | solution.py:430
  63.4 3.3 %collective-permute-start.3 = (bf16[256,1024]{1,0:T(8,128)(2,1)S(1)}, bf16[256,1024]{1,0:T(8,128)(2,1)S(1)}, u32[]{:S(2)}, u32[]{:S(2)}) collective-permute-start(bf16[256,1024]{1,0:T(8,128)(2,1)S(1)} %bitcast.65), channel_id=1, source_target_pairs={{0,17},{17,0},{1,16},{16,1},{2,19},{19,2},{3,18},{18,3},{4,21},{21... | collective-permute-start | bytes 1572872 | tf_op jit(solution)/shard_map/ppermute | solution.py:431
  66.7 18.2 %collective-permute-done.2.win_b = bf16[1024,256]{1,0:T(8,128)(2,1)S(1)} collective-permute-done((bf16[1024,256]{1,0:T(8,128)(2,1)S(1)}, bf16[1024,256]{1,0:T(8,128)(2,1)S(1)}, u32[]{:S(2)}, u32[]{:S(2)}) %collective-permute-start.2) | collective-permute-done | bytes 524320 | tf_op jit(solution)/shard_map/ppermute | solution.py:430
  85.0 2.4 %shard_map.129 = (bf16[2,256,256]{2,1,0:T(8,128)(2,1)S(1)}, bf16[2,256,256]{2,1,0:T(8,128)(2,1)S(1)}, bf16[16,256,128]{2,1,0:T(8,128)(2,1)}) custom-call(bf16[16,256,128]{2,1,0:T(8,128)(2,1)S(1)} %all-to-all-done.1.rows_ref, bf16[1024,256]{1,0:T(8,128)(2,1)S(1)} %bitcast.64, bf16[1024,256]{1,0:T(8,128)(2,1)S(1)} %collective-permute-done.2.win_b, ...), custom_call_target="tpu_custom_call" | custom-call | flops 1073741824 | bytes 5242880 | tf_op jit(solution)/shard_map/pallas_call | solution.py:244
  88.0 7.0 %all-to-all-start.2 = ((bf16[16,256,128]{2,1,0:T(8,128)(2,1)}), bf16[16,256,128]{2,1,0:T(8,128)(2,1)}, u32[]{:S(2)}, u32[]{:S(2)}) async-start(bf16[16,256,128]{2,1,0:T(8,128)(2,1)} %get-tuple-element.27), calls=%async_computation.2 | async-start | bytes 2097152 | tf_op jit(solution)/shard_map/all_to_all | solution.py:438
  95.0 0.9 copy-done.11
  95.9 0.9 shard_map.130
  96.8 4.5 %collective-permute-start.4 = (bf16[1024,256]{1,0:T(8,128)(2,1)S(1)}, bf16[1024,256]{1,0:T(8,128)(2,1)S(1)}, u32[]{:S(2)}, u32[]{:S(2)}) collective-permute-start(bf16[1024,256]{1,0:T(8,128)(2,1)S(1)} %get-tuple-element.30), channel_id=1, source_target_pairs={{0,17},{17,0},{1,16},{16,1},{2,19},{19,2},{3,18},{18,3},{4,21},{21... | collective-permute-start | bytes 1572872 | tf_op jit(solution)/shard_map/ppermute | solution.py:441
  101.3 1.9 %collective-permute-start.5 = (bf16[1024,256]{1,0:T(8,128)(2,1)S(1)}, bf16[1024,256]{1,0:T(8,128)(2,1)}, u32[]{:S(2)}, u32[]{:S(2)}) collective-permute-start(bf16[1024,256]{1,0:T(8,128)(2,1)S(1)} %get-tuple-element.31), channel_id=1, source_target_pairs={{0,16},{16,0},{1,17},{17,1},{2,18},{18,2},{3,19},{19,3},{4,20},{20... | collective-permute-start | bytes 1572872 | tf_op jit(solution)/shard_map/ppermute | solution.py:442
  103.3 3.2 %collective-permute-start.6 = (bf16[1024,256]{1,0:T(8,128)(2,1)S(1)}, bf16[1024,256]{1,0:T(8,128)(2,1)S(1)}, u32[]{:S(2)}, u32[]{:S(2)}) collective-permute-start(bf16[1024,256]{1,0:T(8,128)(2,1)S(1)} %get-tuple-element.33), channel_id=1, source_target_pairs={{0,1},{1,0},{2,3},{3,2},{4,5},{5,4},{6,7},{7,6},{8,9},{9,8},{10,11... | collective-permute-start | bytes 1572872 | tf_op jit(solution)/shard_map/ppermute | solution.py:443
  106.5 5.7 %collective-permute-done.4 = bf16[1024,256]{1,0:T(8,128)(2,1)S(1)} collective-permute-done((bf16[1024,256]{1,0:T(8,128)(2,1)S(1)}, bf16[1024,256]{1,0:T(8,128)(2,1)S(1)}, u32[]{:S(2)}, u32[]{:S(2)}) %collective-permute-start.4) | collective-permute-done | bytes 524320 | tf_op jit(solution)/shard_map/ppermute | solution.py:441
  112.9 9.5 %collective-permute-done.5 = bf16[1024,256]{1,0:T(8,128)(2,1)} collective-permute-done((bf16[1024,256]{1,0:T(8,128)(2,1)S(1)}, bf16[1024,256]{1,0:T(8,128)(2,1)}, u32[]{:S(2)}, u32[]{:S(2)}) %collective-permute-start.5) | collective-permute-done | bytes 524320 | tf_op jit(solution)/shard_map/ppermute | solution.py:442
  122.5 1.4 reduce_sum.12
  124.5 6.9 %all-to-all-start.3 = ((bf16[32,16,128]{2,1,0:T(8,128)(2,1)}), bf16[32,16,128]{2,1,0:T(8,128)(2,1)S(1)}, u32[]{:S(2)}, u32[]{:S(2)}) async-start(bf16[32,16,128]{2,1,0:T(8,128)(2,1)} %copy_bitcast_fusion), calls=%async_computation.3 | async-start | bytes 262144 | tf_op jit(solution)/shard_map/all_to_all | solution.py:448
  132.8 1.5 collective-permute-done.6
  134.2 13.4 %all-to-all-done.3 = bf16[32,16,128]{2,1,0:T(8,128)(2,1)S(1)} async-done(((bf16[32,16,128]{2,1,0:T(8,128)(2,1)}), bf16[32,16,128]{2,1,0:T(8,128)(2,1)S(1)}, u32[]{:S(2)}, u32[]{:S(2)}) %all-to-all-start.3) | async-done | bytes 131104 | tf_op jit(solution)/shard_map/all_to_all | solution.py:448
  148.6 0.9 broadcast_in_dim.37
  149.5 6.5 %all-to-all-start.4 = ((bf16[16,128,128]{2,1,0:T(8,128)(2,1)}), bf16[16,128,128]{2,1,0:T(8,128)(2,1)S(1)}, u32[]{:S(2)}, u32[]{:S(2)}) async-start(bf16[16,128,128]{2,1,0:T(8,128)(2,1)} %broadcast_in_dim.37), calls=%async_computation.4 | async-start | bytes 1048576 | tf_op jit(solution)/shard_map/all_to_all | solution.py:456
  156.1 2.1 %shard_map.131 = (bf16[128,1024]{1,0:T(8,128)(2,1)S(1)}, f32[128,1024]{1,0:T(8,128)S(1)}) custom-call(bf16[128,2048]{1,0:T(8,128)(2,1)S(1)} %bitcast.55, bf16[128,2048]{1,0:T(8,128)(2,1)S(1)} %bitcast.56, bf16[16,2048]{1,0:T(8,128)(2,1)S(1)} %copy-done.5, bf16[16,2048]{1,0:T(8,128)(2,1)S(1)} %copy-done.5, bf16[16,2048]{1,0:T(8,128)(2,1)S(1)} %copy-done.7, ...), custom_call_target="tpu_custom_call" | custom-call | flops 20000000 | bytes 2097152 | tf_op jit(solution)/shard_map/pallas_call | solution.py:334
  158.2 2.0 %convert_add_fusion = (f32[512,256]{1,0:T(8,128)S(1)}, f32[1,512,256]{2,1,0:T(8,128)}) fusion(bf16[1024,256]{1,0:T(8,128)(2,1)S(1)} %copy-done.13, bf16[1024,256]{1,0:T(8,128)(2,1)} %collective-permute-done.5, bf16[1024,256]{1,0:T(8,128)(2,1)S(1)} %copy-done.15, f32[512,256]{1,0:T(8,128)S(1)} %get-tuple-element.40), kind=kLoop, calls=%fused_computation.1 | loop fusion | flops 1441792 | bytes 3145728 | tf_op jit(solution)/shard_map/add | solution.py:471
  160.3 8.9 %all-to-all-done.4.summed.part_ref = bf16[16,128,128]{2,1,0:T(8,128)(2,1)S(1)} async-done(((bf16[16,128,128]{2,1,0:T(8,128)(2,1)}), bf16[16,128,128]{2,1,0:T(8,128)(2,1)S(1)}, u32[]{:S(2)}, u32[]{:S(2)}) %all-to-all-start.4) | async-done | bytes 524320 | tf_op jit(solution)/shard_map/all_to_all | solution.py:456
  169.3 4.8 %collective-permute-start.7 = (bf16[16,1024]{1,0:T(8,128)(2,1)S(1)}, bf16[16,1024]{1,0:T(8,128)(2,1)S(1)}, u32[]{:S(2)}, u32[]{:S(2)}) collective-permute-start(bf16[16,1024]{1,0:T(8,128)(2,1)S(1)} %get-tuple-element.50), channel_id=1, source_target_pairs={{0,32},{32,64},{64,96},{96,128},{128,160},{160,192},{192,224},{224... | collective-permute-start | bytes 98312 | tf_op jit(solution)/shard_map/ppermute | solution.py:30
  174.1 1.9 %collective-permute-start.8 = (bf16[16,1024]{1,0:T(8,128)(2,1)S(1)}, bf16[16,1024]{1,0:T(8,128)(2,1)S(1)}, u32[]{:S(2)}, u32[]{:S(2)}) collective-permute-start(bf16[16,1024]{1,0:T(8,128)(2,1)S(1)} %get-tuple-element.49), channel_id=1, source_target_pairs={{32,0},{64,32},{96,64},{128,96},{160,128},{192,160},{224,192},{256... | collective-permute-start | bytes 98312 | tf_op jit(solution)/shard_map/ppermute | solution.py:30
  176.9 1.0 shard_map.132
  177.8 1.5 collective-permute-done.8.after
  179.3 2.2 %shard_map.134 = bf16[128,2048]{1,0:T(8,128)(2,1)} custom-call(f32[128,1024]{1,0:T(8,128)S(1)} %get-tuple-element.39.conv_grad, bf16[16,1024]{1,0:T(8,128)(2,1)S(1)} %collective-permute-done.7.before, bf16[16,1024]{1,0:T(8,128)(2,1)S(1)} %collective-permute-done.8.after, f32[31,1024]{1,0:T(8,128)S(1)} %copy-done.2, bf16[128,2048]{1,0:T(8,128)(2,1)S(1)} %bitcast.57), custom_call_target="tpu_custom_call" | custom-call | flops 20000000 | bytes 2097152 | tf_op jit(solution)/shard_map/pallas_call | solution.py:381
  (55 shorter events, 7.9 us)
Async XLA Ops:
  1.5 18.0 %collective-permute-start = (bf16[16,2048]{1,0:T(8,128)(2,1)S(1)}, bf16[16,2048]{1,0:T(8,128)(2,1)S(1)}, u32[]{:S(2)}, u32[]{:S(2)}) collective-permute-start(bf16[16,2048]{1,0:T(8,128)(2,1)S(1)} %get-tuple-element.48), channel_id=1, source_target_pairs={{0,32},{32,64},{64,96},{96,128},{128,160},{160,192},{192,224},{224... | collective-permute-start | bytes 196616 | tf_op jit(solution)/shard_map/ppermute | solution.py:30
  6.9 12.9 %collective-permute-start.1 = (bf16[16,2048]{1,0:T(8,128)(2,1)S(1)}, bf16[16,2048]{1,0:T(8,128)(2,1)S(1)}, u32[]{:S(2)}, u32[]{:S(2)}) collective-permute-start(bf16[16,2048]{1,0:T(8,128)(2,1)S(1)} %get-tuple-element.47), channel_id=1, source_target_pairs={{32,0},{64,32},{96,64},{128,96},{160,128},{192,160},{224,192},{256... | collective-permute-start | bytes 196616 | tf_op jit(solution)/shard_map/ppermute | solution.py:30
  19.5 0.6 copy-start.4
  19.8 0.6 copy-start.6
  52.1 8.0 %copy-start.8 = (bf16[1,1024,256]{2,1,0:T(8,128)(2,1)S(1)}, bf16[1,1024,256]{2,1,0:T(8,128)(2,1)}, u32[]{:S(2)}) copy-start(bf16[1,1024,256]{2,1,0:T(8,128)(2,1)} %param.12) | copy-start | bytes 1572868
  52.1 11.3 %copy-start.9 = (bf16[1,256,1024]{2,1,0:T(8,128)(2,1)S(1)}, bf16[1,256,1024]{2,1,0:T(8,128)(2,1)}, u32[]{:S(2)}) copy-start(bf16[1,256,1024]{2,1,0:T(8,128)(2,1)} %param.13) | copy-start | bytes 1572868
  52.1 32.8 %all-to-all-start.1 = ((bf16[16,256,128]{2,1,0:T(8,128)(2,1)}), bf16[16,256,128]{2,1,0:T(8,128)(2,1)S(1)}, u32[]{:S(2)}, u32[]{:S(2)}) async-start(bf16[16,256,128]{2,1,0:T(8,128)(2,1)} %bitcast.16), calls=%async_computation.1 | async-start | bytes 2097152 | tf_op jit(solution)/shard_map/all_to_all | solution.py:435
  60.1 24.8 %collective-permute-start.2 = (bf16[1024,256]{1,0:T(8,128)(2,1)S(1)}, bf16[1024,256]{1,0:T(8,128)(2,1)S(1)}, u32[]{:S(2)}, u32[]{:S(2)}) collective-permute-start(bf16[1024,256]{1,0:T(8,128)(2,1)S(1)} %bitcast.63), channel_id=1, source_target_pairs={{0,16},{16,0},{1,17},{17,1},{2,18},{18,2},{3,19},{19,3},{4,20},{20... | collective-permute-start | bytes 1572872 | tf_op jit(solution)/shard_map/ppermute | solution.py:430
  63.4 21.5 %collective-permute-start.3 = (bf16[256,1024]{1,0:T(8,128)(2,1)S(1)}, bf16[256,1024]{1,0:T(8,128)(2,1)S(1)}, u32[]{:S(2)}, u32[]{:S(2)}) collective-permute-start(bf16[256,1024]{1,0:T(8,128)(2,1)S(1)} %bitcast.65), channel_id=1, source_target_pairs={{0,17},{17,0},{1,16},{16,1},{2,19},{19,2},{3,18},{18,3},{4,21},{21... | collective-permute-start | bytes 1572872 | tf_op jit(solution)/shard_map/ppermute | solution.py:431
  87.3 0.7 copy-start.10
  88.0 34.5 %all-to-all-start.2 = ((bf16[16,256,128]{2,1,0:T(8,128)(2,1)}), bf16[16,256,128]{2,1,0:T(8,128)(2,1)}, u32[]{:S(2)}, u32[]{:S(2)}) async-start(bf16[16,256,128]{2,1,0:T(8,128)(2,1)} %get-tuple-element.27), calls=%async_computation.2 | async-start | bytes 2097152 | tf_op jit(solution)/shard_map/all_to_all | solution.py:438
  95.0 1.0 copy-start.11
  96.8 15.3 %collective-permute-start.4 = (bf16[1024,256]{1,0:T(8,128)(2,1)S(1)}, bf16[1024,256]{1,0:T(8,128)(2,1)S(1)}, u32[]{:S(2)}, u32[]{:S(2)}) collective-permute-start(bf16[1024,256]{1,0:T(8,128)(2,1)S(1)} %get-tuple-element.30), channel_id=1, source_target_pairs={{0,17},{17,0},{1,16},{16,1},{2,19},{19,2},{3,18},{18,3},{4,21},{21... | collective-permute-start | bytes 1572872 | tf_op jit(solution)/shard_map/ppermute | solution.py:441
  101.3 21.1 %collective-permute-start.5 = (bf16[1024,256]{1,0:T(8,128)(2,1)S(1)}, bf16[1024,256]{1,0:T(8,128)(2,1)}, u32[]{:S(2)}, u32[]{:S(2)}) collective-permute-start(bf16[1024,256]{1,0:T(8,128)(2,1)S(1)} %get-tuple-element.31), channel_id=1, source_target_pairs={{0,16},{16,0},{1,17},{17,1},{2,18},{18,2},{3,19},{19,3},{4,20},{20... | collective-permute-start | bytes 1572872 | tf_op jit(solution)/shard_map/ppermute | solution.py:442
  103.3 31.0 %collective-permute-start.6 = (bf16[1024,256]{1,0:T(8,128)(2,1)S(1)}, bf16[1024,256]{1,0:T(8,128)(2,1)S(1)}, u32[]{:S(2)}, u32[]{:S(2)}) collective-permute-start(bf16[1024,256]{1,0:T(8,128)(2,1)S(1)} %get-tuple-element.33), channel_id=1, source_target_pairs={{0,1},{1,0},{2,3},{3,2},{4,5},{5,4},{6,7},{7,6},{8,9},{9,8},{10,11... | collective-permute-start | bytes 1572872 | tf_op jit(solution)/shard_map/ppermute | solution.py:443
  112.1 0.8 copy-start.12
  124.5 23.1 %all-to-all-start.3 = ((bf16[32,16,128]{2,1,0:T(8,128)(2,1)}), bf16[32,16,128]{2,1,0:T(8,128)(2,1)S(1)}, u32[]{:S(2)}, u32[]{:S(2)}) async-start(bf16[32,16,128]{2,1,0:T(8,128)(2,1)} %copy_bitcast_fusion), calls=%async_computation.3 | async-start | bytes 262144 | tf_op jit(solution)/shard_map/all_to_all | solution.py:448
  131.4 0.7 copy-start.17
  132.1 0.7 copy-start.16
  134.2 14.4 %copy-start.14 = (bf16[1024,256]{1,0:T(8,128)(2,1)}, bf16[1024,256]{1,0:T(8,128)(2,1)S(1)}, u32[]{:S(2)}) copy-start(bf16[1024,256]{1,0:T(8,128)(2,1)S(1)} %collective-permute-done.6) | copy-start | bytes 1572868
  147.6 0.7 copy-start.18
  149.5 6.6 %copy-start = (bf16[1,128,2048]{2,1,0:T(8,128)(2,1)S(1)}, bf16[1,128,2048]{2,1,0:T(8,128)(2,1)}, u32[]{:S(2)}) copy-start(bf16[1,128,2048]{2,1,0:T(8,128)(2,1)} %param.10) | copy-start | bytes 1572868
  149.5 6.6 %copy-start.2 = (f32[31,1024]{1,0:T(8,128)S(1)}, f32[31,1024]{1,0:T(8,128)}, u32[]{:S(2)}) copy-start(f32[31,1024]{1,0:T(8,128)} %taps.5) | copy-start | bytes 380932
  149.5 6.6 %copy-start.3 = (bf16[1,128,1024]{2,1,0:T(8,128)(2,1)S(1)}, bf16[1,128,1024]{2,1,0:T(8,128)(2,1)}, u32[]{:S(2)}) copy-start(bf16[1,128,1024]{2,1,0:T(8,128)(2,1)} %param.9) | copy-start | bytes 786436
  149.5 6.6 %copy-start.5 = (bf16[16,2048]{1,0:T(8,128)(2,1)S(1)}, bf16[16,2048]{1,0:T(8,128)(2,1)}, u32[]{:S(2)}) copy-start(bf16[16,2048]{1,0:T(8,128)(2,1)} %copy-done.4) | copy-start | bytes 196612
  149.5 6.6 %copy-start.7 = (bf16[16,2048]{1,0:T(8,128)(2,1)S(1)}, bf16[16,2048]{1,0:T(8,128)(2,1)}, u32[]{:S(2)}) copy-start(bf16[16,2048]{1,0:T(8,128)(2,1)} %copy-done.6) | copy-start | bytes 196612
  149.5 19.7 %all-to-all-start.4 = ((bf16[16,128,128]{2,1,0:T(8,128)(2,1)}), bf16[16,128,128]{2,1,0:T(8,128)(2,1)S(1)}, u32[]{:S(2)}, u32[]{:S(2)}) async-start(bf16[16,128,128]{2,1,0:T(8,128)(2,1)} %broadcast_in_dim.37), calls=%async_computation.4 | async-start | bytes 1048576 | tf_op jit(solution)/shard_map/all_to_all | solution.py:456
  156.1 2.1 %copy-start.13 = (bf16[1024,256]{1,0:T(8,128)(2,1)S(1)}, bf16[1024,256]{1,0:T(8,128)(2,1)}, u32[]{:S(2)}) copy-start(bf16[1024,256]{1,0:T(8,128)(2,1)} %copy-done.12) | copy-start | bytes 1572868
  156.1 2.1 %copy-start.15 = (bf16[1024,256]{1,0:T(8,128)(2,1)S(1)}, bf16[1024,256]{1,0:T(8,128)(2,1)}, u32[]{:S(2)}) copy-start(bf16[1024,256]{1,0:T(8,128)(2,1)} %copy-done.14) | copy-start | bytes 1572868
  160.2 9.0 %copy-start.1 = (bf16[1,128,1024]{2,1,0:T(8,128)(2,1)S(1)}, bf16[1,128,1024]{2,1,0:T(8,128)(2,1)}, u32[]{:S(2)}) copy-start(bf16[1,128,1024]{2,1,0:T(8,128)(2,1)} %param.17) | copy-start | bytes 786436
  169.3 8.6 %collective-permute-start.7 = (bf16[16,1024]{1,0:T(8,128)(2,1)S(1)}, bf16[16,1024]{1,0:T(8,128)(2,1)S(1)}, u32[]{:S(2)}, u32[]{:S(2)}) collective-permute-start(bf16[16,1024]{1,0:T(8,128)(2,1)S(1)} %get-tuple-element.50), channel_id=1, source_target_pairs={{0,32},{32,64},{64,96},{96,128},{128,160},{160,192},{192,224},{224... | collective-permute-start | bytes 98312 | tf_op jit(solution)/shard_map/ppermute | solution.py:30
  174.1 5.2 %collective-permute-start.8 = (bf16[16,1024]{1,0:T(8,128)(2,1)S(1)}, bf16[16,1024]{1,0:T(8,128)(2,1)S(1)}, u32[]{:S(2)}, u32[]{:S(2)}) collective-permute-start(bf16[16,1024]{1,0:T(8,128)(2,1)S(1)} %get-tuple-element.49), channel_id=1, source_target_pairs={{32,0},{64,32},{96,64},{128,96},{160,128},{192,160},{224,192},{256... | collective-permute-start | bytes 98312 | tf_op jit(solution)/shard_map/ppermute | solution.py:30

commit v4 on v3

--- a/solution.py
+++ b/solution.py
@@ -28,6 +28,13 @@
     up = [(i, i + 1) for i in range(size - 1)]
     down = [(j, i) for i, j in up]
     return lax.ppermute(bottom, "tm", up), lax.ppermute(top, "tm", down)
+
+
+def edge_rims(top, bottom, half):
+    size = lax.axis_size("tm")
+    up = [(2 * i + 1, 2 * (i + 1) + half) for i in range(size - 1)]
+    down = [(2 * (i + 1) + 1, 2 * i + half) for i in range(size - 1)]
+    return lax.ppermute(bottom, ("tm", "xl"), up), lax.ppermute(top, ("tm", "xl"), down)
 
 
 def taps_sum(padded, taps, frames, start, step):
@@ -126,34 +133,49 @@
     slope_ref[...] = sig * (1.0 + conv * (1.0 - sig))
 
 
-def edges_kernel(part_ref, out_grad, slope, edges_ref):
-    for at in range(part_ref.shape[0]):
-        cols = slice(at * part_ref.shape[2], (at + 1) * part_ref.shape[2])
-        hid_grad = out_grad[:, cols].astype(F32) + part_ref[at].astype(F32)
-        edges_ref[:, cols] = (hid_grad * slope[:, cols]).astype(BF16)
-
-
-def outputs_kernel(summed, hidden, out_grad, slope, block_ref, resid_ref, conv_grad_ref):
-    blocks = summed.shape[0] // 2
-    for at in range(blocks):
-        cols = slice(at * summed.shape[2], (at + 1) * summed.shape[2])
-        moe = summed[at].astype(F32)
-        block_ref[:, cols] = (hidden[:, cols].astype(F32) + moe).astype(BF16)
-        hid_grad = out_grad[:, cols].astype(F32) + summed[blocks + at].astype(F32)
-        resid_ref[:, cols] = hid_grad.astype(BF16)
-        conv_grad_ref[:, cols] = hid_grad * slope[:, cols]
-
-
-def backward_kernel(conv_grad, before, after, taps, glu_in, out, padded):
-    frames, width = conv_grad.shape
+def edges_kernel(part_ref, out_grad, slope, copy_ref, top_ref, bottom_ref):
+    copy_ref[...] = part_ref[...]
+    frames = out_grad.shape[0]
+    for edge, rows in ((top_ref, slice(RIM)), (bottom_ref, slice(frames - RIM, frames))):
+        for at in range(part_ref.shape[0]):
+            cols = slice(at * part_ref.shape[2], (at + 1) * part_ref.shape[2])
+            hid_grad = out_grad[rows, cols].astype(F32) + part_ref[at, rows].astype(F32)
+            edge[:, cols] = (hid_grad * slope[rows, cols]).astype(BF16)
+
+
+def backward_kernel(
+    where_ref,
+    mine,
+    other,
+    hidden,
+    out_grad,
+    slope,
+    before_a,
+    after_a,
+    before_b,
+    after_b,
+    taps,
+    glu_in,
+    block_ref,
+    resid_ref,
+    out,
+    padded,
+):
+    frames, width = out_grad.shape
     cols = padded.shape[1]
+    first = where_ref[0] == 0
 
     def step(index, carry):
         at = pl.ds(pl.multiple_of(index * cols, cols), cols)
         at_gate = pl.ds(pl.multiple_of(width + index * cols, cols), cols)
-        padded[:RIM] = before[:, at].astype(F32)
-        padded[RIM : RIM + frames] = conv_grad[:, at]
-        padded[RIM + frames :] = after[:, at].astype(F32)
+        here, there = mine[index].astype(F32), other[index].astype(F32)
+        moe = jnp.where(first, here, there)
+        block_ref[:, at] = (hidden[:, at].astype(F32) + moe).astype(BF16)
+        hid_grad = out_grad[:, at].astype(F32) + jnp.where(first, there, here)
+        resid_ref[:, at] = hid_grad.astype(BF16)
+        padded[:RIM] = before_a[:, at].astype(F32) + before_b[:, at].astype(F32)
+        padded[RIM : RIM + frames] = hid_grad * slope[:, at]
+        padded[RIM + frames :] = after_a[:, at].astype(F32) + after_b[:, at].astype(F32)
         back = taps_sum(padded, taps[:, at], frames, RIM + HALF, -1)
         sig = jax.nn.sigmoid(glu_in[:, at_gate].astype(F32))
         grad = back * sig
@@ -347,46 +369,31 @@
     )(glu_in, glu_in, before, before, after, after, taps, resid)
 
 
-def edge_rows(summed, out_grad, slope):
-    blocks, frames, cols = summed.shape
-    blocks //= 2
-    width = blocks * cols
-    last = frames // RIM - 1
-    row = pl.BlockSpec((RIM, width), lambda i: (i * last, 0))
+def edge_rows(part, out_grad, slope):
+    rim = jax.ShapeDtypeStruct((RIM, out_grad.shape[1]), BF16)
     return pl.pallas_call(
         edges_kernel,
-        grid=(2,),
-        out_shape=jax.ShapeDtypeStruct((2 * RIM, width), BF16),
-        in_specs=[pl.BlockSpec((blocks, RIM, cols), lambda i: (1, i * last, 0)), row, row],
-        out_specs=pl.BlockSpec((RIM, width), lambda i: (i, 0)),
+        out_shape=(jax.ShapeDtypeStruct(part.shape, BF16), rim, rim),
+        in_specs=vmem(3),
+        out_specs=tuple(vmem(3)),
         compiler_params=pltpu.CompilerParams(vmem_limit_bytes=16 * 2**20),
         cost_estimate=pl.CostEstimate(flops=10**5, bytes_accessed=2**18, transcendentals=0),
-    )(summed, out_grad, slope)
-
-
-def finish(summed, hidden_in, out_grad, slope):
-    half = jax.ShapeDtypeStruct(hidden_in.shape, BF16)
-    return pl.pallas_call(
-        outputs_kernel,
-        out_shape=(half, half, jax.ShapeDtypeStruct(hidden_in.shape, F32)),
-        in_specs=vmem(4),
-        out_specs=tuple(vmem(3)),
-        compiler_params=pltpu.CompilerParams(vmem_limit_bytes=16 * 2**20),
-        cost_estimate=pl.CostEstimate(flops=10**6, bytes_accessed=2**21, transcendentals=0),
-    )(summed, hidden_in, out_grad, slope)
-
-
-def backward_full(conv_grad, before, after, taps, glu_in, cols):
-    frames = conv_grad.shape[0]
+    )(part, out_grad, slope)
+
+
+def backward_full(where, mine, other, hidden_in, out_grad, slope, halos, taps, glu_in):
+    cols = mine.shape[2]
+    frames = out_grad.shape[0]
+    half = jax.ShapeDtypeStruct(out_grad.shape, BF16)
     return pl.pallas_call(
         backward_kernel,
-        out_shape=jax.ShapeDtypeStruct(glu_in.shape, BF16),
-        in_specs=vmem(5),
-        out_specs=pl.BlockSpec(memory_space=pltpu.VMEM),
+        out_shape=(half, half, jax.ShapeDtypeStruct(glu_in.shape, BF16)),
+        in_specs=[pl.BlockSpec(memory_space=pltpu.SMEM)] + vmem(7 + len(halos)),
+        out_specs=tuple(vmem(3)),
         scratch_shapes=[pltpu.VMEM((frames + 2 * RIM, cols), F32)],
         compiler_params=pltpu.CompilerParams(vmem_limit_bytes=16 * 2**20),
         cost_estimate=pl.CostEstimate(flops=2 * 10**7, bytes_accessed=2**21, transcendentals=0),
-    )(conv_grad, before, after, taps, glu_in)
+    )(where, mine, other, hidden_in, out_grad, slope, *halos, taps, glu_in)
 
 
 def shards(resid, glu_input, dw_kernel, w_in, w_out, expert_ids, mix_weights, frame_kept, out_grad):
@@ -441,26 +448,28 @@
     got_both = lax.ppermute(send[2], ("xl", "dp"), swap_both)
     got_xl = lax.ppermute(send[1], "xl", swap)
     got_dp = lax.ppermute(send[0], "dp", swap)
-    parts, got_both, got_xl = lax.optimization_barrier((parts, got_both, got_xl))
+    parts, got_both = lax.optimization_barrier((parts, got_both))
 
     parts = parts.reshape(2, ranks, experts, half_cap, cols).astype(F32).sum(axis=1)
     parts = parts.astype(BF16).transpose(1, 0, 2, 3).reshape(experts, capacity, cols)
     parts = lax.all_to_all(parts, "tm", 0, 0, tiled=True).reshape(experts * capacity, cols)
-    parts, got_dp = lax.optimization_barrier((parts, got_dp))
+    parts, got_dp, got_xl = lax.optimization_barrier((parts, got_dp, got_xl))
     got = (got_dp, got_xl, got_both)
     scale = (mix * frame_kept.astype(F32)).reshape(-1)
     pick = (dest.reshape(-1)[:, None] == jnp.arange(experts * capacity)[None, :]).astype(BF16)
     pick_scale = jnp.where(xl == 0, scale, 1.0)
     picked = jnp.dot(pick, parts, preferred_element_type=F32) * pick_scale[:, None]
     summed = (picked[:frames] + picked[frames:]).astype(BF16)
-    summed = lax.all_to_all(
-        jnp.broadcast_to(summed[None], (2 * ranks,) + summed.shape), ("xl", "y"), 0, 0, tiled=True
-    )
-
-    edges = edge_rows(summed, out_grad[0], slope)
-    before, after = rims(edges[:RIM], edges[RIM:])
-    block_out, resid_grad, conv_grad = finish(summed, hidden_in, out_grad[0], slope)
-    glu_grad = backward_full(conv_grad, before, after, dw_kernel, glu_in, cols)
+    mine = lax.all_to_all(
+        jnp.broadcast_to(summed[None], (ranks,) + summed.shape), "y", 0, 0, tiled=True
+    )
+
+    mine, top, bottom = edge_rows(mine, out_grad[0], slope)
+    halos = [rim for half in (0, 1) for rim in edge_rims(top, bottom, half)]
+    other = lax.ppermute(mine, "xl", swap)
+    block_out, resid_grad, glu_grad = backward_full(
+        xl.reshape(1), mine, other, hidden_in, out_grad[0], slope, halos, dw_kernel, glu_in
+    )
 
     hidden = weight_in.shape[1]
     w_in_grad = own_in + sum(piece[: width // 2].astype(F32) for piece in got)

time: 182 us -> 188 us (1.033)
  starting transfers between devices: 68.6 us -> 75.5 us
    ppermute x0 -> x5, starting transfers between devices: none -> 13.1 us  [the longest x1 9.24 us: shards(): other = lax.ppermute(mine, 'xl', swap)]
    ppermute x1, waiting for transfers between devices: 5.67 us -> 14.5 us  [shards(): got_both = lax.ppermute(send[2], ('xl', 'dp'), swap_both)]
    ppermute x1, waiting for transfers between devices: 9.54 us -> 1.39 us  [shards(): got_xl = lax.ppermute(send[1], 'xl', swap)]
    ppermute x4 -> x2, starting transfers between devices: 24.1 us -> 17.4 us  [rims(): return (lax.ppermute(bottom, 'tm', up), lax.ppermute(top, 'tm', down))]
    ppermute x0 -> x5, waiting for transfers between devices: none -> 5.09 us  [the longest x1 5.08 us: shards(): other = lax.ppermute(mine, 'xl', swap)]
    all_to_all x1, waiting for transfers between devices: 8.88 us -> 5.55 us  [shards(): lax.all_to_all(jnp.broadcast_to(summed[None], (ranks,) + summed.shape), '...]
    unnamed x38 -> x42, local copies, waits for them, and re-layouts: 5.1 us -> 5.01 us
  transfers between devices with their start and end apart: 13 -> 16, of which waited for: 8 -> 7; matrix products, arithmetic and copies ran while one was open for 3% -> 3% of each run, Pallas kernels for 2% -> 2%
where the time goes in v4:
time: 188 us; the launch traced here: 187 us
  starting transfers between devices  75.5 us (40%)
  waiting for transfers between devices  58.5 us (31%)
  blocking collectives  27.9 us (15%)
  Pallas kernels  10.4 us (6%)
  local copies, waits for them, and re-layouts  8.59 us (5%)
  other arithmetic  4.86 us (3%)
    all_to_all x1, blocking collectives, shards(): lax.all_to_all(rows.reshape(experts, capacity, cols), 'tm', 0, 0, tiled=T...  27.9 us
    ppermute x1, waiting for transfers between devices, shards(): win_other = lax.ppermute(weight_in, 'xl', swap)  18.2 us
    ppermute x2, starting transfers between devices, rims(): return (lax.ppermute(bottom, 'tm', up), lax.ppermute(top, 'tm', down))  17.4 us
    ppermute x1, waiting for transfers between devices, shards(): got_both = lax.ppermute(send[2], ('xl', 'dp'), swap_both)  14.5 us
    all_to_all x1, waiting for transfers between devices, shards(): lax.all_to_all(parts, 'tm', 0, 0, tiled=True)  13.4 us
    ppermute x1, starting transfers between devices, shards(): other = lax.ppermute(mine, 'xl', swap)  9.24 us
    all_to_all x1, starting transfers between devices, shards(): rows = lax.all_to_all(rows, ('xl', 'y'), 0, 0, tiled=True)  7.99 us
    all_to_all x1, starting transfers between devices, shards(): lax.all_to_all(parts, 'tm', 0, 0, tiled=True)  7.9 us
  transfers between devices with their start and end apart: 16, of which 7 were waited for; matrix products, arithmetic and copies ran while one was open for 3% of the time, Pallas kernels for 2%

profile of v4, /device:TPU:1, one launch (start us, length us, event | category | flops | bytes accessed | tf_op | source)
XLA Modules:
  0.0 187.0 jit_solution(13284960480496347095)
XLA Ops:
  0.6 0.9 slice_bitcast_fusion
  1.5 5.4 %collective-permute-start = (bf16[16,2048]{1,0:T(8,128)(2,1)S(1)}, bf16[16,2048]{1,0:T(8,128)(2,1)S(1)}, u32[]{:S(2)}, u32[]{:S(2)}) collective-permute-start(bf16[16,2048]{1,0:T(8,128)(2,1)S(1)} %get-tuple-element.54), channel_id=1, source_target_pairs={{0,32},{32,64},{64,96},{96,128},{128,160},{160,192},{192,224},{224... | collective-permute-start | bytes 196616 | tf_op jit(solution)/shard_map/ppermute | solution.py:30
  6.9 12.0 %collective-permute-start.1 = (bf16[16,2048]{1,0:T(8,128)(2,1)S(1)}, bf16[16,2048]{1,0:T(8,128)(2,1)S(1)}, u32[]{:S(2)}, u32[]{:S(2)}) collective-permute-start(bf16[16,2048]{1,0:T(8,128)(2,1)S(1)} %get-tuple-element.53), channel_id=1, source_target_pairs={{32,0},{64,32},{96,64},{128,96},{160,128},{192,160},{224,192},{256... | collective-permute-start | bytes 196616 | tf_op jit(solution)/shard_map/ppermute | solution.py:30
  20.4 2.6 %shard_map.128 = (bf16[512,128]{1,0:T(8,128)(2,1)}, s32[2,128]{1,0:T(2,128)}) custom-call(s32[2]{0:T(128)} %pad_add_fusion.where_ref, bf16[128,2048]{1,0:T(8,128)(2,1)} %bitcast.53, bf16[128,2048]{1,0:T(8,128)(2,1)} %bitcast.54, bf16[16,2048]{1,0:T(8,128)(2,1)} %copy-done.4, bf16[16,2048]{1,0:T(8,128)(2,1)} %copy-done.4, bf16[16,2048]{1,0:T(8,128)(2,1)} %copy-done.6, ...), custom_call_target="tpu_custom_call" | custom-call | flops 20000000 | bytes 1048576 | tf_op jit(solution)/shard_map/pallas_call | solution.py:329
  23.0 27.9 %all_to_all.25 = bf16[32,16,128]{2,1,0:T(8,128)(2,1)S(1)} all-to-all(bf16[32,16,128]{2,1,0:T(8,128)(2,1)} %bitcast.70), channel_id=1, replica_groups=mesh['tm'=32,'xl'=2,'y'=8,'dp'=2] {'tm'}, dimensions={0} | all-to-all | bytes 262144 | tf_op jit(solution)/shard_map/all_to_all | solution.py:435
  50.9 1.2 broadcast_in_dim.35
  52.2 8.0 %all-to-all-start.1 = ((bf16[16,256,128]{2,1,0:T(8,128)(2,1)}), bf16[16,256,128]{2,1,0:T(8,128)(2,1)S(1)}, u32[]{:S(2)}, u32[]{:S(2)}) async-start(bf16[16,256,128]{2,1,0:T(8,128)(2,1)} %bitcast.16), calls=%async_computation.1 | async-start | bytes 2097152 | tf_op jit(solution)/shard_map/all_to_all | solution.py:442
  60.2 3.3 %collective-permute-start.2 = (bf16[1024,256]{1,0:T(8,128)(2,1)S(1)}, bf16[1024,256]{1,0:T(8,128)(2,1)S(1)}, u32[]{:S(2)}, u32[]{:S(2)}) collective-permute-start(bf16[1024,256]{1,0:T(8,128)(2,1)S(1)} %bitcast.63), channel_id=1, source_target_pairs={{0,16},{16,0},{1,17},{17,1},{2,18},{18,2},{3,19},{19,3},{4,20},{20... | collective-permute-start | bytes 1572872 | tf_op jit(solution)/shard_map/ppermute | solution.py:437
  63.5 3.3 %collective-permute-start.3 = (bf16[256,1024]{1,0:T(8,128)(2,1)S(1)}, bf16[256,1024]{1,0:T(8,128)(2,1)S(1)}, u32[]{:S(2)}, u32[]{:S(2)}) collective-permute-start(bf16[256,1024]{1,0:T(8,128)(2,1)S(1)} %bitcast.65), channel_id=1, source_target_pairs={{0,17},{17,0},{1,16},{16,1},{2,19},{19,2},{3,18},{18,3},{4,21},{21... | collective-permute-start | bytes 1572872 | tf_op jit(solution)/shard_map/ppermute | solution.py:438
  66.7 18.2 %collective-permute-done.2.win_b = bf16[1024,256]{1,0:T(8,128)(2,1)S(1)} collective-permute-done((bf16[1024,256]{1,0:T(8,128)(2,1)S(1)}, bf16[1024,256]{1,0:T(8,128)(2,1)S(1)}, u32[]{:S(2)}, u32[]{:S(2)}) %collective-permute-start.2) | collective-permute-done | bytes 524320 | tf_op jit(solution)/shard_map/ppermute | solution.py:437
  85.0 2.4 %shard_map.129 = (bf16[2,256,256]{2,1,0:T(8,128)(2,1)S(1)}, bf16[2,256,256]{2,1,0:T(8,128)(2,1)S(1)}, bf16[16,256,128]{2,1,0:T(8,128)(2,1)}) custom-call(bf16[16,256,128]{2,1,0:T(8,128)(2,1)S(1)} %all-to-all-done.1.rows_ref, bf16[1024,256]{1,0:T(8,128)(2,1)S(1)} %bitcast.64, bf16[1024,256]{1,0:T(8,128)(2,1)S(1)} %collective-permute-done.2.win_b, ...), custom_call_target="tpu_custom_call" | custom-call | flops 1073741824 | bytes 5242880 | tf_op jit(solution)/shard_map/pallas_call | solution.py:266
  88.8 7.1 %all-to-all-start.2 = ((bf16[16,256,128]{2,1,0:T(8,128)(2,1)}), bf16[16,256,128]{2,1,0:T(8,128)(2,1)}, u32[]{:S(2)}, u32[]{:S(2)}) async-start(bf16[16,256,128]{2,1,0:T(8,128)(2,1)} %get-tuple-element.30), calls=%async_computation.2 | async-start | bytes 2097152 | tf_op jit(solution)/shard_map/all_to_all | solution.py:445
  95.9 0.9 copy-done.13
  96.8 0.9 shard_map.130
  97.7 4.5 %collective-permute-start.4 = (bf16[1024,256]{1,0:T(8,128)(2,1)S(1)}, bf16[1024,256]{1,0:T(8,128)(2,1)}, u32[]{:S(2)}, u32[]{:S(2)}) collective-permute-start(bf16[1024,256]{1,0:T(8,128)(2,1)S(1)} %get-tuple-element.33), channel_id=1, source_target_pairs={{0,17},{17,0},{1,16},{16,1},{2,19},{19,2},{3,18},{18,3},{4,21},{21... | collective-permute-start | bytes 1572872 | tf_op jit(solution)/shard_map/ppermute | solution.py:448
  102.2 2.4 %collective-permute-start.5 = (bf16[1024,256]{1,0:T(8,128)(2,1)S(1)}, bf16[1024,256]{1,0:T(8,128)(2,1)S(1)}, u32[]{:S(2)}, u32[]{:S(2)}) collective-permute-start(bf16[1024,256]{1,0:T(8,128)(2,1)S(1)} %get-tuple-element.35), channel_id=1, source_target_pairs={{0,1},{1,0},{2,3},{3,2},{4,5},{5,4},{6,7},{7,6},{8,9},{9,8},{10,11... | collective-permute-start | bytes 1572872 | tf_op jit(solution)/shard_map/ppermute | solution.py:450
  104.7 2.1 %collective-permute-start.6 = (bf16[1024,256]{1,0:T(8,128)(2,1)S(1)}, bf16[1024,256]{1,0:T(8,128)(2,1)S(1)}, u32[]{:S(2)}, u32[]{:S(2)}) collective-permute-start(bf16[1024,256]{1,0:T(8,128)(2,1)S(1)} %get-tuple-element.36), channel_id=1, source_target_pairs={{0,16},{16,0},{1,17},{17,1},{2,18},{18,2},{3,19},{19,3},{4,20},{20... | collective-permute-start | bytes 1572872 | tf_op jit(solution)/shard_map/ppermute | solution.py:449
  106.7 14.5 %collective-permute-done.4 = bf16[1024,256]{1,0:T(8,128)(2,1)} collective-permute-done((bf16[1024,256]{1,0:T(8,128)(2,1)S(1)}, bf16[1024,256]{1,0:T(8,128)(2,1)}, u32[]{:S(2)}, u32[]{:S(2)}) %collective-permute-start.4) | collective-permute-done | bytes 524320 | tf_op jit(solution)/shard_map/ppermute | solution.py:448
  121.2 1.4 reduce_sum.12
  123.3 7.9 %all-to-all-start.3 = ((bf16[32,16,128]{2,1,0:T(8,128)(2,1)}), bf16[32,16,128]{2,1,0:T(8,128)(2,1)S(1)}, u32[]{:S(2)}, u32[]{:S(2)}) async-start(bf16[32,16,128]{2,1,0:T(8,128)(2,1)} %copy_bitcast_fusion), calls=%async_computation.3 | async-start | bytes 262144 | tf_op jit(solution)/shard_map/all_to_all | solution.py:455
  132.5 1.4 collective-permute-done.6
  133.9 13.4 %all-to-all-done.3 = bf16[32,16,128]{2,1,0:T(8,128)(2,1)S(1)} async-done(((bf16[32,16,128]{2,1,0:T(8,128)(2,1)}), bf16[32,16,128]{2,1,0:T(8,128)(2,1)S(1)}, u32[]{:S(2)}, u32[]{:S(2)}) %all-to-all-start.3) | async-done | bytes 131104 | tf_op jit(solution)/shard_map/all_to_all | solution.py:455
  149.1 6.5 %all-to-all-start.4 = ((bf16[8,128,128]{2,1,0:T(8,128)(2,1)}), bf16[8,128,128]{2,1,0:T(8,128)(2,1)S(1)}, u32[]{:S(2)}, u32[]{:S(2)}) async-start(bf16[8,128,128]{2,1,0:T(8,128)(2,1)} %broadcast_in_dim.37), calls=%async_computation.4 | async-start | bytes 524288 | tf_op jit(solution)/shard_map/all_to_all | solution.py:463
  155.7 2.1 %shard_map.131 = (bf16[128,1024]{1,0:T(8,128)(2,1)S(1)}, f32[128,1024]{1,0:T(8,128)S(1)}) custom-call(bf16[128,2048]{1,0:T(8,128)(2,1)S(1)} %bitcast.55, bf16[128,2048]{1,0:T(8,128)(2,1)S(1)} %bitcast.56, bf16[16,2048]{1,0:T(8,128)(2,1)S(1)} %copy-done.5, bf16[16,2048]{1,0:T(8,128)(2,1)S(1)} %copy-done.5, bf16[16,2048]{1,0:T(8,128)(2,1)S(1)} %copy-done.7, ...), custom_call_target="tpu_custom_call" | custom-call | flops 20000000 | bytes 2097152 | tf_op jit(solution)/shard_map/pallas_call | solution.py:356
  157.8 2.0 %convert_add_fusion = (f32[512,256]{1,0:T(8,128)S(1)}, f32[1,512,256]{2,1,0:T(8,128)}) fusion(bf16[1024,256]{1,0:T(8,128)(2,1)} %collective-permute-done.4, bf16[1024,256]{1,0:T(8,128)(2,1)S(1)} %copy-done.17, bf16[1024,256]{1,0:T(8,128)(2,1)S(1)} %copy-done.15, f32[512,256]{1,0:T(8,128)S(1)} %get-tuple-element.46), kind=kLoop, calls=%fused_computation.1 | loop fusion | flops 1441792 | bytes 3145728 | tf_op jit(solution)/shard_map/add | solution.py:480
  159.8 5.5 %all-to-all-done.4.part_ref = bf16[8,128,128]{2,1,0:T(8,128)(2,1)S(1)} async-done(((bf16[8,128,128]{2,1,0:T(8,128)(2,1)}), bf16[8,128,128]{2,1,0:T(8,128)(2,1)S(1)}, u32[]{:S(2)}, u32[]{:S(2)}) %all-to-all-start.4) | async-done | bytes 262176 | tf_op jit(solution)/shard_map/all_to_all | solution.py:463
  165.4 1.3 collective-permute-start.8
  167.4 1.3 collective-permute-start.9
  169.4 9.2 %collective-permute-start.7 = (bf16[8,128,128]{2,1,0:T(8,128)(2,1)S(1)}, bf16[8,128,128]{2,1,0:T(8,128)(2,1)S(1)}, u32[]{:S(2)}, u32[]{:S(2)}) collective-permute-start(bf16[8,128,128]{2,1,0:T(8,128)(2,1)S(1)} %get-tuple-element.39.mine), channel_id=1, source_target_pairs={{0,16},{16,0},{1,17},{17,1},{2,18},{18,2},{3,19},{19,3},{4,20},{20... | collective-permute-start | bytes 786440 | tf_op jit(solution)/shard_map/ppermute | solution.py:469
  178.6 0.9 add_bitcast_fusion
  179.5 5.1 %collective-permute-done.7.other = bf16[8,128,128]{2,1,0:T(8,128)(2,1)S(1)} collective-permute-done((bf16[8,128,128]{2,1,0:T(8,128)(2,1)S(1)}, bf16[8,128,128]{2,1,0:T(8,128)(2,1)S(1)}, u32[]{:S(2)}, u32[]{:S(2)}) %collective-permute-start.7) | collective-permute-done | bytes 262176 | tf_op jit(solution)/shard_map/ppermute | solution.py:469
  184.6 2.4 %shard_map.133 = (bf16[128,1024]{1,0:T(8,128)(2,1)}, bf16[128,1024]{1,0:T(8,128)(2,1)}, bf16[128,2048]{1,0:T(8,128)(2,1)}) custom-call(s32[1]{0:T(128)} %bitcast.where_ref, bf16[8,128,128]{2,1,0:T(8,128)(2,1)S(1)} %get-tuple-element.39.mine, bf16[8,128,128]{2,1,0:T(8,128)(2,1)S(1)} %collective-permute-done.7.other, ...), custom_call_target="tpu_custom_call" | custom-call | flops 20000000 | bytes 2097152 | tf_op jit(solution)/shard_map/pallas_call | solution.py:388
  (63 shorter events, 8.1 us)
Async XLA Ops:
  1.5 18.0 %collective-permute-start = (bf16[16,2048]{1,0:T(8,128)(2,1)S(1)}, bf16[16,2048]{1,0:T(8,128)(2,1)S(1)}, u32[]{:S(2)}, u32[]{:S(2)}) collective-permute-start(bf16[16,2048]{1,0:T(8,128)(2,1)S(1)} %get-tuple-element.54), channel_id=1, source_target_pairs={{0,32},{32,64},{64,96},{96,128},{128,160},{160,192},{192,224},{224... | collective-permute-start | bytes 196616 | tf_op jit(solution)/shard_map/ppermute | solution.py:30
  6.9 12.9 %collective-permute-start.1 = (bf16[16,2048]{1,0:T(8,128)(2,1)S(1)}, bf16[16,2048]{1,0:T(8,128)(2,1)S(1)}, u32[]{:S(2)}, u32[]{:S(2)}) collective-permute-start(bf16[16,2048]{1,0:T(8,128)(2,1)S(1)} %get-tuple-element.53), channel_id=1, source_target_pairs={{32,0},{64,32},{96,64},{128,96},{160,128},{192,160},{224,192},{256... | collective-permute-start | bytes 196616 | tf_op jit(solution)/shard_map/ppermute | solution.py:30
  52.2 8.0 %copy-start.8 = (bf16[1,1024,256]{2,1,0:T(8,128)(2,1)S(1)}, bf16[1,1024,256]{2,1,0:T(8,128)(2,1)}, u32[]{:S(2)}) copy-start(bf16[1,1024,256]{2,1,0:T(8,128)(2,1)} %param.12) | copy-start | bytes 1572868
  52.2 11.3 %copy-start.9 = (bf16[1,256,1024]{2,1,0:T(8,128)(2,1)S(1)}, bf16[1,256,1024]{2,1,0:T(8,128)(2,1)}, u32[]{:S(2)}) copy-start(bf16[1,256,1024]{2,1,0:T(8,128)(2,1)} %param.13) | copy-start | bytes 1572868
  52.2 32.8 %all-to-all-start.1 = ((bf16[16,256,128]{2,1,0:T(8,128)(2,1)}), bf16[16,256,128]{2,1,0:T(8,128)(2,1)S(1)}, u32[]{:S(2)}, u32[]{:S(2)}) async-start(bf16[16,256,128]{2,1,0:T(8,128)(2,1)} %bitcast.16), calls=%async_computation.1 | async-start | bytes 2097152 | tf_op jit(solution)/shard_map/all_to_all | solution.py:442
  60.2 24.8 %collective-permute-start.2 = (bf16[1024,256]{1,0:T(8,128)(2,1)S(1)}, bf16[1024,256]{1,0:T(8,128)(2,1)S(1)}, u32[]{:S(2)}, u32[]{:S(2)}) collective-permute-start(bf16[1024,256]{1,0:T(8,128)(2,1)S(1)} %bitcast.63), channel_id=1, source_target_pairs={{0,16},{16,0},{1,17},{17,1},{2,18},{18,2},{3,19},{19,3},{4,20},{20... | collective-permute-start | bytes 1572872 | tf_op jit(solution)/shard_map/ppermute | solution.py:437
  63.5 21.5 %collective-permute-start.3 = (bf16[256,1024]{1,0:T(8,128)(2,1)S(1)}, bf16[256,1024]{1,0:T(8,128)(2,1)S(1)}, u32[]{:S(2)}, u32[]{:S(2)}) collective-permute-start(bf16[256,1024]{1,0:T(8,128)(2,1)S(1)} %bitcast.65), channel_id=1, source_target_pairs={{0,17},{17,0},{1,16},{16,1},{2,19},{19,2},{3,18},{18,3},{4,21},{21... | collective-permute-start | bytes 1572872 | tf_op jit(solution)/shard_map/ppermute | solution.py:438
  87.3 0.7 copy-start.10
  88.0 0.7 copy-start.12
  88.8 7.1 %copy-start.11 = (bf16[2,256,256]{2,1,0:T(8,128)(2,1)S(1)}, bf16[2,256,256]{2,1,0:T(8,128)(2,1)}, u32[]{:S(2)}) copy-start(bf16[2,256,256]{2,1,0:T(8,128)(2,1)} %copy-done.10) | copy-start | bytes 786436
  88.8 32.5 %all-to-all-start.2 = ((bf16[16,256,128]{2,1,0:T(8,128)(2,1)}), bf16[16,256,128]{2,1,0:T(8,128)(2,1)}, u32[]{:S(2)}, u32[]{:S(2)}) async-start(bf16[16,256,128]{2,1,0:T(8,128)(2,1)} %get-tuple-element.30), calls=%async_computation.2 | async-start | bytes 2097152 | tf_op jit(solution)/shard_map/all_to_all | solution.py:445
  95.9 1.0 copy-start.13
  97.7 23.5 %collective-permute-start.4 = (bf16[1024,256]{1,0:T(8,128)(2,1)S(1)}, bf16[1024,256]{1,0:T(8,128)(2,1)}, u32[]{:S(2)}, u32[]{:S(2)}) collective-permute-start(bf16[1024,256]{1,0:T(8,128)(2,1)S(1)} %get-tuple-element.33), channel_id=1, source_target_pairs={{0,17},{17,0},{1,16},{16,1},{2,19},{19,2},{3,18},{18,3},{4,21},{21... | collective-permute-start | bytes 1572872 | tf_op jit(solution)/shard_map/ppermute | solution.py:448
  102.2 30.3 %collective-permute-start.5 = (bf16[1024,256]{1,0:T(8,128)(2,1)S(1)}, bf16[1024,256]{1,0:T(8,128)(2,1)S(1)}, u32[]{:S(2)}, u32[]{:S(2)}) collective-permute-start(bf16[1024,256]{1,0:T(8,128)(2,1)S(1)} %get-tuple-element.35), channel_id=1, source_target_pairs={{0,1},{1,0},{2,3},{3,2},{4,5},{5,4},{6,7},{7,6},{8,9},{9,8},{10,11... | collective-permute-start | bytes 1572872 | tf_op jit(solution)/shard_map/ppermute | solution.py:450
  104.7 29.3 %collective-permute-start.6 = (bf16[1024,256]{1,0:T(8,128)(2,1)S(1)}, bf16[1024,256]{1,0:T(8,128)(2,1)S(1)}, u32[]{:S(2)}, u32[]{:S(2)}) collective-permute-start(bf16[1024,256]{1,0:T(8,128)(2,1)S(1)} %get-tuple-element.36), channel_id=1, source_target_pairs={{0,16},{16,0},{1,17},{17,1},{2,18},{18,2},{3,19},{19,3},{4,20},{20... | collective-permute-start | bytes 1572872 | tf_op jit(solution)/shard_map/ppermute | solution.py:449
  123.3 24.1 %all-to-all-start.3 = ((bf16[32,16,128]{2,1,0:T(8,128)(2,1)}), bf16[32,16,128]{2,1,0:T(8,128)(2,1)S(1)}, u32[]{:S(2)}, u32[]{:S(2)}) async-start(bf16[32,16,128]{2,1,0:T(8,128)(2,1)} %copy_bitcast_fusion), calls=%async_computation.3 | async-start | bytes 262144 | tf_op jit(solution)/shard_map/all_to_all | solution.py:455
  132.5 14.8 %copy-start.14 = (bf16[1024,256]{1,0:T(8,128)(2,1)}, bf16[1024,256]{1,0:T(8,128)(2,1)S(1)}, u32[]{:S(2)}) copy-start(bf16[1024,256]{1,0:T(8,128)(2,1)S(1)} %collective-permute-done.5) | copy-start | bytes 1572868
  133.9 14.4 %copy-start.16 = (bf16[1024,256]{1,0:T(8,128)(2,1)}, bf16[1024,256]{1,0:T(8,128)(2,1)S(1)}, u32[]{:S(2)}) copy-start(bf16[1024,256]{1,0:T(8,128)(2,1)S(1)} %collective-permute-done.6) | copy-start | bytes 1572868
  148.0 7.6 %copy-start.7 = (bf16[16,2048]{1,0:T(8,128)(2,1)S(1)}, bf16[16,2048]{1,0:T(8,128)(2,1)}, u32[]{:S(2)}) copy-start(bf16[16,2048]{1,0:T(8,128)(2,1)} %copy-done.6) | copy-start | bytes 196612
  148.3 7.3 %copy-start = (bf16[1,128,2048]{2,1,0:T(8,128)(2,1)S(1)}, bf16[1,128,2048]{2,1,0:T(8,128)(2,1)}, u32[]{:S(2)}) copy-start(bf16[1,128,2048]{2,1,0:T(8,128)(2,1)} %param.10) | copy-start | bytes 1572868
  149.1 6.5 %copy-start.2 = (f32[31,1024]{1,0:T(8,128)S(1)}, f32[31,1024]{1,0:T(8,128)}, u32[]{:S(2)}) copy-start(f32[31,1024]{1,0:T(8,128)} %taps.5) | copy-start | bytes 380932
  149.1 6.5 %copy-start.3 = (bf16[1,128,1024]{2,1,0:T(8,128)(2,1)S(1)}, bf16[1,128,1024]{2,1,0:T(8,128)(2,1)}, u32[]{:S(2)}) copy-start(bf16[1,128,1024]{2,1,0:T(8,128)(2,1)} %param.9) | copy-start | bytes 786436
  149.1 6.5 %copy-start.5 = (bf16[16,2048]{1,0:T(8,128)(2,1)S(1)}, bf16[16,2048]{1,0:T(8,128)(2,1)}, u32[]{:S(2)}) copy-start(bf16[16,2048]{1,0:T(8,128)(2,1)} %copy-done.4) | copy-start | bytes 196612
  149.1 16.3 %all-to-all-start.4 = ((bf16[8,128,128]{2,1,0:T(8,128)(2,1)}), bf16[8,128,128]{2,1,0:T(8,128)(2,1)S(1)}, u32[]{:S(2)}, u32[]{:S(2)}) async-start(bf16[8,128,128]{2,1,0:T(8,128)(2,1)} %broadcast_in_dim.37), calls=%async_computation.4 | async-start | bytes 524288 | tf_op jit(solution)/shard_map/all_to_all | solution.py:463
  155.7 2.1 %copy-start.15 = (bf16[1024,256]{1,0:T(8,128)(2,1)S(1)}, bf16[1024,256]{1,0:T(8,128)(2,1)}, u32[]{:S(2)}) copy-start(bf16[1024,256]{1,0:T(8,128)(2,1)} %copy-done.14) | copy-start | bytes 1572868
  155.7 2.1 %copy-start.17 = (bf16[1024,256]{1,0:T(8,128)(2,1)S(1)}, bf16[1024,256]{1,0:T(8,128)(2,1)}, u32[]{:S(2)}) copy-start(bf16[1024,256]{1,0:T(8,128)(2,1)} %copy-done.16) | copy-start | bytes 1572868
  159.8 5.6 %copy-start.1 = (bf16[1,128,1024]{2,1,0:T(8,128)(2,1)S(1)}, bf16[1,128,1024]{2,1,0:T(8,128)(2,1)}, u32[]{:S(2)}) copy-start(bf16[1,128,1024]{2,1,0:T(8,128)(2,1)} %param.17) | copy-start | bytes 786436
  165.4 14.1 %collective-permute-start.8 = (bf16[16,1024]{1,0:T(8,128)(2,1)S(1)}, bf16[16,1024]{1,0:T(8,128)(2,1)S(1)}, u32[]{:S(2)}, u32[]{:S(2)}) collective-permute-start(bf16[16,1024]{1,0:T(8,128)(2,1)S(1)} %get-tuple-element.41), channel_id=1, source_target_pairs={{16,32},{48,64},{80,96},{112,128},{144,160},{176,192},{208,224},{2... | collective-permute-start | bytes 98312 | tf_op jit(solution)/shard_map/ppermute | solution.py:37
  166.7 12.8 %collective-permute-start.10 = (bf16[16,1024]{1,0:T(8,128)(2,1)S(1)}, bf16[16,1024]{1,0:T(8,128)(2,1)S(1)}, u32[]{:S(2)}, u32[]{:S(2)}) collective-permute-start(bf16[16,1024]{1,0:T(8,128)(2,1)S(1)} %get-tuple-element.41), channel_id=1, source_target_pairs={{16,48},{48,80},{80,112},{112,144},{144,176},{176,208},{208,240},{... | collective-permute-start | bytes 98312 | tf_op jit(solution)/shard_map/ppermute | solution.py:37
  167.4 12.1 %collective-permute-start.9 = (bf16[16,1024]{1,0:T(8,128)(2,1)S(1)}, bf16[16,1024]{1,0:T(8,128)(2,1)S(1)}, u32[]{:S(2)}, u32[]{:S(2)}) collective-permute-start(bf16[16,1024]{1,0:T(8,128)(2,1)S(1)} %get-tuple-element.42), channel_id=1, source_target_pairs={{48,0},{80,32},{112,64},{144,96},{176,128},{208,160},{240,192},{27... | collective-permute-start | bytes 98312 | tf_op jit(solution)/shard_map/ppermute | solution.py:37
  168.7 10.8 %collective-permute-start.11 = (bf16[16,1024]{1,0:T(8,128)(2,1)S(1)}, bf16[16,1024]{1,0:T(8,128)(2,1)S(1)}, u32[]{:S(2)}, u32[]{:S(2)}) collective-permute-start(bf16[16,1024]{1,0:T(8,128)(2,1)S(1)} %get-tuple-element.42), channel_id=1, source_target_pairs={{48,16},{80,48},{112,80},{144,112},{176,144},{208,176},{240,208},{... | collective-permute-start | bytes 98312 | tf_op jit(solution)/shard_map/ppermute | solution.py:37
  169.4 15.2 %collective-permute-start.7 = (bf16[8,128,128]{2,1,0:T(8,128)(2,1)S(1)}, bf16[8,128,128]{2,1,0:T(8,128)(2,1)S(1)}, u32[]{:S(2)}, u32[]{:S(2)}) collective-permute-start(bf16[8,128,128]{2,1,0:T(8,128)(2,1)S(1)} %get-tuple-element.39.mine), channel_id=1, source_target_pairs={{0,16},{16,0},{1,17},{17,1},{2,18},{18,2},{3,19},{19,3},{4,20},{20... | collective-permute-start | bytes 786440 | tf_op jit(solution)/shard_map/ppermute | solution.py:469
  (5 other events, 3.3 us)

commit v5 on v3

--- a/solution.py
+++ b/solution.py
@@ -439,14 +439,15 @@
     pieces = [(0, 0), (0, 1), (1, 0), (1, 1)]
     own_in, own_out, *send = weight_grads(pieces, dp.reshape(1), rows, act, act_grad)
     got_both = lax.ppermute(send[2], ("xl", "dp"), swap_both)
-    got_xl = lax.ppermute(send[1], "xl", swap)
-    got_dp = lax.ppermute(send[0], "dp", swap)
-    parts, got_both, got_xl = lax.optimization_barrier((parts, got_both, got_xl))
+    got_both, send_dp, send_xl = lax.optimization_barrier((got_both, send[0], send[1]))
+    got_dp = lax.ppermute(send_dp, "dp", swap)
+    got_xl = lax.ppermute(send_xl, "xl", swap)
+    parts, got_both = lax.optimization_barrier((parts, got_both))
 
     parts = parts.reshape(2, ranks, experts, half_cap, cols).astype(F32).sum(axis=1)
     parts = parts.astype(BF16).transpose(1, 0, 2, 3).reshape(experts, capacity, cols)
     parts = lax.all_to_all(parts, "tm", 0, 0, tiled=True).reshape(experts * capacity, cols)
-    parts, got_dp = lax.optimization_barrier((parts, got_dp))
+    parts, got_dp, got_xl = lax.optimization_barrier((parts, got_dp, got_xl))
     got = (got_dp, got_xl, got_both)
     scale = (mix * frame_kept.astype(F32)).reshape(-1)
     pick = (dest.reshape(-1)[:, None] == jnp.arange(experts * capacity)[None, :]).astype(BF16)

time: 182 us -> 179 us (0.984)
  waiting for transfers between devices: 58.9 us -> 55.5 us
    all_to_all x1, waiting for transfers between devices: 13.4 us -> 4.94 us  [shards(): lax.all_to_all(parts, 'tm', 0, 0, tiled=True)]
    ppermute x1, waiting for transfers between devices: 5.67 us -> 10.8 us  [shards(): got_both = lax.ppermute(send[2], ('xl', 'dp'), swap_both)]
where the time goes in v5:
time: 179 us; the launch traced here: 178 us
  starting transfers between devices  68.9 us (38%)
  waiting for transfers between devices  55.5 us (31%)
  blocking collectives  27.9 us (16%)
  Pallas kernels  11.1 us (6%)
  local copies, waits for them, and re-layouts  8.04 us (4%)
  other arithmetic  4.86 us (3%)
    all_to_all x1, blocking collectives, shards(): lax.all_to_all(rows.reshape(experts, capacity, cols), 'tm', 0, 0, tiled=T...  27.9 us
    ppermute x4, starting transfers between devices, rims(): return (lax.ppermute(bottom, 'tm', up), lax.ppermute(top, 'tm', down))  24.1 us
    ppermute x1, waiting for transfers between devices, shards(): win_other = lax.ppermute(weight_in, 'xl', swap)  18.2 us
    ppermute x1, waiting for transfers between devices, shards(): got_both = lax.ppermute(send[2], ('xl', 'dp'), swap_both)  10.8 us
    ppermute x1, waiting for transfers between devices, shards(): got_xl = lax.ppermute(send_xl, 'xl', swap)  9.56 us
    all_to_all x1, waiting for transfers between devices, shards(): lax.all_to_all(jnp.broadcast_to(summed[None], (2 * ranks,) + summed.shape...  8.88 us
    all_to_all x1, starting transfers between devices, shards(): rows = lax.all_to_all(rows, ('xl', 'y'), 0, 0, tiled=True)  7.98 us
    all_to_all x1, starting transfers between devices, shards(): parts = lax.all_to_all(parts, ('xl', 'y'), 0, 0, tiled=True)  6.96 us
  transfers between devices with their start and end apart: 13, of which 8 were waited for; matrix products, arithmetic and copies ran while one was open for 3% of the time, Pallas kernels for 2%

profile of v5, /device:TPU:1, one launch (start us, length us, event | category | flops | bytes accessed | tf_op | source)
XLA Modules:
  0.0 177.6 jit_solution(16295123730002087911)
XLA Ops:
  1.5 5.4 %collective-permute-start = (bf16[16,2048]{1,0:T(8,128)(2,1)S(1)}, bf16[16,2048]{1,0:T(8,128)(2,1)S(1)}, u32[]{:S(2)}, u32[]{:S(2)}) collective-permute-start(bf16[16,2048]{1,0:T(8,128)(2,1)S(1)} %get-tuple-element.54), channel_id=1, source_target_pairs={{0,32},{32,64},{64,96},{96,128},{128,160},{160,192},{192,224},{224... | collective-permute-start | bytes 196616 | tf_op jit(solution)/shard_map/ppermute | solution.py:30
  6.9 12.0 %collective-permute-start.1 = (bf16[16,2048]{1,0:T(8,128)(2,1)S(1)}, bf16[16,2048]{1,0:T(8,128)(2,1)S(1)}, u32[]{:S(2)}, u32[]{:S(2)}) collective-permute-start(bf16[16,2048]{1,0:T(8,128)(2,1)S(1)} %get-tuple-element.53), channel_id=1, source_target_pairs={{32,0},{64,32},{96,64},{128,96},{160,128},{192,160},{224,192},{256... | collective-permute-start | bytes 196616 | tf_op jit(solution)/shard_map/ppermute | solution.py:30
  20.4 2.6 %shard_map.128 = (bf16[512,128]{1,0:T(8,128)(2,1)}, s32[2,128]{1,0:T(2,128)}) custom-call(s32[2]{0:T(128)} %pad_add_fusion.where_ref, bf16[128,2048]{1,0:T(8,128)(2,1)} %bitcast.53, bf16[128,2048]{1,0:T(8,128)(2,1)} %bitcast.54, bf16[16,2048]{1,0:T(8,128)(2,1)} %copy-done.4, bf16[16,2048]{1,0:T(8,128)(2,1)} %copy-done.4, bf16[16,2048]{1,0:T(8,128)(2,1)} %copy-done.6, ...), custom_call_target="tpu_custom_call" | custom-call | flops 20000000 | bytes 1048576 | tf_op jit(solution)/shard_map/pallas_call | solution.py:307
  23.0 27.9 %all_to_all.25 = bf16[32,16,128]{2,1,0:T(8,128)(2,1)S(1)} all-to-all(bf16[32,16,128]{2,1,0:T(8,128)(2,1)} %bitcast.71), channel_id=1, replica_groups=mesh['tm'=32,'xl'=2,'y'=8,'dp'=2] {'tm'}, dimensions={0} | all-to-all | bytes 262144 | tf_op jit(solution)/shard_map/all_to_all | solution.py:428
  50.9 1.2 broadcast_in_dim.35
  52.1 8.0 %all-to-all-start.1 = ((bf16[16,256,128]{2,1,0:T(8,128)(2,1)}), bf16[16,256,128]{2,1,0:T(8,128)(2,1)S(1)}, u32[]{:S(2)}, u32[]{:S(2)}) async-start(bf16[16,256,128]{2,1,0:T(8,128)(2,1)} %bitcast.16), calls=%async_computation.1 | async-start | bytes 2097152 | tf_op jit(solution)/shard_map/all_to_all | solution.py:435
  60.1 3.3 %collective-permute-start.2 = (bf16[1024,256]{1,0:T(8,128)(2,1)S(1)}, bf16[1024,256]{1,0:T(8,128)(2,1)S(1)}, u32[]{:S(2)}, u32[]{:S(2)}) collective-permute-start(bf16[1024,256]{1,0:T(8,128)(2,1)S(1)} %bitcast.63), channel_id=1, source_target_pairs={{0,16},{16,0},{1,17},{17,1},{2,18},{18,2},{3,19},{19,3},{4,20},{20... | collective-permute-start | bytes 1572872 | tf_op jit(solution)/shard_map/ppermute | solution.py:430
  63.4 3.3 %collective-permute-start.3 = (bf16[256,1024]{1,0:T(8,128)(2,1)S(1)}, bf16[256,1024]{1,0:T(8,128)(2,1)S(1)}, u32[]{:S(2)}, u32[]{:S(2)}) collective-permute-start(bf16[256,1024]{1,0:T(8,128)(2,1)S(1)} %bitcast.65), channel_id=1, source_target_pairs={{0,17},{17,0},{1,16},{16,1},{2,19},{19,2},{3,18},{18,3},{4,21},{21... | collective-permute-start | bytes 1572872 | tf_op jit(solution)/shard_map/ppermute | solution.py:431
  66.7 18.2 %collective-permute-done.2.win_b = bf16[1024,256]{1,0:T(8,128)(2,1)S(1)} collective-permute-done((bf16[1024,256]{1,0:T(8,128)(2,1)S(1)}, bf16[1024,256]{1,0:T(8,128)(2,1)S(1)}, u32[]{:S(2)}, u32[]{:S(2)}) %collective-permute-start.2) | collective-permute-done | bytes 524320 | tf_op jit(solution)/shard_map/ppermute | solution.py:430
  85.0 2.4 %shard_map.129 = (bf16[2,256,256]{2,1,0:T(8,128)(2,1)S(1)}, bf16[2,256,256]{2,1,0:T(8,128)(2,1)S(1)}, bf16[16,256,128]{2,1,0:T(8,128)(2,1)}) custom-call(bf16[16,256,128]{2,1,0:T(8,128)(2,1)S(1)} %all-to-all-done.1.rows_ref, bf16[1024,256]{1,0:T(8,128)(2,1)S(1)} %bitcast.64, bf16[1024,256]{1,0:T(8,128)(2,1)S(1)} %collective-permute-done.2.win_b, ...), custom_call_target="tpu_custom_call" | custom-call | flops 1073741824 | bytes 5242880 | tf_op jit(solution)/shard_map/pallas_call | solution.py:244
  88.0 7.0 %all-to-all-start.2 = ((bf16[16,256,128]{2,1,0:T(8,128)(2,1)}), bf16[16,256,128]{2,1,0:T(8,128)(2,1)}, u32[]{:S(2)}, u32[]{:S(2)}) async-start(bf16[16,256,128]{2,1,0:T(8,128)(2,1)} %get-tuple-element.30), calls=%async_computation.2 | async-start | bytes 2097152 | tf_op jit(solution)/shard_map/all_to_all | solution.py:438
  95.0 0.9 copy-done.11
  95.9 0.9 shard_map.130
  96.8 4.5 %collective-permute-start.4 = (bf16[1024,256]{1,0:T(8,128)(2,1)S(1)}, bf16[1024,256]{1,0:T(8,128)(2,1)S(1)}, u32[]{:S(2)}, u32[]{:S(2)}) collective-permute-start(bf16[1024,256]{1,0:T(8,128)(2,1)S(1)} %get-tuple-element.33), channel_id=1, source_target_pairs={{0,17},{17,0},{1,16},{16,1},{2,19},{19,2},{3,18},{18,3},{4,21},{21... | collective-permute-start | bytes 1572872 | tf_op jit(solution)/shard_map/ppermute | solution.py:441
  101.3 10.8 %collective-permute-done.4 = bf16[1024,256]{1,0:T(8,128)(2,1)S(1)} collective-permute-done((bf16[1024,256]{1,0:T(8,128)(2,1)S(1)}, bf16[1024,256]{1,0:T(8,128)(2,1)S(1)}, u32[]{:S(2)}, u32[]{:S(2)}) %collective-permute-start.4) | collective-permute-done | bytes 524320 | tf_op jit(solution)/shard_map/ppermute | solution.py:441
  112.1 3.1 %collective-permute-start.5 = (bf16[1024,256]{1,0:T(8,128)(2,1)S(1)}, bf16[1024,256]{1,0:T(8,128)(2,1)S(1)}, u32[]{:S(2)}, u32[]{:S(2)}) collective-permute-start(bf16[1024,256]{1,0:T(8,128)(2,1)S(1)} %get-tuple-element.38), channel_id=1, source_target_pairs={{0,1},{1,0},{2,3},{3,2},{4,5},{5,4},{6,7},{7,6},{8,9},{9,8},{10,11... | collective-permute-start | bytes 1572872 | tf_op jit(solution)/shard_map/ppermute | solution.py:443
  115.3 3.4 %collective-permute-start.6 = (bf16[1024,256]{1,0:T(8,128)(2,1)S(1)}, bf16[1024,256]{1,0:T(8,128)(2,1)}, u32[]{:S(2)}, u32[]{:S(2)}) collective-permute-start(bf16[1024,256]{1,0:T(8,128)(2,1)S(1)} %get-tuple-element.39), channel_id=1, source_target_pairs={{0,16},{16,0},{1,17},{17,1},{2,18},{18,2},{3,19},{19,3},{4,20},{20... | collective-permute-start | bytes 1572872 | tf_op jit(solution)/shard_map/ppermute | solution.py:444
  118.7 1.3 all-to-all-done.2
  120.0 1.4 reduce_sum.12
  122.1 6.4 %all-to-all-start.3 = ((bf16[32,16,128]{2,1,0:T(8,128)(2,1)}), bf16[32,16,128]{2,1,0:T(8,128)(2,1)S(1)}, u32[]{:S(2)}, u32[]{:S(2)}) async-start(bf16[32,16,128]{2,1,0:T(8,128)(2,1)} %copy_bitcast_fusion), calls=%async_computation.3 | async-start | bytes 262144 | tf_op jit(solution)/shard_map/all_to_all | solution.py:449
  129.9 9.6 %collective-permute-done.6 = bf16[1024,256]{1,0:T(8,128)(2,1)} collective-permute-done((bf16[1024,256]{1,0:T(8,128)(2,1)S(1)}, bf16[1024,256]{1,0:T(8,128)(2,1)}, u32[]{:S(2)}, u32[]{:S(2)}) %collective-permute-start.6) | collective-permute-done | bytes 524320 | tf_op jit(solution)/shard_map/ppermute | solution.py:444
  139.4 4.9 %all-to-all-done.3 = bf16[32,16,128]{2,1,0:T(8,128)(2,1)S(1)} async-done(((bf16[32,16,128]{2,1,0:T(8,128)(2,1)}), bf16[32,16,128]{2,1,0:T(8,128)(2,1)S(1)}, u32[]{:S(2)}, u32[]{:S(2)}) %all-to-all-start.3) | async-done | bytes 131104 | tf_op jit(solution)/shard_map/all_to_all | solution.py:449
  145.4 0.9 broadcast_in_dim.37
  146.3 5.9 %all-to-all-start.4 = ((bf16[16,128,128]{2,1,0:T(8,128)(2,1)}), bf16[16,128,128]{2,1,0:T(8,128)(2,1)S(1)}, u32[]{:S(2)}, u32[]{:S(2)}) async-start(bf16[16,128,128]{2,1,0:T(8,128)(2,1)} %broadcast_in_dim.37), calls=%async_computation.4 | async-start | bytes 1048576 | tf_op jit(solution)/shard_map/all_to_all | solution.py:457
  152.2 2.1 %shard_map.131 = (bf16[128,1024]{1,0:T(8,128)(2,1)S(1)}, f32[128,1024]{1,0:T(8,128)S(1)}) custom-call(bf16[128,2048]{1,0:T(8,128)(2,1)S(1)} %bitcast.55, bf16[128,2048]{1,0:T(8,128)(2,1)S(1)} %bitcast.56, bf16[16,2048]{1,0:T(8,128)(2,1)S(1)} %copy-done.5, bf16[16,2048]{1,0:T(8,128)(2,1)S(1)} %copy-done.5, bf16[16,2048]{1,0:T(8,128)(2,1)S(1)} %copy-done.7, ...), custom_call_target="tpu_custom_call" | custom-call | flops 20000000 | bytes 2097152 | tf_op jit(solution)/shard_map/pallas_call | solution.py:334
  154.3 2.0 %convert_add_fusion = (f32[512,256]{1,0:T(8,128)S(1)}, f32[1,512,256]{2,1,0:T(8,128)}) fusion(bf16[1024,256]{1,0:T(8,128)(2,1)S(1)} %copy-done.13, bf16[1024,256]{1,0:T(8,128)(2,1)} %collective-permute-done.6, bf16[1024,256]{1,0:T(8,128)(2,1)S(1)} %copy-done.15, f32[512,256]{1,0:T(8,128)S(1)} %get-tuple-element.46), kind=kLoop, calls=%fused_computation.1 | loop fusion | flops 1441792 | bytes 3145728 | tf_op jit(solution)/shard_map/add | solution.py:472
  156.4 8.9 %all-to-all-done.4.summed.part_ref = bf16[16,128,128]{2,1,0:T(8,128)(2,1)S(1)} async-done(((bf16[16,128,128]{2,1,0:T(8,128)(2,1)}), bf16[16,128,128]{2,1,0:T(8,128)(2,1)S(1)}, u32[]{:S(2)}, u32[]{:S(2)}) %all-to-all-start.4) | async-done | bytes 524320 | tf_op jit(solution)/shard_map/all_to_all | solution.py:457
  165.4 4.8 %collective-permute-start.7 = (bf16[16,1024]{1,0:T(8,128)(2,1)S(1)}, bf16[16,1024]{1,0:T(8,128)(2,1)S(1)}, u32[]{:S(2)}, u32[]{:S(2)}) collective-permute-start(bf16[16,1024]{1,0:T(8,128)(2,1)S(1)} %get-tuple-element.56), channel_id=1, source_target_pairs={{0,32},{32,64},{64,96},{96,128},{128,160},{160,192},{192,224},{224... | collective-permute-start | bytes 98312 | tf_op jit(solution)/shard_map/ppermute | solution.py:30
  170.2 1.9 %collective-permute-start.8 = (bf16[16,1024]{1,0:T(8,128)(2,1)S(1)}, bf16[16,1024]{1,0:T(8,128)(2,1)S(1)}, u32[]{:S(2)}, u32[]{:S(2)}) collective-permute-start(bf16[16,1024]{1,0:T(8,128)(2,1)S(1)} %get-tuple-element.55), channel_id=1, source_target_pairs={{32,0},{64,32},{96,64},{128,96},{160,128},{192,160},{224,192},{256... | collective-permute-start | bytes 98312 | tf_op jit(solution)/shard_map/ppermute | solution.py:30
  173.0 1.0 shard_map.132
  174.0 1.5 collective-permute-done.8.after
  175.4 2.2 %shard_map.134 = bf16[128,2048]{1,0:T(8,128)(2,1)} custom-call(f32[128,1024]{1,0:T(8,128)S(1)} %get-tuple-element.45.conv_grad, bf16[16,1024]{1,0:T(8,128)(2,1)S(1)} %collective-permute-done.7.before, bf16[16,1024]{1,0:T(8,128)(2,1)S(1)} %collective-permute-done.8.after, f32[31,1024]{1,0:T(8,128)S(1)} %copy-done.2, bf16[128,2048]{1,0:T(8,128)(2,1)S(1)} %bitcast.57), custom_call_target="tpu_custom_call" | custom-call | flops 20000000 | bytes 2097152 | tf_op jit(solution)/shard_map/pallas_call | solution.py:381
  (55 shorter events, 7.1 us)
Async XLA Ops:
  1.5 18.0 %collective-permute-start = (bf16[16,2048]{1,0:T(8,128)(2,1)S(1)}, bf16[16,2048]{1,0:T(8,128)(2,1)S(1)}, u32[]{:S(2)}, u32[]{:S(2)}) collective-permute-start(bf16[16,2048]{1,0:T(8,128)(2,1)S(1)} %get-tuple-element.54), channel_id=1, source_target_pairs={{0,32},{32,64},{64,96},{96,128},{128,160},{160,192},{192,224},{224... | collective-permute-start | bytes 196616 | tf_op jit(solution)/shard_map/ppermute | solution.py:30
  6.9 12.9 %collective-permute-start.1 = (bf16[16,2048]{1,0:T(8,128)(2,1)S(1)}, bf16[16,2048]{1,0:T(8,128)(2,1)S(1)}, u32[]{:S(2)}, u32[]{:S(2)}) collective-permute-start(bf16[16,2048]{1,0:T(8,128)(2,1)S(1)} %get-tuple-element.53), channel_id=1, source_target_pairs={{32,0},{64,32},{96,64},{128,96},{160,128},{192,160},{224,192},{256... | collective-permute-start | bytes 196616 | tf_op jit(solution)/shard_map/ppermute | solution.py:30
  19.5 0.6 copy-start.4
  19.8 0.6 copy-start.6
  52.1 8.0 %copy-start.8 = (bf16[1,1024,256]{2,1,0:T(8,128)(2,1)S(1)}, bf16[1,1024,256]{2,1,0:T(8,128)(2,1)}, u32[]{:S(2)}) copy-start(bf16[1,1024,256]{2,1,0:T(8,128)(2,1)} %param.12) | copy-start | bytes 1572868
  52.1 11.3 %copy-start.9 = (bf16[1,256,1024]{2,1,0:T(8,128)(2,1)S(1)}, bf16[1,256,1024]{2,1,0:T(8,128)(2,1)}, u32[]{:S(2)}) copy-start(bf16[1,256,1024]{2,1,0:T(8,128)(2,1)} %param.13) | copy-start | bytes 1572868
  52.1 32.8 %all-to-all-start.1 = ((bf16[16,256,128]{2,1,0:T(8,128)(2,1)}), bf16[16,256,128]{2,1,0:T(8,128)(2,1)S(1)}, u32[]{:S(2)}, u32[]{:S(2)}) async-start(bf16[16,256,128]{2,1,0:T(8,128)(2,1)} %bitcast.16), calls=%async_computation.1 | async-start | bytes 2097152 | tf_op jit(solution)/shard_map/all_to_all | solution.py:435
  60.1 24.8 %collective-permute-start.2 = (bf16[1024,256]{1,0:T(8,128)(2,1)S(1)}, bf16[1024,256]{1,0:T(8,128)(2,1)S(1)}, u32[]{:S(2)}, u32[]{:S(2)}) collective-permute-start(bf16[1024,256]{1,0:T(8,128)(2,1)S(1)} %bitcast.63), channel_id=1, source_target_pairs={{0,16},{16,0},{1,17},{17,1},{2,18},{18,2},{3,19},{19,3},{4,20},{20... | collective-permute-start | bytes 1572872 | tf_op jit(solution)/shard_map/ppermute | solution.py:430
  63.4 21.5 %collective-permute-start.3 = (bf16[256,1024]{1,0:T(8,128)(2,1)S(1)}, bf16[256,1024]{1,0:T(8,128)(2,1)S(1)}, u32[]{:S(2)}, u32[]{:S(2)}) collective-permute-start(bf16[256,1024]{1,0:T(8,128)(2,1)S(1)} %bitcast.65), channel_id=1, source_target_pairs={{0,17},{17,0},{1,16},{16,1},{2,19},{19,2},{3,18},{18,3},{4,21},{21... | collective-permute-start | bytes 1572872 | tf_op jit(solution)/shard_map/ppermute | solution.py:431
  87.3 0.7 copy-start.10
  88.0 32.0 %all-to-all-start.2 = ((bf16[16,256,128]{2,1,0:T(8,128)(2,1)}), bf16[16,256,128]{2,1,0:T(8,128)(2,1)}, u32[]{:S(2)}, u32[]{:S(2)}) async-start(bf16[16,256,128]{2,1,0:T(8,128)(2,1)} %get-tuple-element.30), calls=%async_computation.2 | async-start | bytes 2097152 | tf_op jit(solution)/shard_map/all_to_all | solution.py:438
  95.0 1.0 copy-start.11
  96.8 15.3 %collective-permute-start.4 = (bf16[1024,256]{1,0:T(8,128)(2,1)S(1)}, bf16[1024,256]{1,0:T(8,128)(2,1)S(1)}, u32[]{:S(2)}, u32[]{:S(2)}) collective-permute-start(bf16[1024,256]{1,0:T(8,128)(2,1)S(1)} %get-tuple-element.33), channel_id=1, source_target_pairs={{0,17},{17,0},{1,16},{16,1},{2,19},{19,2},{3,18},{18,3},{4,21},{21... | collective-permute-start | bytes 1572872 | tf_op jit(solution)/shard_map/ppermute | solution.py:441
  112.1 3.1 %copy-start.12 = (bf16[1024,256]{1,0:T(8,128)(2,1)}, bf16[1024,256]{1,0:T(8,128)(2,1)S(1)}, u32[]{:S(2)}) copy-start(bf16[1024,256]{1,0:T(8,128)(2,1)S(1)} %collective-permute-done.4) | copy-start | bytes 1572868
  112.1 17.7 %collective-permute-start.5 = (bf16[1024,256]{1,0:T(8,128)(2,1)S(1)}, bf16[1024,256]{1,0:T(8,128)(2,1)S(1)}, u32[]{:S(2)}, u32[]{:S(2)}) collective-permute-start(bf16[1024,256]{1,0:T(8,128)(2,1)S(1)} %get-tuple-element.38), channel_id=1, source_target_pairs={{0,1},{1,0},{2,3},{3,2},{4,5},{5,4},{6,7},{7,6},{8,9},{9,8},{10,11... | collective-permute-start | bytes 1572872 | tf_op jit(solution)/shard_map/ppermute | solution.py:443
  115.3 24.2 %collective-permute-start.6 = (bf16[1024,256]{1,0:T(8,128)(2,1)S(1)}, bf16[1024,256]{1,0:T(8,128)(2,1)}, u32[]{:S(2)}, u32[]{:S(2)}) collective-permute-start(bf16[1024,256]{1,0:T(8,128)(2,1)S(1)} %get-tuple-element.39), channel_id=1, source_target_pairs={{0,16},{16,0},{1,17},{17,1},{2,18},{18,2},{3,19},{19,3},{4,20},{20... | collective-permute-start | bytes 1572872 | tf_op jit(solution)/shard_map/ppermute | solution.py:444
  122.1 22.3 %all-to-all-start.3 = ((bf16[32,16,128]{2,1,0:T(8,128)(2,1)}), bf16[32,16,128]{2,1,0:T(8,128)(2,1)S(1)}, u32[]{:S(2)}, u32[]{:S(2)}) async-start(bf16[32,16,128]{2,1,0:T(8,128)(2,1)} %copy_bitcast_fusion), calls=%async_computation.3 | async-start | bytes 262144 | tf_op jit(solution)/shard_map/all_to_all | solution.py:449
  128.5 0.7 copy-start.17
  129.2 0.7 copy-start.16
  129.9 15.5 %copy-start.14 = (bf16[1024,256]{1,0:T(8,128)(2,1)}, bf16[1024,256]{1,0:T(8,128)(2,1)S(1)}, u32[]{:S(2)}) copy-start(bf16[1024,256]{1,0:T(8,128)(2,1)S(1)} %collective-permute-done.5) | copy-start | bytes 1572868
  144.4 0.7 copy-start.18
  146.2 5.9 %copy-start = (bf16[1,128,2048]{2,1,0:T(8,128)(2,1)S(1)}, bf16[1,128,2048]{2,1,0:T(8,128)(2,1)}, u32[]{:S(2)}) copy-start(bf16[1,128,2048]{2,1,0:T(8,128)(2,1)} %param.10) | copy-start | bytes 1572868
  146.3 5.9 %copy-start.2 = (f32[31,1024]{1,0:T(8,128)S(1)}, f32[31,1024]{1,0:T(8,128)}, u32[]{:S(2)}) copy-start(f32[31,1024]{1,0:T(8,128)} %taps.5) | copy-start | bytes 380932
  146.3 5.9 %copy-start.3 = (bf16[1,128,1024]{2,1,0:T(8,128)(2,1)S(1)}, bf16[1,128,1024]{2,1,0:T(8,128)(2,1)}, u32[]{:S(2)}) copy-start(bf16[1,128,1024]{2,1,0:T(8,128)(2,1)} %param.9) | copy-start | bytes 786436
  146.3 5.9 %copy-start.5 = (bf16[16,2048]{1,0:T(8,128)(2,1)S(1)}, bf16[16,2048]{1,0:T(8,128)(2,1)}, u32[]{:S(2)}) copy-start(bf16[16,2048]{1,0:T(8,128)(2,1)} %copy-done.4) | copy-start | bytes 196612
  146.3 5.9 %copy-start.7 = (bf16[16,2048]{1,0:T(8,128)(2,1)S(1)}, bf16[16,2048]{1,0:T(8,128)(2,1)}, u32[]{:S(2)}) copy-start(bf16[16,2048]{1,0:T(8,128)(2,1)} %copy-done.6) | copy-start | bytes 196612
  146.3 19.0 %all-to-all-start.4 = ((bf16[16,128,128]{2,1,0:T(8,128)(2,1)}), bf16[16,128,128]{2,1,0:T(8,128)(2,1)S(1)}, u32[]{:S(2)}, u32[]{:S(2)}) async-start(bf16[16,128,128]{2,1,0:T(8,128)(2,1)} %broadcast_in_dim.37), calls=%async_computation.4 | async-start | bytes 1048576 | tf_op jit(solution)/shard_map/all_to_all | solution.py:457
  152.2 2.1 %copy-start.13 = (bf16[1024,256]{1,0:T(8,128)(2,1)S(1)}, bf16[1024,256]{1,0:T(8,128)(2,1)}, u32[]{:S(2)}) copy-start(bf16[1024,256]{1,0:T(8,128)(2,1)} %copy-done.12) | copy-start | bytes 1572868
  152.2 2.1 %copy-start.15 = (bf16[1024,256]{1,0:T(8,128)(2,1)S(1)}, bf16[1024,256]{1,0:T(8,128)(2,1)}, u32[]{:S(2)}) copy-start(bf16[1024,256]{1,0:T(8,128)(2,1)} %copy-done.14) | copy-start | bytes 1572868
  156.3 9.0 %copy-start.1 = (bf16[1,128,1024]{2,1,0:T(8,128)(2,1)S(1)}, bf16[1,128,1024]{2,1,0:T(8,128)(2,1)}, u32[]{:S(2)}) copy-start(bf16[1,128,1024]{2,1,0:T(8,128)(2,1)} %param.17) | copy-start | bytes 786436
  165.4 8.6 %collective-permute-start.7 = (bf16[16,1024]{1,0:T(8,128)(2,1)S(1)}, bf16[16,1024]{1,0:T(8,128)(2,1)S(1)}, u32[]{:S(2)}, u32[]{:S(2)}) collective-permute-start(bf16[16,1024]{1,0:T(8,128)(2,1)S(1)} %get-tuple-element.56), channel_id=1, source_target_pairs={{0,32},{32,64},{64,96},{96,128},{128,160},{160,192},{192,224},{224... | collective-permute-start | bytes 98312 | tf_op jit(solution)/shard_map/ppermute | solution.py:30
  170.2 5.2 %collective-permute-start.8 = (bf16[16,1024]{1,0:T(8,128)(2,1)S(1)}, bf16[16,1024]{1,0:T(8,128)(2,1)S(1)}, u32[]{:S(2)}, u32[]{:S(2)}) collective-permute-start(bf16[16,1024]{1,0:T(8,128)(2,1)S(1)} %get-tuple-element.55), channel_id=1, source_target_pairs={{32,0},{64,32},{96,64},{128,96},{160,128},{192,160},{224,192},{256... | collective-permute-start | bytes 98312 | tf_op jit(solution)/shard_map/ppermute | solution.py:30
